TPU v7x, 512 devices: a whole 4x8x8 slice. The times are simulated.
512 devices in a mesh: ctx: 32 (over y, x), tp: 16 (over z, core).
Axes of the slice: x: 4, y: 8, z: 8, core: 2. Of those that a mesh axis runs over, the one named last changes fastest.
Arguments:
- queries: bfloat16 [16384, 4096], P('ctx', 'tp'), may hold values from -6 to 6
- keys: bfloat16 [16384, 4096], P('ctx', 'tp'), may hold values from -6 to 6
- values: bfloat16 [16384, 8192], P('ctx', 'tp'), may hold values from -6 to 6
- coef_table: float32 [16, 16], P(None, 'tp'), may hold values from 0.25 to 2
- level_index: int32 [16384, 15], P('ctx'), may hold values from 0 to 15
- out_weight: bfloat16 [8192, 4096], P('tp', 'ctx'), may hold values from -0.0625 to 0.0625
Outputs:
- mixed: bfloat16 [16384, 4096], P(('ctx', 'tp'))
All inputs are finite; a program needn't handle non-finite values.
Results may differ from a plain program's by a relative error of at most 0.025.
Values may be sent and summed in bfloat16 or wider, within the bound.
No kernel may reach another device: no remote copies, remote signals or barrier semaphores. Data moves between devices by JAX's collectives and lax.ppermute only.
A program may use at most 64 MiB of HBM per device.

v0:
```python
import jax
import jax.numpy as jnp
from jax import lax
from jax.sharding import PartitionSpec as P


def from_partner(value, axis, stride):
    mask = 2**stride
    pairs = [(source, source ^ mask) for source in range(lax.axis_size(axis))]
    return lax.ppermute(value, axis, pairs)


def level_weights(lam_block, bits):
    pos = jnp.arange(lam_block.shape[0], dtype=jnp.int32)
    crossed = jnp.bitwise_xor(pos[:, None], pos[None, :])
    level = jnp.zeros(crossed.shape, jnp.int32)
    for i in range(bits):
        level = level + (crossed >= 2**i).astype(jnp.int32)
    weight = jnp.zeros(crossed.shape, jnp.float32)
    for lev in range(bits + 1):
        weight = weight + jnp.where(level == lev, lam_block[:, lev][:, None], 0.0)
    return jnp.where(pos[:, None] >= pos[None, :], weight, 0.0)


def on_device(queries, keys, values, coef_table, level_index, out_weight):
    tok_rows = queries.shape[0]
    head_count = coef_table.shape[1]
    key_size = queries.shape[1] // head_count
    tok_bits = tok_rows.bit_length() - 1
    ctx_bits = lax.axis_size("ctx").bit_length() - 1
    levels_all = level_index.shape[1]
    inverse_scale = 1.0 / key_size**0.5
    my_block = lax.axis_index("ctx")
    scales = jnp.exp2(-0.5 * jnp.arange(levels_all).astype(jnp.float32))
    picked = jnp.zeros((tok_rows, levels_all, head_count), jnp.float32)
    for row in range(coef_table.shape[0]):
        picked = picked + jnp.where(
            (level_index == row)[:, :, None], coef_table[row][None, None, :], 0.0
        )
    lam = picked * scales[None, :, None]
    head = 0
    q_one = queries
    scores = (
        lax.dot_general(q_one, keys, (((1,), (1,)), ((), ())), preferred_element_type=jnp.float32)
        * inverse_scale
    )
    attn = (scores * level_weights(lam[:, :, head], tok_bits)).astype(jnp.bfloat16)
    outputs = [jnp.dot(attn, values, preferred_element_type=jnp.float32)]
    states = [
        lax.dot_general(keys, values, (((0,), (0,)), ((), ())), preferred_element_type=jnp.float32)
    ]
    subtree = jnp.stack(states)
    for bit in range(ctx_bits):
        partner = from_partner(subtree.astype(jnp.bfloat16), "ctx", bit).astype(subtree.dtype)
        setbit = (my_block >> bit & 1).astype(jnp.float32)
        sibling_node = partner.astype(jnp.bfloat16)
        head = 0
        q_one = queries
        outer_product = jnp.dot(q_one, sibling_node[head], preferred_element_type=jnp.float32)
        factor = lam[:, tok_bits + 1 + bit, head] * inverse_scale * setbit
        outputs[head] = outputs[head] + outer_product * factor[:, None]
        subtree = subtree + partner
    attended = jnp.concatenate([piece.astype(jnp.bfloat16) for piece in outputs], axis=1)
    terms = jnp.dot(
        attended,
        lax.all_gather(out_weight, "ctx", axis=1, tiled=True),
        preferred_element_type=jnp.float32,
    )
    mixed = lax.psum_scatter(terms.astype(jnp.bfloat16), "tp", scatter_dimension=0, tiled=True)
    return mixed


def solution(mesh):
    in_specs = (
        P("ctx", "tp"),
        P("ctx", "tp"),
        P("ctx", "tp"),
        P(None, "tp"),
        P("ctx", None),
        P("tp", "ctx"),
    )
    out_specs = P(("ctx", "tp"), None)
    return jax.shard_map(
        on_device, mesh=mesh, in_specs=in_specs, out_specs=out_specs, check_vma=False
    )
```

profile of v0, /device:TPU:1, one launch (start us, length us, event | category | flops | bytes accessed | tf_op | source)
XLA Modules:
  0.0 193.5 jit_solution(6322504694172674432)
XLA Ops:
  6.5 0.7 all-gather.2.cloned.1.call-update
  7.3 0.0 reduce-scatter.2.cloned.1.call-start
  7.3 0.3 copy-done
  7.6 1.3 fusion.109
  8.9 3.9 %collective-permute-start = (bf16[1,256,512]{2,1,0:T(8,128)(2,1)S(1)}, bf16[1,256,512]{2,1,0:T(8,128)(2,1)S(1)}, u32[]{:S(2)}, u32[]{:S(2)}) collective-permute-start(bf16[1,256,512]{2,1,0:T(8,128)(2,1)S(1)} %convert_bitcast_fusion), channel_id=1, source_target_pairs={{0,16},{16,0},{32,48},{48,32},{64,80},{80,64},{96,112},{112,96},{1... | collective-permute-start | bytes 786440 | tf_op jit(solution)/shard_map/ppermute | solution.py:10
  12.9 1.9 %fusion.108 = (f32[1,1]{0,1:T(1,128)}, f32[1,1]{0,1:T(1,128)}, f32[1,1]{0,1:T(1,128)}, f32[1,1]{0,1:T(1,128)}, f32[1,1]{0,1:T(1,128)}, /*index=5*/f32[1,1]{0,1:T...) fusion(f32[16,1]{0,1:T(1,128)} %param.9), kind=kLoop, calls=%fused_computation.129 | loop fusion | bytes 128 | tf_op jit(solution)/shard_map/slice | solution.py:38
  14.8 10.9 %add_multiply_fusion = f32[512,15]{0,1:T(8,128)S(1)} fusion(s32[512,15]{0,1:T(8,128)} %param.10, f32[15]{0:T(128)S(1)} %multiply_exponential_fusion, f32[]{:T(128)} %bitcast.15, f32[]{:T(128)} %bitcast.14, f32[]{:T(128)} %bitcast.13, f32[]{:T(128)} %bitcast.12, f32[]{:T(128)} %bitcast.11, f32[]{:T(128)} %bitcast.10, f32[]{:T(128)} %bitcast.9, f32[]{:T(128)} %bitcast.8, ...), kind=kLoop, calls=%fused_computation.104 | loop fusion | flops 368640 | bytes 61564 | tf_op jit(solution)/shard_map/mul | solution.py:40
  25.7 0.0 copy-start.2
  25.7 0.0 copy-start.1
  25.8 2.0 %fusion.13 = f32[512,512]{1,0:T(8,128)S(1)} fusion(bf16[512,512]{1,0:T(8,128)(2,1)S(1)} %copy-done, bf16[512,256]{1,0:T(8,128)(2,1)} %param.6, bf16[512,256]{1,0:T(8,128)(2,1)} %param.7, f32[512]{0:T(512)S(1)} %bitcast.102, f32[512]{0:T(512)S(1)} %bitcast.103, f32[512]{0:T(512)S(1)} %bitcast.104, f32[512]{0:T(512)S(1)} %bitcast.105, f32[512]{0:T(512)S(1)} %bitcast.106, ...), kind=kOutput, calls=%fused_computation.20 | convolution fusion | flops 418643968 | bytes 2117632 | tf_op jit(solution)/shard_map/dot_general | solution.py:48
  27.7 0.0 collective-permute-done
  27.8 0.1 fusion.89
  27.8 4.4 %collective-permute-start.1 = (bf16[1,256,512]{2,1,0:T(8,128)(2,1)S(1)}, bf16[1,256,512]{2,1,0:T(8,128)(2,1)S(1)}, u32[]{:S(2)}, u32[]{:S(2)}) collective-permute-start(bf16[1,256,512]{2,1,0:T(8,128)(2,1)S(1)} %fusion.89), channel_id=1, source_target_pairs={{0,32},{16,48},{32,0},{48,16},{64,96},{80,112},{96,64},{112,80},{1... | collective-permute-start | bytes 786440 | tf_op jit(solution)/shard_map/ppermute | solution.py:10
  32.2 10.2 %fusion.121 = f32[512,15,1]{0,1,2:T(8,128)S(1)} fusion(f32[15]{0:T(128)S(1)} %multiply_exponential_fusion, f32[]{:T(128)} %bitcast.15, s32[512,15]{0,1:T(8,128)S(1)} %copy-done.2, f32[]{:T(128)} %bitcast.14, f32[]{:T(128)} %bitcast.13, f32[]{:T(128)} %bitcast.12, f32[]{:T(128)} %bitcast.11, f32[]{:T(128)} %bitcast.10, f32[]{:T(128)} %bitcast.9, f32[]{:T(128)} %bitcast.8, ...), kind=kLoop, calls=%fused_computation.131 | loop fusion | flops 368640 | bytes 61564 | tf_op jit(solution)/shard_map/mul | solution.py:40
  42.4 0.0 collective-permute-done.1
  42.4 0.1 fusion.81
  42.5 3.2 %collective-permute-start.2 = (bf16[1,256,512]{2,1,0:T(8,128)(2,1)S(1)}, bf16[1,256,512]{2,1,0:T(8,128)(2,1)S(1)}, u32[]{:S(2)}, u32[]{:S(2)}) collective-permute-start(bf16[1,256,512]{2,1,0:T(8,128)(2,1)S(1)} %fusion.81), channel_id=1, source_target_pairs={{0,64},{16,80},{32,96},{48,112},{64,0},{80,16},{96,32},{112,48},{1... | collective-permute-start | bytes 786440 | tf_op jit(solution)/shard_map/ppermute | solution.py:10
  45.7 0.3 fusion.8
  46.0 5.2 %collective-permute-done.2 = bf16[1,256,512]{2,1,0:T(8,128)(2,1)S(1)} collective-permute-done((bf16[1,256,512]{2,1,0:T(8,128)(2,1)S(1)}, bf16[1,256,512]{2,1,0:T(8,128)(2,1)S(1)}, u32[]{:S(2)}, u32[]{:S(2)}) %collective-permute-start.2) | collective-permute-done | bytes 262176 | tf_op jit(solution)/shard_map/ppermute | solution.py:10
  51.2 0.2 fusion.88
  51.4 5.6 %collective-permute-start.3 = (bf16[1,256,512]{2,1,0:T(8,128)(2,1)S(1)}, bf16[1,256,512]{2,1,0:T(8,128)(2,1)S(1)}, u32[]{:S(2)}, u32[]{:S(2)}) collective-permute-start(bf16[1,256,512]{2,1,0:T(8,128)(2,1)S(1)} %fusion.88), channel_id=1, source_target_pairs={{0,128},{16,144},{32,160},{48,176},{64,192},{80,208},{96,224},{112... | collective-permute-start | bytes 786440 | tf_op jit(solution)/shard_map/ppermute | solution.py:10
  57.0 0.3 fusion.6
  57.3 11.5 %collective-permute-done.3 = bf16[1,256,512]{2,1,0:T(8,128)(2,1)S(1)} collective-permute-done((bf16[1,256,512]{2,1,0:T(8,128)(2,1)S(1)}, bf16[1,256,512]{2,1,0:T(8,128)(2,1)S(1)}, u32[]{:S(2)}, u32[]{:S(2)}) %collective-permute-start.3) | collective-permute-done | bytes 262176 | tf_op jit(solution)/shard_map/ppermute | solution.py:10
  68.8 0.2 add_convert_fusion
  69.0 6.1 %collective-permute-start.4 = (bf16[1,256,512]{2,1,0:T(8,128)(2,1)S(1)}, bf16[1,256,512]{2,1,0:T(8,128)(2,1)S(1)}, u32[]{:S(2)}, u32[]{:S(2)}) collective-permute-start(bf16[1,256,512]{2,1,0:T(8,128)(2,1)S(1)} %add_convert_fusion), channel_id=1, source_target_pairs={{0,256},{16,272},{32,288},{48,304},{64,320},{80,336},{96,352},{112... | collective-permute-start | bytes 786440 | tf_op jit(solution)/shard_map/ppermute | solution.py:10
  75.1 1.4 fusion.4
  76.5 16.7 %collective-permute-done.4 = bf16[1,256,512]{2,1,0:T(8,128)(2,1)S(1)} collective-permute-done((bf16[1,256,512]{2,1,0:T(8,128)(2,1)S(1)}, bf16[1,256,512]{2,1,0:T(8,128)(2,1)S(1)}, u32[]{:S(2)}, u32[]{:S(2)}) %collective-permute-start.4) | collective-permute-done | bytes 262176 | tf_op jit(solution)/shard_map/ppermute | solution.py:10
  93.2 0.3 fusion
  93.5 20.5 %all-gather.2.cloned.1.call-done = bf16[512,4096]{1,0:T(8,128)(2,1)} async-done(((bf16[512,128]{1,0:T(8,128)(2,1)}), bf16[512,4096]{1,0:T(8,128)(2,1)}) %all-gather.2.cloned.1.call-update) | async-done | bytes 4194320 | tf_op jit(solution)/shard_map/all_gather | solution.py:66
  114.1 6.5 %convolution_convert_fusion = bf16[512,4096]{1,0:T(8,128)(2,1)} fusion(bf16[512,4096]{1,0:T(8,128)(2,1)} %all-gather.2.cloned.1.call-done, f32[512,512]{1,0:T(8,128)S(1)} %fusion, f32[512,512]{1,0:T(8,128)} %fusion.4, bf16[512,256]{1,0:T(8,128)(2,1)S(1)} %copy-done.1, f32[512]{0:T(512)S(1)} %bitcast.100, bf16[1,256,512]{2,1,0:T(8,128)(2,1)S(1)} %collective-permute-done.3), kind=kOutput, calls=%fused_computation | convolution fusion | flops 2284847104 | bytes 11012096 | tf_op jit(solution)/shard_map/dot_general | solution.py:64
  120.6 0.0 reduce-scatter.2.cloned.1.call-update
  120.6 66.0 %reduce-scatter.2.cloned.1.call-done = bf16[32,4096]{1,0:T(8,128)(2,1)} async-done(((bf16[512,4096]{1,0:T(8,128)(2,1)}), bf16[32,4096]{1,0:T(8,128)(2,1)}) %reduce-scatter.2.cloned.1.call-update) | async-done | bytes 262160 | tf_op jit(solution)/shard_map/reduce_scatter | solution.py:69
  (8 shorter events, 0.1 us)
Async XLA Ops:
  6.5 1.0 copy-start
  6.5 107.5 %all-gather.2.cloned.1.call-start = ((), (), s32[]{:S(2)}) async-start(), calls=%async_computation.1 | async-start | bytes 4325376 | tf_op jit(solution)/shard_map/all_gather | solution.py:66
  7.3 179.4 %reduce-scatter.2.cloned.1.call-start = ((), (), s32[]{:S(2)}) async-start(), calls=%async_computation.2 | async-start | bytes 4456448 | tf_op jit(solution)/shard_map/reduce_scatter | solution.py:69
  8.9 18.9 %collective-permute-start = (bf16[1,256,512]{2,1,0:T(8,128)(2,1)S(1)}, bf16[1,256,512]{2,1,0:T(8,128)(2,1)S(1)}, u32[]{:S(2)}, u32[]{:S(2)}) collective-permute-start(bf16[1,256,512]{2,1,0:T(8,128)(2,1)S(1)} %convert_bitcast_fusion), channel_id=1, source_target_pairs={{0,16},{16,0},{32,48},{48,32},{64,80},{80,64},{96,112},{112,96},{1... | collective-permute-start | bytes 786440 | tf_op jit(solution)/shard_map/ppermute | solution.py:10
  25.7 6.5 %copy-start.2 = (s32[512,15]{0,1:T(8,128)S(1)}, s32[512,15]{0,1:T(8,128)}, u32[]{:S(2)}) copy-start(s32[512,15]{0,1:T(8,128)} %param.10) | copy-start | bytes 92164
  25.7 20.0 %copy-start.1 = (bf16[512,256]{1,0:T(8,128)(2,1)S(1)}, bf16[512,256]{1,0:T(8,128)(2,1)}, u32[]{:S(2)}) copy-start(bf16[512,256]{1,0:T(8,128)(2,1)} %param.6) | copy-start | bytes 786436
  27.8 14.6 %collective-permute-start.1 = (bf16[1,256,512]{2,1,0:T(8,128)(2,1)S(1)}, bf16[1,256,512]{2,1,0:T(8,128)(2,1)S(1)}, u32[]{:S(2)}, u32[]{:S(2)}) collective-permute-start(bf16[1,256,512]{2,1,0:T(8,128)(2,1)S(1)} %fusion.89), channel_id=1, source_target_pairs={{0,32},{16,48},{32,0},{48,16},{64,96},{80,112},{96,64},{112,80},{1... | collective-permute-start | bytes 786440 | tf_op jit(solution)/shard_map/ppermute | solution.py:10
  42.5 8.7 %collective-permute-start.2 = (bf16[1,256,512]{2,1,0:T(8,128)(2,1)S(1)}, bf16[1,256,512]{2,1,0:T(8,128)(2,1)S(1)}, u32[]{:S(2)}, u32[]{:S(2)}) collective-permute-start(bf16[1,256,512]{2,1,0:T(8,128)(2,1)S(1)} %fusion.81), channel_id=1, source_target_pairs={{0,64},{16,80},{32,96},{48,112},{64,0},{80,16},{96,32},{112,48},{1... | collective-permute-start | bytes 786440 | tf_op jit(solution)/shard_map/ppermute | solution.py:10
  51.4 17.5 %collective-permute-start.3 = (bf16[1,256,512]{2,1,0:T(8,128)(2,1)S(1)}, bf16[1,256,512]{2,1,0:T(8,128)(2,1)S(1)}, u32[]{:S(2)}, u32[]{:S(2)}) collective-permute-start(bf16[1,256,512]{2,1,0:T(8,128)(2,1)S(1)} %fusion.88), channel_id=1, source_target_pairs={{0,128},{16,144},{32,160},{48,176},{64,192},{80,208},{96,224},{112... | collective-permute-start | bytes 786440 | tf_op jit(solution)/shard_map/ppermute | solution.py:10
  69.0 24.2 %collective-permute-start.4 = (bf16[1,256,512]{2,1,0:T(8,128)(2,1)S(1)}, bf16[1,256,512]{2,1,0:T(8,128)(2,1)S(1)}, u32[]{:S(2)}, u32[]{:S(2)}) collective-permute-start(bf16[1,256,512]{2,1,0:T(8,128)(2,1)S(1)} %add_convert_fusion), channel_id=1, source_target_pairs={{0,256},{16,272},{32,288},{48,304},{64,320},{80,336},{96,352},{112... | collective-permute-start | bytes 786440 | tf_op jit(solution)/shard_map/ppermute | solution.py:10
Sparse Core Ops, SparseCore 0:
  10.4 103.6 all-gather.1
  120.8 65.8 reduce-scatter.1
where the time goes:
time: 196 us; the launch traced here: 193 us
  waiting for transfers between devices  121 us (62%)
  starting transfers between devices  23.3 us (12%)
  other arithmetic  21.7 us (11%)
  between operations  13.6 us (7%)
  matrix products  12.1 us (6%)
  local copies, waits for them, and re-layouts  2.25 us (1%)
    reduce_scatter x1, waiting for transfers between devices, on_device(): lax.psum_scatter(terms.astype(jnp.bfloat16), 'tp', scatter_dimension=0, t...  66 us
    ppermute x5, waiting for transfers between devices, from_partner(): return lax.ppermute(value, axis, pairs)  33.4 us
    ppermute x5, starting transfers between devices, from_partner(): return lax.ppermute(value, axis, pairs)  23.2 us
    mul x2, other arithmetic, on_device(): lam = picked * scales[None, :, None]  21.1 us
    all_gather x1, waiting for transfers between devices, on_device(): lax.all_gather(out_weight, 'ctx', axis=1, tiled=True)  20.5 us
    dot_general x1, matrix products, on_device(): jnp.dot(attended, lax.all_gather(out_weight, 'ctx', axis=1, tiled=True),...  6.55 us
  transfers between devices with their start and end apart: 7, of which 5 were waited for; matrix products, arithmetic and copies ran while one was open for 15% of the time, Pallas kernels for 0%

commit v1 on v0

v1 whole, which is shorter than its diff:
```python
import functools

import jax
import jax.numpy as jnp
from jax import lax
from jax.experimental import pallas as pl
from jax.experimental.pallas import tpu as pltpu
from jax.sharding import Mesh, PartitionSpec as P

F32, BF16 = jnp.float32, jnp.bfloat16
QUAD = ("zl", "core")
TP = ("zh", "zl", "core")
CTX = ("y", "x")
VMEM = pl.BlockSpec(memory_space=pltpu.VMEM)
SMEM = pl.BlockSpec(memory_space=pltpu.SMEM)
PARAMS = pltpu.CompilerParams(vmem_limit_bytes=48 * 1024 * 1024)


def shifted(value, axis, by):
    n = lax.axis_size(axis)
    return lax.ppermute(value, axis, [(i, (i + by) % n) for i in range(n)])


def flipped(value, axis):
    return lax.ppermute(value, axis, [(0, 1), (1, 0)])


def local_kernel(coef_ref, index_ref, q_ref, k_ref, v_ref, local_ref, lam_ref):
    index = index_ref[...]
    lam = jnp.zeros(index.shape, F32)
    for row in range(coef_ref.shape[0]):
        lam = jnp.where(index == row, coef_ref[row, 0], lam)
    level_of = lax.broadcasted_iota(jnp.int32, index.shape, 1).astype(F32)
    lam = lam * jnp.exp2(-0.5 * level_of)
    lam_ref[...] = lam
    inverse_scale = 1.0 / q_ref.shape[1] ** 0.5
    tile = 128
    t = lax.broadcasted_iota(jnp.int32, (tile, tile), 0)
    s = lax.broadcasted_iota(jnp.int32, (tile, tile), 1)
    crossed = jnp.bitwise_xor(t, s)
    causal = t >= s
    for i in range(q_ref.shape[0] // tile):
        rows = slice(i * tile, (i + 1) * tile)
        lam_rows = lam[rows]
        scores = lax.dot_general(
            q_ref[rows, :], k_ref[: (i + 1) * tile, :], (((1,), (1,)), ((), ())), preferred_element_type=F32
        )
        scores = scores * inverse_scale
        pieces = []
        for j in range(i):
            level = 7 + (i ^ j).bit_length()
            pieces.append(scores[:, j * tile : (j + 1) * tile] * lam_rows[:, level : level + 1])
        weight = jnp.broadcast_to(lam_rows[:, 0:1], (tile, tile))
        for bit in range(7):
            weight = jnp.where(crossed >= 2**bit, lam_rows[:, bit + 1 : bit + 2], weight)
        weight = jnp.where(causal, weight, 0.0)
        pieces.append(scores[:, i * tile :] * weight)
        attn = jnp.concatenate([piece.astype(BF16) for piece in pieces], axis=1)
        local_ref[rows, :] = jnp.dot(attn, v_ref[: (i + 1) * tile, :], preferred_element_type=F32)


def inter_kernel(base, bits_ref, local_ref, lam_ref, q_ref, near_ref, pair_ref, far_ref, o_ref):
    q = q_ref[...]
    inverse_scale = 1.0 / q.shape[1] ** 0.5
    total = local_ref[...]
    count = 2 + far_ref.shape[1]
    for bit in range(count):
        if bit == 0:
            node = near_ref[...]
        elif bit == 1:
            node = pair_ref[...]
        else:
            node = jnp.concatenate([far_ref[i, bit - 2] for i in range(far_ref.shape[0])], axis=0)
        setbit = (bits_ref[0] >> bit & 1).astype(F32)
        factor = lam_ref[:, base + bit : base + bit + 1] * inverse_scale * setbit
        total = total + jnp.dot(q, node, preferred_element_type=F32) * factor
    o_ref[...] = total.astype(BF16)


def project_kernel(flip_ref, o0_ref, o1_ref, o2_ref, o3_ref, w_ref, part_ref):
    total = None
    for j, o_ref in enumerate((o0_ref, o1_ref, o2_ref, o3_ref)):
        k = jnp.bitwise_xor(flip_ref[0], j)
        w = jnp.concatenate([w_ref[0, k], w_ref[1, k]], axis=1)
        term = jnp.dot(o_ref[...], w, preferred_element_type=F32)
        total = term if total is None else total + term
    part_ref[...] = total.astype(BF16)


def sum_kernel(got_ref, out_ref):
    quads, members, _, columns = got_ref.shape
    for u in range(members):
        total = got_ref[0, u].astype(F32)
        for i in range(1, quads):
            total = total + got_ref[i, u].astype(F32)
        total = total.astype(BF16)
        for block in range(columns // 128):
            start = (block * members + u) * 128
            out_ref[:, start : start + 128] = total[:, block * 128 : (block + 1) * 128]


def on_device(queries, keys, values, coef_table, level_index, out_weight):
    rows, key_size = queries.shape
    value_size = values.shape[1]
    x, y = lax.axis_index("x"), lax.axis_index("y")
    u = lax.axis_index(QUAD)
    nx, ny, nu = lax.axis_size("x"), lax.axis_size("y"), 4

    got = []
    for k in range(nu):
        pairs = [(i * nu + j, (j ^ k) * nu + i) for i in range(nx) for j in range(nu)]
        got.append(lax.ppermute(out_weight, ("x",) + QUAD, pairs))
    weight = jnp.stack(got)

    state = lax.dot_general(keys, values, (((0,), (0,)), ((), ())), preferred_element_type=F32)
    sent = state.astype(BF16)
    after, across, before = shifted(sent, "x", 1), shifted(sent, "x", 2), shifted(sent, "x", -1)

    gathered = lax.all_gather(weight, "y", axis=0)

    local, lam = pl.pallas_call(
        local_kernel,
        out_shape=(
            jax.ShapeDtypeStruct((rows, value_size), F32),
            jax.ShapeDtypeStruct(level_index.shape, F32),
        ),
        in_specs=[SMEM] + [VMEM] * 4,
        out_specs=(VMEM, VMEM),
        compiler_params=PARAMS,
    )(coef_table, level_index, queries, keys, values)

    piece = key_size // nx
    start = x * piece
    quarter = lax.dynamic_slice_in_dim(state, start, piece)
    for other in (after, across, before):
        quarter = quarter + lax.dynamic_slice_in_dim(other, start, piece).astype(F32)
    pair = (across.astype(F32) + jnp.where(x == 2, after, before).astype(F32)).astype(BF16)
    row_sums = lax.all_gather(quarter.astype(BF16), "y", axis=0).astype(F32)
    far = []
    for bit in range(ny.bit_length() - 1):
        first = ((y >> bit) - 1) << bit
        source = jnp.arange(ny)
        mine = (source >= first) & (source < first + 2**bit)
        far.append(jnp.sum(jnp.where(mine[:, None, None], row_sums, 0.0), axis=0))
    far = lax.all_gather(jnp.stack(far).astype(BF16), "x", axis=0)

    levels = level_index.shape[1]
    block = lax.axis_index(CTX).astype(jnp.int32).reshape(1)
    o = pl.pallas_call(
        functools.partial(inter_kernel, levels - 2 - far.shape[1]),
        out_shape=jax.ShapeDtypeStruct((rows, value_size), BF16),
        in_specs=[SMEM] + [VMEM] * 6,
        out_specs=VMEM,
        compiler_params=PARAMS,
    )(block, local, lam, queries, after, pair, far)

    o_z = flipped(o, "zl")
    o_c = flipped(o, "core")
    o_zc = flipped(o_z, "core")
    flip = jnp.bitwise_xor(x, u).astype(jnp.int32).reshape(1)
    width = out_weight.shape[1]
    whole = pl.BlockSpec((rows, value_size), lambda i: (0, 0))
    part = pl.pallas_call(
        project_kernel,
        grid=(ny // 2,),
        out_shape=jax.ShapeDtypeStruct((rows, ny * width), BF16),
        in_specs=[SMEM]
        + [whole] * 4
        + [pl.BlockSpec((2, nu, value_size, width), lambda i: (i, 0, 0, 0))],
        out_specs=pl.BlockSpec((rows, 2 * width), lambda i: (0, i)),
        compiler_params=PARAMS,
    )(flip, o, o_c, o_z, o_zc, gathered)

    n = lax.axis_size(TP)
    back = lax.all_to_all(part, TP, 0, 0, tiled=True)
    return pl.pallas_call(
        sum_kernel,
        out_shape=jax.ShapeDtypeStruct((rows // n, nu * ny * width), BF16),
        in_specs=[VMEM],
        out_specs=VMEM,
        compiler_params=PARAMS,
    )(back.reshape(n // nu, nu, rows // n, ny * width))


def solution(mesh):
    split = Mesh(mesh.devices.reshape(8, 4, 4, 2, 2), CTX + TP)
    in_specs = (P(CTX, TP), P(CTX, TP), P(CTX, TP), P(None, TP), P(CTX, None), P(TP, CTX))
    out_specs = P(CTX + TP, None)
    return jax.shard_map(on_device, mesh=split, in_specs=in_specs, out_specs=out_specs, check_vma=False)
```

time: 196 us -> 162 us (0.83)
  waiting for transfers between devices: 121 us -> 8.24 us
  blocking collectives: 0 us -> 76 us
  starting transfers between devices: 23.3 us -> 47.5 us
  other arithmetic: 21.7 us -> 1.38 us
  matrix products: 12.1 us -> 1.48 us
  Pallas kernels: 0 us -> 8.32 us
  local copies, waits for them, and re-layouts: 2.25 us -> 4.57 us
    reduce_scatter x1 -> x0, waiting for transfers between devices: 66 us -> none  [on_device(): lax.psum_scatter(terms.astype(jnp.bfloat16), 'tp', scatter_dimension=0, t...]
    all_to_all x0 -> x1, blocking collectives: none -> 39.1 us  [on_device(): back = lax.all_to_all(part, TP, 0, 0, tiled=True)]
    all_gather x0 -> x2, blocking collectives: none -> 36.9 us  [the longest x1 23.7 us: on_device(): row_sums = lax.all_gather(quarter.astype(BF16), 'y', axis=0).astype(F32)]
    ppermute x5 -> x10, waiting for transfers between devices: 33.4 us -> 8.22 us  [the longest x4 4.54 us: on_device(): got.append(lax.ppermute(out_weight, ('x',) + QUAD, pairs))]
    ppermute x5 -> x10, starting transfers between devices: 23.2 us -> 47.5 us  [the longest x3 19.4 us: flipped(): return lax.ppermute(value, axis, [(0, 1), (1, 0)])]
    mul x3 -> x0, other arithmetic: 21.1 us -> none  [the longest x2 21.1 us: on_device(): lam = picked * scales[None, :, None]]
    all_gather x1, waiting for transfers between devices: 20.5 us -> 0.01 us  [on_device(): gathered = lax.all_gather(weight, 'y', axis=0)]
    dot_general x6 -> x0, matrix products: 10.8 us -> none  [the longest x1 6.55 us: on_device(): jnp.dot(attended, lax.all_gather(out_weight, 'ctx', axis=1, tiled=True),...]
  transfers between devices with their start and end apart: 7 -> 11, of which waited for: 5 -> 3; matrix products, arithmetic and copies ran while one was open for 15% -> 2% of each run, Pallas kernels for 0% -> 2%
where the time goes in v1:
time: 162 us; the launch traced here: 161 us
  blocking collectives  76 us (47%)
  starting transfers between devices  47.5 us (29%)
  between operations  13.7 us (8%)
  Pallas kernels  8.32 us (5%)
  waiting for transfers between devices  8.24 us (5%)
  local copies, waits for them, and re-layouts  4.57 us (3%)
    all_to_all x1, blocking collectives, on_device(): back = lax.all_to_all(part, TP, 0, 0, tiled=True)  39.1 us
    all_gather x1, blocking collectives, on_device(): row_sums = lax.all_gather(quarter.astype(BF16), 'y', axis=0).astype(F32)  23.7 us
    ppermute x3, starting transfers between devices, flipped(): return lax.ppermute(value, axis, [(0, 1), (1, 0)])  19.4 us
    ppermute x4, starting transfers between devices, on_device(): got.append(lax.ppermute(out_weight, ('x',) + QUAD, pairs))  18.5 us
    all_gather x1, blocking collectives, on_device(): far = lax.all_gather(jnp.stack(far).astype(BF16), 'x', axis=0)  13.2 us
    ppermute x3, starting transfers between devices, shifted(): return lax.ppermute(value, axis, [(i, (i + by) % n) for i in range(n)])  9.61 us
    pallas_call x1, Pallas kernels, on_device(): pl.pallas_call(project_kernel, grid=(ny // 2,), out_shape=jax.ShapeDtypeS...  4.74 us
    unnamed x10, local copies, waits for them, and re-layouts  4.57 us
  transfers between devices with their start and end apart: 11, of which 3 were waited for; matrix products, arithmetic and copies ran while one was open for 2% of the time, Pallas kernels for 2%

profile of v1, /device:TPU:1, one launch (start us, length us, event | category | flops | bytes accessed | tf_op | source)
XLA Modules:
  0.0 161.2 jit_solution(6978864566294955517)
XLA Ops:
  6.5 6.0 %collective-permute-start.9 = (bf16[512,128]{1,0:T(8,128)(2,1)}, bf16[512,128]{1,0:T(8,128)(2,1)S(1)}, u32[]{:S(2)}, u32[]{:S(2)}) collective-permute-start(bf16[512,128]{1,0:T(8,128)(2,1)} %param.11), channel_id=1, source_target_pairs={{0,48},{1,32},{2,16},{3,0},{16,49},{17,33},{18,17},{19,1},{32,50},... | collective-permute-start | bytes 393224 | tf_op jit(solution)/shard_map/ppermute | solution.py:112
  12.6 1.9 %collective-permute-start.6 = (bf16[512,128]{1,0:T(8,128)(2,1)}, bf16[512,128]{1,0:T(8,128)(2,1)S(1)}, u32[]{:S(2)}, u32[]{:S(2)}) collective-permute-start(bf16[512,128]{1,0:T(8,128)(2,1)} %param.11), channel_id=1, source_target_pairs={{0,0},{1,16},{2,32},{3,48},{16,1},{17,17},{18,33},{19,49},{32,2},{... | collective-permute-start | bytes 393224 | tf_op jit(solution)/shard_map/ppermute | solution.py:112
  14.5 4.3 %collective-permute-start.7 = (bf16[512,128]{1,0:T(8,128)(2,1)}, bf16[512,128]{1,0:T(8,128)(2,1)S(1)}, u32[]{:S(2)}, u32[]{:S(2)}) collective-permute-start(bf16[512,128]{1,0:T(8,128)(2,1)} %param.11), channel_id=1, source_target_pairs={{0,16},{1,0},{2,48},{3,32},{16,17},{17,1},{18,49},{19,33},{32,18},... | collective-permute-start | bytes 393224 | tf_op jit(solution)/shard_map/ppermute | solution.py:112
  18.8 6.3 %collective-permute-start.8 = (bf16[512,128]{1,0:T(8,128)(2,1)}, bf16[512,128]{1,0:T(8,128)(2,1)S(1)}, u32[]{:S(2)}, u32[]{:S(2)}) collective-permute-start(bf16[512,128]{1,0:T(8,128)(2,1)} %param.11), channel_id=1, source_target_pairs={{0,32},{1,48},{2,0},{3,16},{16,33},{17,49},{18,1},{19,17},{32,34},... | collective-permute-start | bytes 393224 | tf_op jit(solution)/shard_map/ppermute | solution.py:112
  25.1 0.0 collective-permute-done.9
  25.1 0.0 collective-permute-done.6
  25.1 4.5 %collective-permute-done.8 = bf16[512,128]{1,0:T(8,128)(2,1)S(1)} collective-permute-done((bf16[512,128]{1,0:T(8,128)(2,1)}, bf16[512,128]{1,0:T(8,128)(2,1)S(1)}, u32[]{:S(2)}, u32[]{:S(2)}) %collective-permute-start.8) | collective-permute-done | bytes 131104 | tf_op jit(solution)/shard_map/ppermute | solution.py:112
  29.7 0.9 pad_maximum_fusion
  30.5 0.0 all-gather.4.cloned.1.call-update
  30.6 1.5 fusion.3
  32.0 1.9 %collective-permute-start = (bf16[256,512]{1,0:T(8,128)(2,1)S(1)}, bf16[256,512]{1,0:T(8,128)(2,1)S(1)}, u32[]{:S(2)}, u32[]{:S(2)}) collective-permute-start(bf16[256,512]{1,0:T(8,128)(2,1)S(1)} %get-tuple-element.12), channel_id=1, source_target_pairs={{0,16},{16,32},{32,48},{48,0},{1,17},{17,33},{33,49},{49,1},{2,18}... | collective-permute-start | bytes 786440 | tf_op jit(solution)/shard_map/ppermute | solution.py:21
  34.0 4.8 %collective-permute-start.1 = (bf16[256,512]{1,0:T(8,128)(2,1)S(1)}, bf16[256,512]{1,0:T(8,128)(2,1)S(1)}, u32[]{:S(2)}, u32[]{:S(2)}) collective-permute-start(bf16[256,512]{1,0:T(8,128)(2,1)S(1)} %get-tuple-element.12), channel_id=1, source_target_pairs={{0,32},{16,48},{32,0},{48,16},{1,33},{17,49},{33,1},{49,17},{2,34}... | collective-permute-start | bytes 786440 | tf_op jit(solution)/shard_map/ppermute | solution.py:21
  38.8 2.9 %collective-permute-start.2 = (bf16[256,512]{1,0:T(8,128)(2,1)S(1)}, bf16[256,512]{1,0:T(8,128)(2,1)S(1)}, u32[]{:S(2)}, u32[]{:S(2)}) collective-permute-start(bf16[256,512]{1,0:T(8,128)(2,1)S(1)} %get-tuple-element.12), channel_id=1, source_target_pairs={{0,48},{16,0},{32,16},{48,32},{1,49},{17,1},{33,17},{49,33},{2,50}... | collective-permute-start | bytes 786440 | tf_op jit(solution)/shard_map/ppermute | solution.py:21
  41.7 0.9 copy.10.index_ref
  42.6 0.7 copy.9.coef_ref
  43.4 1.0 copy-done
  44.4 0.9 copy-done.1
  45.3 0.9 copy-done.3
  46.3 1.8 %shard_map.64 = (f32[512,512]{1,0:T(8,128)S(1)}, f32[512,15]{1,0:T(8,128)S(1)}) custom-call(f32[16,1]{1,0:T(8,128)S(1)} %copy.9.coef_ref, s32[512,15]{1,0:T(8,128)S(1)} %copy.10.index_ref, bf16[512,256]{1,0:T(8,128)(2,1)S(1)} %copy-done.1, bf16[512,256]{1,0:T(8,128)(2,1)S(1)} %copy-done.3, bf16[512,512]{1,0:T(8,128)(2,1)S(1)} %copy-done), custom_call_target="tpu_custom_call" | custom-call | tf_op jit(solution)/shard_map/pallas_call | solution.py:121
  48.1 2.2 %collective-permute-done.2 = bf16[256,512]{1,0:T(8,128)(2,1)S(1)} collective-permute-done((bf16[256,512]{1,0:T(8,128)(2,1)S(1)}, bf16[256,512]{1,0:T(8,128)(2,1)S(1)}, u32[]{:S(2)}, u32[]{:S(2)}) %collective-permute-start.2) | collective-permute-done | bytes 262176 | tf_op jit(solution)/shard_map/ppermute | solution.py:21
  50.3 23.7 %all-gather = bf16[512,512]{1,0:T(8,128)(2,1)S(1)} all-gather(bf16[64,512]{1,0:T(8,128)(2,1)S(1)} %add_convert_fusion.1), channel_id=2, replica_groups=mesh['y'=8,'x'=4,'zh'=4,'zl'=2,'core'=2] {'y'}, dimensions={0}, use_global_device_ids=true | all-gather | bytes 589824 | tf_op jit(solution)/shard_map/all_gather | solution.py:138
  74.1 0.3 fusion
  74.4 0.1 add_convert_fusion.pair_ref
  74.6 13.2 %all_gather.18.far_ref = bf16[4,3,64,512]{3,2,1,0:T(8,128)(2,1)S(1)} all-gather(bf16[1,3,64,512]{3,2,1,0:T(8,128)(2,1)S(1)} %pad_maximum_fusion.1), channel_id=1, replica_groups=mesh['y'=8,'x'=4,'zh'=4,'zl'=2,'core'=2] {'x'}, dimensions={0}, use_global_device_ids=true | all-gather | bytes 983040 | tf_op jit(solution)/shard_map/all_gather | solution.py:145
  87.8 1.0 shard_map.65.o0_ref
  88.7 3.5 %collective-permute-start.4 = (bf16[512,512]{1,0:T(8,128)(2,1)S(1)}, bf16[512,512]{1,0:T(8,128)(2,1)S(1)}, u32[]{:S(2)}, u32[]{:S(2)}) collective-permute-start(bf16[512,512]{1,0:T(8,128)(2,1)S(1)} %shard_map.65.o0_ref), channel_id=1, source_target_pairs={{0,2},{2,0},{1,3},{3,1},{4,6},{6,4},{5,7},{7,5},{8,10},{10,8},{9,1... | collective-permute-start | bytes 1572872 | tf_op jit(solution)/shard_map/ppermute | solution.py:25
  92.3 8.7 %collective-permute-start.3 = (bf16[512,512]{1,0:T(8,128)(2,1)S(1)}, bf16[512,512]{1,0:T(8,128)(2,1)S(1)}, u32[]{:S(2)}, u32[]{:S(2)}) collective-permute-start(bf16[512,512]{1,0:T(8,128)(2,1)S(1)} %shard_map.65.o0_ref), channel_id=1, source_target_pairs={{0,1},{1,0},{2,3},{3,2},{4,5},{5,4},{6,7},{7,6},{8,9},{9,8},{10,11... | collective-permute-start | bytes 1572872 | tf_op jit(solution)/shard_map/ppermute | solution.py:25
  101.0 7.1 %collective-permute-start.5 = (bf16[512,512]{1,0:T(8,128)(2,1)S(1)}, bf16[512,512]{1,0:T(8,128)(2,1)S(1)}, u32[]{:S(2)}, u32[]{:S(2)}) collective-permute-start(bf16[512,512]{1,0:T(8,128)(2,1)S(1)} %collective-permute-done.4.o2_ref), channel_id=1, source_target_pairs={{0,1},{1,0},{2,3},{3,2},{4,5},{5,4},{6,7},{7,6},{8,9},{9,8},{10,11... | collective-permute-start | bytes 1572872 | tf_op jit(solution)/shard_map/ppermute | solution.py:25
  108.1 1.5 collective-permute-done.5.o3_ref
  109.6 4.7 %shard_map.66 = bf16[512,1024]{1,0:T(8,128)(2,1)S(1)} custom-call(s32[1]{0:T(128)} %bitcast.flip_ref, bf16[512,512]{1,0:T(8,128)(2,1)S(1)} %shard_map.65.o0_ref, bf16[512,512]{1,0:T(8,128)(2,1)S(1)} %collective-permute-done.3.o1_ref, bf16[512,512]{1,0:T(8,128)(2,1)S(1)} %collective-permute-done.4.o2_ref, bf16[512,512]{1,0:T(8,128)(2,1)S(1)} %collective-permute-done.5.o3_ref, ...), custom_call_target="tpu_custom_call" | custom-call | tf_op jit(solution)/shard_map/pallas_call | solution.py:163
  114.4 39.1 %all_to_all.9 = bf16[16,32,1024]{2,1,0:T(8,128)(2,1)S(1)} all-to-all(bf16[16,32,1024]{2,1,0:T(8,128)(2,1)S(1)} %bitcast.23), channel_id=1, replica_groups=mesh['y'=8,'x'=4,'zh'=4,'zl'=2,'core'=2] {'zh','zl','core'}, dimensions={0} | all-to-all | bytes 2097152 | tf_op jit(solution)/shard_map/all_to_all | solution.py:175
  153.5 0.8 shard_map.67
  (16 shorter events, 0.1 us)
Async XLA Ops:
  6.5 103.1 %all-gather.4.cloned.1.call-start = ((), (), s32[]{:S(2)}) async-start(), calls=%async_computation.1 | async-start | bytes 4718592 | tf_op jit(solution)/shard_map/all_gather | solution.py:119
  6.5 18.6 %collective-permute-start.9 = (bf16[512,128]{1,0:T(8,128)(2,1)}, bf16[512,128]{1,0:T(8,128)(2,1)S(1)}, u32[]{:S(2)}, u32[]{:S(2)}) collective-permute-start(bf16[512,128]{1,0:T(8,128)(2,1)} %param.11), channel_id=1, source_target_pairs={{0,48},{1,32},{2,16},{3,0},{16,49},{17,33},{18,17},{19,1},{32,50},... | collective-permute-start | bytes 393224 | tf_op jit(solution)/shard_map/ppermute | solution.py:112
  12.6 12.5 %collective-permute-start.6 = (bf16[512,128]{1,0:T(8,128)(2,1)}, bf16[512,128]{1,0:T(8,128)(2,1)S(1)}, u32[]{:S(2)}, u32[]{:S(2)}) collective-permute-start(bf16[512,128]{1,0:T(8,128)(2,1)} %param.11), channel_id=1, source_target_pairs={{0,0},{1,16},{2,32},{3,48},{16,1},{17,17},{18,33},{19,49},{32,2},{... | collective-permute-start | bytes 393224 | tf_op jit(solution)/shard_map/ppermute | solution.py:112
  14.5 10.6 %collective-permute-start.7 = (bf16[512,128]{1,0:T(8,128)(2,1)}, bf16[512,128]{1,0:T(8,128)(2,1)S(1)}, u32[]{:S(2)}, u32[]{:S(2)}) collective-permute-start(bf16[512,128]{1,0:T(8,128)(2,1)} %param.11), channel_id=1, source_target_pairs={{0,16},{1,0},{2,48},{3,32},{16,17},{17,1},{18,49},{19,33},{32,18},... | collective-permute-start | bytes 393224 | tf_op jit(solution)/shard_map/ppermute | solution.py:112
  18.8 10.9 %collective-permute-start.8 = (bf16[512,128]{1,0:T(8,128)(2,1)}, bf16[512,128]{1,0:T(8,128)(2,1)S(1)}, u32[]{:S(2)}, u32[]{:S(2)}) collective-permute-start(bf16[512,128]{1,0:T(8,128)(2,1)} %param.11), channel_id=1, source_target_pairs={{0,32},{1,48},{2,0},{3,16},{16,33},{17,49},{18,1},{19,17},{32,34},... | collective-permute-start | bytes 393224 | tf_op jit(solution)/shard_map/ppermute | solution.py:112
  30.5 57.2 %copy-start.2 = (bf16[512,256]{1,0:T(8,128)(2,1)S(1)}, bf16[512,256]{1,0:T(8,128)(2,1)}, u32[]{:S(2)}) copy-start(bf16[512,256]{1,0:T(8,128)(2,1)} %q_ref.3) | copy-start | bytes 786436
  32.0 16.1 %collective-permute-start = (bf16[256,512]{1,0:T(8,128)(2,1)S(1)}, bf16[256,512]{1,0:T(8,128)(2,1)S(1)}, u32[]{:S(2)}, u32[]{:S(2)}) collective-permute-start(bf16[256,512]{1,0:T(8,128)(2,1)S(1)} %get-tuple-element.12), channel_id=1, source_target_pairs={{0,16},{16,32},{32,48},{48,0},{1,17},{17,33},{33,49},{49,1},{2,18}... | collective-permute-start | bytes 786440 | tf_op jit(solution)/shard_map/ppermute | solution.py:21
  34.0 14.1 %collective-permute-start.1 = (bf16[256,512]{1,0:T(8,128)(2,1)S(1)}, bf16[256,512]{1,0:T(8,128)(2,1)S(1)}, u32[]{:S(2)}, u32[]{:S(2)}) collective-permute-start(bf16[256,512]{1,0:T(8,128)(2,1)S(1)} %get-tuple-element.12), channel_id=1, source_target_pairs={{0,32},{16,48},{32,0},{48,16},{1,33},{17,49},{33,1},{49,17},{2,34}... | collective-permute-start | bytes 786440 | tf_op jit(solution)/shard_map/ppermute | solution.py:21
  38.8 11.5 %collective-permute-start.2 = (bf16[256,512]{1,0:T(8,128)(2,1)S(1)}, bf16[256,512]{1,0:T(8,128)(2,1)S(1)}, u32[]{:S(2)}, u32[]{:S(2)}) collective-permute-start(bf16[256,512]{1,0:T(8,128)(2,1)S(1)} %get-tuple-element.12), channel_id=1, source_target_pairs={{0,48},{16,0},{32,16},{48,32},{1,49},{17,1},{33,17},{49,33},{2,50}... | collective-permute-start | bytes 786440 | tf_op jit(solution)/shard_map/ppermute | solution.py:21
  43.3 1.0 copy-start
  44.4 0.9 copy-start.1
  45.3 0.9 copy-start.3
  88.7 12.3 %collective-permute-start.4 = (bf16[512,512]{1,0:T(8,128)(2,1)S(1)}, bf16[512,512]{1,0:T(8,128)(2,1)S(1)}, u32[]{:S(2)}, u32[]{:S(2)}) collective-permute-start(bf16[512,512]{1,0:T(8,128)(2,1)S(1)} %shard_map.65.o0_ref), channel_id=1, source_target_pairs={{0,2},{2,0},{1,3},{3,1},{4,6},{6,4},{5,7},{7,5},{8,10},{10,8},{9,1... | collective-permute-start | bytes 1572872 | tf_op jit(solution)/shard_map/ppermute | solution.py:25
  92.3 15.9 %collective-permute-start.3 = (bf16[512,512]{1,0:T(8,128)(2,1)S(1)}, bf16[512,512]{1,0:T(8,128)(2,1)S(1)}, u32[]{:S(2)}, u32[]{:S(2)}) collective-permute-start(bf16[512,512]{1,0:T(8,128)(2,1)S(1)} %shard_map.65.o0_ref), channel_id=1, source_target_pairs={{0,1},{1,0},{2,3},{3,2},{4,5},{5,4},{6,7},{7,6},{8,9},{9,8},{10,11... | collective-permute-start | bytes 1572872 | tf_op jit(solution)/shard_map/ppermute | solution.py:25
  101.0 8.6 %collective-permute-start.5 = (bf16[512,512]{1,0:T(8,128)(2,1)S(1)}, bf16[512,512]{1,0:T(8,128)(2,1)S(1)}, u32[]{:S(2)}, u32[]{:S(2)}) collective-permute-start(bf16[512,512]{1,0:T(8,128)(2,1)S(1)} %collective-permute-done.4.o2_ref), channel_id=1, source_target_pairs={{0,1},{1,0},{2,3},{3,2},{4,5},{5,4},{6,7},{7,6},{8,9},{9,8},{10,11... | collective-permute-start | bytes 1572872 | tf_op jit(solution)/shard_map/ppermute | solution.py:25
Sparse Core Ops, SparseCore 0:
  30.7 64.3 all-gather.3

commit v2 on v1

--- a/solution.py
+++ b/solution.py
@@ -19,6 +19,10 @@
 def shifted(value, axis, by):
     n = lax.axis_size(axis)
     return lax.ppermute(value, axis, [(i, (i + by) % n) for i in range(n)])
+
+
+def crossed(value, axis, by):
+    return lax.ppermute(value, axis, [(i, i ^ by) for i in range(lax.axis_size(axis))])
 
 
 def flipped(value, axis):
@@ -102,19 +106,20 @@
 def on_device(queries, keys, values, coef_table, level_index, out_weight):
     rows, key_size = queries.shape
     value_size = values.shape[1]
-    x, y = lax.axis_index("x"), lax.axis_index("y")
+    x = lax.axis_index("x")
     u = lax.axis_index(QUAD)
     nx, ny, nu = lax.axis_size("x"), lax.axis_size("y"), 4
+
+    state = lax.dot_general(keys, values, (((0,), (0,)), ((), ())), preferred_element_type=F32)
+    sent = state.astype(BF16)
+    after, across, before = shifted(sent, "x", 1), shifted(sent, "x", 2), shifted(sent, "x", -1)
 
     got = []
     for k in range(nu):
         pairs = [(i * nu + j, (j ^ k) * nu + i) for i in range(nx) for j in range(nu)]
         got.append(lax.ppermute(out_weight, ("x",) + QUAD, pairs))
+    *got, after, before = lax.optimization_barrier((*got, after, before))
     weight = jnp.stack(got)
-
-    state = lax.dot_general(keys, values, (((0,), (0,)), ((), ())), preferred_element_type=F32)
-    sent = state.astype(BF16)
-    after, across, before = shifted(sent, "x", 1), shifted(sent, "x", 2), shifted(sent, "x", -1)
 
     gathered = lax.all_gather(weight, "y", axis=0)
 
@@ -135,14 +140,11 @@
     for other in (after, across, before):
         quarter = quarter + lax.dynamic_slice_in_dim(other, start, piece).astype(F32)
     pair = (across.astype(F32) + jnp.where(x == 2, after, before).astype(F32)).astype(BF16)
-    row_sums = lax.all_gather(quarter.astype(BF16), "y", axis=0).astype(F32)
-    far = []
-    for bit in range(ny.bit_length() - 1):
-        first = ((y >> bit) - 1) << bit
-        source = jnp.arange(ny)
-        mine = (source >= first) & (source < first + 2**bit)
-        far.append(jnp.sum(jnp.where(mine[:, None, None], row_sums, 0.0), axis=0))
-    far = lax.all_gather(jnp.stack(far).astype(BF16), "x", axis=0)
+    beside = crossed(quarter.astype(BF16), "y", 1)
+    both = (quarter + beside.astype(F32)).astype(BF16)
+    third, fourth, fifth = crossed(both, "y", 2), crossed(both, "y", 4), crossed(both, "y", 6)
+    far = [beside, third, (fourth.astype(F32) + fifth.astype(F32)).astype(BF16)]
+    far = lax.all_gather(jnp.stack(far), "x", axis=0)
 
     levels = level_index.shape[1]
     block = lax.axis_index(CTX).astype(jnp.int32).reshape(1)

time: 162 us -> 161 us (level)
  blocking collectives: 76 us -> 51.4 us
  waiting for transfers between devices: 8.24 us -> 25.4 us
  starting transfers between devices: 47.5 us -> 55.9 us
    all_gather x2 -> x1, blocking collectives: 36.9 us -> 12.6 us  [on_device(): far = lax.all_gather(jnp.stack(far), 'x', axis=0)]
    ppermute x0 -> x4, starting transfers between devices: none -> 15 us  [crossed(): lax.ppermute(value, axis, [(i, i ^ by) for i in range(lax.axis_size(axis))])]
    ppermute x0 -> x4, waiting for transfers between devices: none -> 8.89 us  [crossed(): lax.ppermute(value, axis, [(i, i ^ by) for i in range(lax.axis_size(axis))])]
    ppermute x3, starting transfers between devices: 19.4 us -> 14.3 us  [flipped(): return lax.ppermute(value, axis, [(0, 1), (1, 0)])]
    ppermute x4, starting transfers between devices: 18.5 us -> 14.4 us  [on_device(): got.append(lax.ppermute(out_weight, ('x',) + QUAD, pairs))]
    ppermute x3, waiting for transfers between devices: 1.5 us -> 5.27 us  [flipped(): return lax.ppermute(value, axis, [(0, 1), (1, 0)])]
    ppermute x3, waiting for transfers between devices: 2.18 us -> 5.94 us  [shifted(): return lax.ppermute(value, axis, [(i, (i + by) % n) for i in range(n)])]
    ppermute x3, starting transfers between devices: 9.61 us -> 12.1 us  [shifted(): return lax.ppermute(value, axis, [(i, (i + by) % n) for i in range(n)])]
  transfers between devices with their start and end apart: 11 -> 15, of which waited for: 3 -> 7; matrix products, arithmetic and copies ran while one was open for 2% -> 2% of each run, Pallas kernels for 2% -> 2%
where the time goes in v2:
time: 161 us
  starting transfers between devices  55.9 us (35%)
  blocking collectives  51.4 us (32%)
  waiting for transfers between devices  25.4 us (16%)
  between operations  13.6 us (8%)
  Pallas kernels  8.32 us (5%)
  local copies, waits for them, and re-layouts  3.53 us (2%)
    all_to_all x1, blocking collectives, on_device(): back = lax.all_to_all(part, TP, 0, 0, tiled=True)  38.8 us
    ppermute x4, starting transfers between devices, crossed(): lax.ppermute(value, axis, [(i, i ^ by) for i in range(lax.axis_size(axis))])  15 us
    ppermute x4, starting transfers between devices, on_device(): got.append(lax.ppermute(out_weight, ('x',) + QUAD, pairs))  14.4 us
    ppermute x3, starting transfers between devices, flipped(): return lax.ppermute(value, axis, [(0, 1), (1, 0)])  14.3 us
    all_gather x1, blocking collectives, on_device(): far = lax.all_gather(jnp.stack(far), 'x', axis=0)  12.6 us
    ppermute x3, starting transfers between devices, shifted(): return lax.ppermute(value, axis, [(i, (i + by) % n) for i in range(n)])  12.1 us
    ppermute x4, waiting for transfers between devices, crossed(): lax.ppermute(value, axis, [(i, i ^ by) for i in range(lax.axis_size(axis))])  8.89 us
    ppermute x3, waiting for transfers between devices, shifted(): return lax.ppermute(value, axis, [(i, (i + by) % n) for i in range(n)])  5.94 us
  transfers between devices with their start and end apart: 15, of which 7 were waited for; matrix products, arithmetic and copies ran while one was open for 2% of the time, Pallas kernels for 2%

profile of v2, /device:TPU:1, one launch (start us, length us, event | category | flops | bytes accessed | tf_op | source)
XLA Modules:
  0.0 160.7 jit_solution(9929550203063449215)
XLA Ops:
  6.5 4.6 %collective-permute-start = (bf16[512,128]{1,0:T(8,128)(2,1)}, bf16[512,128]{1,0:T(8,128)(2,1)S(1)}, u32[]{:S(2)}, u32[]{:S(2)}) collective-permute-start(bf16[512,128]{1,0:T(8,128)(2,1)} %param.11), channel_id=1, source_target_pairs={{0,0},{1,16},{2,32},{3,48},{16,1},{17,17},{18,33},{19,49},{32,2},{... | collective-permute-start | bytes 393224 | tf_op jit(solution)/shard_map/ppermute | solution.py:120
  11.2 1.4 fusion.2
  12.6 1.9 %collective-permute-start.4 = (bf16[256,512]{1,0:T(8,128)(2,1)S(1)}, bf16[256,512]{1,0:T(8,128)(2,1)S(1)}, u32[]{:S(2)}, u32[]{:S(2)}) collective-permute-start(bf16[256,512]{1,0:T(8,128)(2,1)S(1)} %get-tuple-element.21), channel_id=1, source_target_pairs={{0,16},{16,32},{32,48},{48,0},{1,17},{17,33},{33,49},{49,1},{2,18}... | collective-permute-start | bytes 786440 | tf_op jit(solution)/shard_map/ppermute | solution.py:21
  14.6 5.5 %collective-permute-start.5 = (bf16[256,512]{1,0:T(8,128)(2,1)S(1)}, bf16[256,512]{1,0:T(8,128)(2,1)S(1)}, u32[]{:S(2)}, u32[]{:S(2)}) collective-permute-start(bf16[256,512]{1,0:T(8,128)(2,1)S(1)} %get-tuple-element.21), channel_id=1, source_target_pairs={{0,48},{16,0},{32,16},{48,32},{1,49},{17,1},{33,17},{49,33},{2,50}... | collective-permute-start | bytes 786440 | tf_op jit(solution)/shard_map/ppermute | solution.py:21
  20.1 5.4 %collective-permute-start.1 = (bf16[512,128]{1,0:T(8,128)(2,1)}, bf16[512,128]{1,0:T(8,128)(2,1)S(1)}, u32[]{:S(2)}, u32[]{:S(2)}) collective-permute-start(bf16[512,128]{1,0:T(8,128)(2,1)} %param.11), channel_id=1, source_target_pairs={{0,16},{1,0},{2,48},{3,32},{16,17},{17,1},{18,49},{19,33},{32,18},... | collective-permute-start | bytes 393224 | tf_op jit(solution)/shard_map/ppermute | solution.py:120
  25.5 1.9 %collective-permute-start.2 = (bf16[512,128]{1,0:T(8,128)(2,1)}, bf16[512,128]{1,0:T(8,128)(2,1)S(1)}, u32[]{:S(2)}, u32[]{:S(2)}) collective-permute-start(bf16[512,128]{1,0:T(8,128)(2,1)} %param.11), channel_id=1, source_target_pairs={{0,32},{1,48},{2,0},{3,16},{16,33},{17,49},{18,1},{19,17},{32,34},... | collective-permute-start | bytes 393224 | tf_op jit(solution)/shard_map/ppermute | solution.py:120
  27.5 2.4 %collective-permute-start.3 = (bf16[512,128]{1,0:T(8,128)(2,1)}, bf16[512,128]{1,0:T(8,128)(2,1)S(1)}, u32[]{:S(2)}, u32[]{:S(2)}) collective-permute-start(bf16[512,128]{1,0:T(8,128)(2,1)} %param.11), channel_id=1, source_target_pairs={{0,48},{1,32},{2,16},{3,0},{16,49},{17,33},{18,17},{19,1},{32,50},... | collective-permute-start | bytes 393224 | tf_op jit(solution)/shard_map/ppermute | solution.py:120
  29.9 3.5 %collective-permute-done.2 = bf16[512,128]{1,0:T(8,128)(2,1)S(1)} collective-permute-done((bf16[512,128]{1,0:T(8,128)(2,1)}, bf16[512,128]{1,0:T(8,128)(2,1)S(1)}, u32[]{:S(2)}, u32[]{:S(2)}) %collective-permute-start.2) | collective-permute-done | bytes 131104 | tf_op jit(solution)/shard_map/ppermute | solution.py:120
  33.4 1.9 %collective-permute-done.3 = bf16[512,128]{1,0:T(8,128)(2,1)S(1)} collective-permute-done((bf16[512,128]{1,0:T(8,128)(2,1)}, bf16[512,128]{1,0:T(8,128)(2,1)S(1)}, u32[]{:S(2)}, u32[]{:S(2)}) %collective-permute-start.3) | collective-permute-done | bytes 131104 | tf_op jit(solution)/shard_map/ppermute | solution.py:120
  35.3 0.9 pad_maximum_fusion
  36.2 4.7 %collective-permute-start.6 = (bf16[256,512]{1,0:T(8,128)(2,1)S(1)}, bf16[256,512]{1,0:T(8,128)(2,1)S(1)}, u32[]{:S(2)}, u32[]{:S(2)}) collective-permute-start(bf16[256,512]{1,0:T(8,128)(2,1)S(1)} %get-tuple-element.21), channel_id=1, source_target_pairs={{0,32},{16,48},{32,0},{48,16},{1,33},{17,49},{33,1},{49,17},{2,34}... | collective-permute-start | bytes 786440 | tf_op jit(solution)/shard_map/ppermute | solution.py:21
  40.8 5.9 %collective-permute-done.6 = bf16[256,512]{1,0:T(8,128)(2,1)S(1)} collective-permute-done((bf16[256,512]{1,0:T(8,128)(2,1)S(1)}, bf16[256,512]{1,0:T(8,128)(2,1)S(1)}, u32[]{:S(2)}, u32[]{:S(2)}) %collective-permute-start.6) | collective-permute-done | bytes 262176 | tf_op jit(solution)/shard_map/ppermute | solution.py:21
  46.8 3.6 %collective-permute-start.7 = (bf16[64,512]{1,0:T(8,128)(2,1)S(1)}, bf16[64,512]{1,0:T(8,128)(2,1)S(1)}, u32[]{:S(2)}, u32[]{:S(2)}) collective-permute-start(bf16[64,512]{1,0:T(8,128)(2,1)S(1)} %fusion.1), channel_id=1, source_target_pairs={{0,64},{64,0},{128,192},{192,128},{256,320},{320,256},{384,448},{4... | collective-permute-start | bytes 196616 | tf_op jit(solution)/shard_map/ppermute | solution.py:25
  50.5 0.9 copy.10.index_ref
  52.1 0.9 copy-done.1
  53.0 0.9 copy-done.3
  54.0 1.8 %shard_map.64 = (f32[512,512]{1,0:T(8,128)S(1)}, f32[512,15]{1,0:T(8,128)S(1)}) custom-call(f32[16,1]{1,0:T(8,128)S(1)} %copy.9.coef_ref, s32[512,15]{1,0:T(8,128)S(1)} %copy.10.index_ref, bf16[512,256]{1,0:T(8,128)(2,1)S(1)} %copy-done.1, bf16[512,256]{1,0:T(8,128)(2,1)S(1)} %copy-done.3, bf16[512,512]{1,0:T(8,128)(2,1)S(1)} %copy-done), custom_call_target="tpu_custom_call" | custom-call | tf_op jit(solution)/shard_map/pallas_call | solution.py:126
  55.8 5.0 %collective-permute-start.10 = (bf16[64,512]{1,0:T(8,128)(2,1)S(1)}, bf16[64,512]{1,0:T(8,128)(2,1)S(1)}, u32[]{:S(2)}, u32[]{:S(2)}) collective-permute-start(bf16[64,512]{1,0:T(8,128)(2,1)S(1)} %add_convert_fusion.2), channel_id=1, source_target_pairs={{0,384},{64,448},{128,256},{192,320},{256,128},{320,192},{384,0},{... | collective-permute-start | bytes 196616 | tf_op jit(solution)/shard_map/ppermute | solution.py:25
  60.8 4.4 %collective-permute-start.9 = (bf16[64,512]{1,0:T(8,128)(2,1)S(1)}, bf16[64,512]{1,0:T(8,128)(2,1)S(1)}, u32[]{:S(2)}, u32[]{:S(2)}) collective-permute-start(bf16[64,512]{1,0:T(8,128)(2,1)S(1)} %add_convert_fusion.2), channel_id=1, source_target_pairs={{0,256},{64,320},{128,384},{192,448},{256,0},{320,64},{384,128},{4... | collective-permute-start | bytes 196616 | tf_op jit(solution)/shard_map/ppermute | solution.py:25
  65.4 2.0 %collective-permute-start.8 = (bf16[64,512]{1,0:T(8,128)(2,1)S(1)}, bf16[64,512]{1,0:T(8,128)(2,1)S(1)}, u32[]{:S(2)}, u32[]{:S(2)}) collective-permute-start(bf16[64,512]{1,0:T(8,128)(2,1)S(1)} %add_convert_fusion.2), channel_id=1, source_target_pairs={{0,128},{64,192},{128,0},{192,64},{256,384},{320,448},{384,256},{4... | collective-permute-start | bytes 196616 | tf_op jit(solution)/shard_map/ppermute | solution.py:25
  67.4 6.4 %collective-permute-done.9 = bf16[64,512]{1,0:T(8,128)(2,1)S(1)} collective-permute-done((bf16[64,512]{1,0:T(8,128)(2,1)S(1)}, bf16[64,512]{1,0:T(8,128)(2,1)S(1)}, u32[]{:S(2)}, u32[]{:S(2)}) %collective-permute-start.9) | collective-permute-done | bytes 65568 | tf_op jit(solution)/shard_map/ppermute | solution.py:25
  73.7 2.5 %collective-permute-done.8 = bf16[64,512]{1,0:T(8,128)(2,1)S(1)} collective-permute-done((bf16[64,512]{1,0:T(8,128)(2,1)S(1)}, bf16[64,512]{1,0:T(8,128)(2,1)S(1)}, u32[]{:S(2)}, u32[]{:S(2)}) %collective-permute-start.8) | collective-permute-done | bytes 65568 | tf_op jit(solution)/shard_map/ppermute | solution.py:25
  76.3 12.6 %all-gather = bf16[12,64,512]{2,1,0:T(8,128)(2,1)S(1)} all-gather(bf16[3,64,512]{2,1,0:T(8,128)(2,1)S(1)} %pad_maximum_fusion.1), channel_id=2, replica_groups=mesh['y'=8,'x'=4,'zh'=4,'zl'=2,'core'=2] {'x'}, dimensions={0}, use_global_device_ids=true | all-gather | bytes 983040 | tf_op jit(solution)/shard_map/all_gather | solution.py:147
  88.9 1.0 shard_map.65.o0_ref
  89.9 3.0 %collective-permute-start.12 = (bf16[512,512]{1,0:T(8,128)(2,1)S(1)}, bf16[512,512]{1,0:T(8,128)(2,1)S(1)}, u32[]{:S(2)}, u32[]{:S(2)}) collective-permute-start(bf16[512,512]{1,0:T(8,128)(2,1)S(1)} %shard_map.65.o0_ref), channel_id=1, source_target_pairs={{0,2},{2,0},{1,3},{3,1},{4,6},{6,4},{5,7},{7,5},{8,10},{10,8},{9,1... | collective-permute-start | bytes 1572872 | tf_op jit(solution)/shard_map/ppermute | solution.py:29
  92.9 5.7 %collective-permute-start.11 = (bf16[512,512]{1,0:T(8,128)(2,1)S(1)}, bf16[512,512]{1,0:T(8,128)(2,1)S(1)}, u32[]{:S(2)}, u32[]{:S(2)}) collective-permute-start(bf16[512,512]{1,0:T(8,128)(2,1)S(1)} %shard_map.65.o0_ref), channel_id=1, source_target_pairs={{0,1},{1,0},{2,3},{3,2},{4,5},{5,4},{6,7},{7,6},{8,9},{9,8},{10,11... | collective-permute-start | bytes 1572872 | tf_op jit(solution)/shard_map/ppermute | solution.py:29
  98.6 3.8 %collective-permute-done.12.o2_ref = bf16[512,512]{1,0:T(8,128)(2,1)S(1)} collective-permute-done((bf16[512,512]{1,0:T(8,128)(2,1)S(1)}, bf16[512,512]{1,0:T(8,128)(2,1)S(1)}, u32[]{:S(2)}, u32[]{:S(2)}) %collective-permute-start.12) | collective-permute-done | bytes 524320 | tf_op jit(solution)/shard_map/ppermute | solution.py:29
  102.4 5.6 %collective-permute-start.13 = (bf16[512,512]{1,0:T(8,128)(2,1)S(1)}, bf16[512,512]{1,0:T(8,128)(2,1)S(1)}, u32[]{:S(2)}, u32[]{:S(2)}) collective-permute-start(bf16[512,512]{1,0:T(8,128)(2,1)S(1)} %collective-permute-done.12.o2_ref), channel_id=1, source_target_pairs={{0,1},{1,0},{2,3},{3,2},{4,5},{5,4},{6,7},{7,6},{8,9},{9,8},{10,11... | collective-permute-start | bytes 1572872 | tf_op jit(solution)/shard_map/ppermute | solution.py:29
  108.0 1.5 collective-permute-done.13.o3_ref
  109.5 4.7 %shard_map.66 = bf16[512,1024]{1,0:T(8,128)(2,1)S(1)} custom-call(s32[1]{0:T(128)} %bitcast.flip_ref, bf16[512,512]{1,0:T(8,128)(2,1)S(1)} %shard_map.65.o0_ref, bf16[512,512]{1,0:T(8,128)(2,1)S(1)} %collective-permute-done.11.o1_ref, bf16[512,512]{1,0:T(8,128)(2,1)S(1)} %collective-permute-done.12.o2_ref, ...), custom_call_target="tpu_custom_call" | custom-call | tf_op jit(solution)/shard_map/pallas_call | solution.py:165
  114.3 38.8 %all_to_all.9 = bf16[16,32,1024]{2,1,0:T(8,128)(2,1)S(1)} all-to-all(bf16[16,32,1024]{2,1,0:T(8,128)(2,1)S(1)} %bitcast.17), channel_id=1, replica_groups=mesh['y'=8,'x'=4,'zh'=4,'zl'=2,'core'=2] {'zh','zl','core'}, dimensions={0} | all-to-all | bytes 2097152 | tf_op jit(solution)/shard_map/all_to_all | solution.py:177
  153.0 0.8 shard_map.67
  (22 shorter events, 1.0 us)
Async XLA Ops:
  6.5 45.6 %copy-start = (bf16[512,512]{1,0:T(8,128)(2,1)S(1)}, bf16[512,512]{1,0:T(8,128)(2,1)}, u32[]{:S(2)}) copy-start(bf16[512,512]{1,0:T(8,128)(2,1)} %v_ref.1) | copy-start | bytes 1572868
  6.5 82.4 %copy-start.2 = (bf16[512,256]{1,0:T(8,128)(2,1)S(1)}, bf16[512,256]{1,0:T(8,128)(2,1)}, u32[]{:S(2)}) copy-start(bf16[512,256]{1,0:T(8,128)(2,1)} %q_ref.3) | copy-start | bytes 786436
  6.5 103.0 %all-gather.4.cloned.1.call-start = ((), (), s32[]{:S(2)}) async-start(), calls=%async_computation.1 | async-start | bytes 4718592 | tf_op jit(solution)/shard_map/all_gather | solution.py:124
  6.5 20.9 %collective-permute-start = (bf16[512,128]{1,0:T(8,128)(2,1)}, bf16[512,128]{1,0:T(8,128)(2,1)S(1)}, u32[]{:S(2)}, u32[]{:S(2)}) collective-permute-start(bf16[512,128]{1,0:T(8,128)(2,1)} %param.11), channel_id=1, source_target_pairs={{0,0},{1,16},{2,32},{3,48},{16,1},{17,17},{18,33},{19,49},{32,2},{... | collective-permute-start | bytes 393224 | tf_op jit(solution)/shard_map/ppermute | solution.py:120
  12.6 22.6 %collective-permute-start.4 = (bf16[256,512]{1,0:T(8,128)(2,1)S(1)}, bf16[256,512]{1,0:T(8,128)(2,1)S(1)}, u32[]{:S(2)}, u32[]{:S(2)}) collective-permute-start(bf16[256,512]{1,0:T(8,128)(2,1)S(1)} %get-tuple-element.21), channel_id=1, source_target_pairs={{0,16},{16,32},{32,48},{48,0},{1,17},{17,33},{33,49},{49,1},{2,18}... | collective-permute-start | bytes 786440 | tf_op jit(solution)/shard_map/ppermute | solution.py:21
  14.6 20.7 %collective-permute-start.5 = (bf16[256,512]{1,0:T(8,128)(2,1)S(1)}, bf16[256,512]{1,0:T(8,128)(2,1)S(1)}, u32[]{:S(2)}, u32[]{:S(2)}) collective-permute-start(bf16[256,512]{1,0:T(8,128)(2,1)S(1)} %get-tuple-element.21), channel_id=1, source_target_pairs={{0,48},{16,0},{32,16},{48,32},{1,49},{17,1},{33,17},{49,33},{2,50}... | collective-permute-start | bytes 786440 | tf_op jit(solution)/shard_map/ppermute | solution.py:21
  20.1 9.8 %collective-permute-start.1 = (bf16[512,128]{1,0:T(8,128)(2,1)}, bf16[512,128]{1,0:T(8,128)(2,1)S(1)}, u32[]{:S(2)}, u32[]{:S(2)}) collective-permute-start(bf16[512,128]{1,0:T(8,128)(2,1)} %param.11), channel_id=1, source_target_pairs={{0,16},{1,0},{2,48},{3,32},{16,17},{17,1},{18,49},{19,33},{32,18},... | collective-permute-start | bytes 393224 | tf_op jit(solution)/shard_map/ppermute | solution.py:120
  25.5 7.9 %collective-permute-start.2 = (bf16[512,128]{1,0:T(8,128)(2,1)}, bf16[512,128]{1,0:T(8,128)(2,1)S(1)}, u32[]{:S(2)}, u32[]{:S(2)}) collective-permute-start(bf16[512,128]{1,0:T(8,128)(2,1)} %param.11), channel_id=1, source_target_pairs={{0,32},{1,48},{2,0},{3,16},{16,33},{17,49},{18,1},{19,17},{32,34},... | collective-permute-start | bytes 393224 | tf_op jit(solution)/shard_map/ppermute | solution.py:120
  27.5 7.8 %collective-permute-start.3 = (bf16[512,128]{1,0:T(8,128)(2,1)}, bf16[512,128]{1,0:T(8,128)(2,1)S(1)}, u32[]{:S(2)}, u32[]{:S(2)}) collective-permute-start(bf16[512,128]{1,0:T(8,128)(2,1)} %param.11), channel_id=1, source_target_pairs={{0,48},{1,32},{2,16},{3,0},{16,49},{17,33},{18,17},{19,1},{32,50},... | collective-permute-start | bytes 393224 | tf_op jit(solution)/shard_map/ppermute | solution.py:120
  36.2 10.6 %collective-permute-start.6 = (bf16[256,512]{1,0:T(8,128)(2,1)S(1)}, bf16[256,512]{1,0:T(8,128)(2,1)S(1)}, u32[]{:S(2)}, u32[]{:S(2)}) collective-permute-start(bf16[256,512]{1,0:T(8,128)(2,1)S(1)} %get-tuple-element.21), channel_id=1, source_target_pairs={{0,32},{16,48},{32,0},{48,16},{1,33},{17,49},{33,1},{49,17},{2,34}... | collective-permute-start | bytes 786440 | tf_op jit(solution)/shard_map/ppermute | solution.py:21
  46.8 9.0 %collective-permute-start.7 = (bf16[64,512]{1,0:T(8,128)(2,1)S(1)}, bf16[64,512]{1,0:T(8,128)(2,1)S(1)}, u32[]{:S(2)}, u32[]{:S(2)}) collective-permute-start(bf16[64,512]{1,0:T(8,128)(2,1)S(1)} %fusion.1), channel_id=1, source_target_pairs={{0,64},{64,0},{128,192},{192,128},{256,320},{320,256},{384,448},{4... | collective-permute-start | bytes 196616 | tf_op jit(solution)/shard_map/ppermute | solution.py:25
  52.1 1.0 copy-start.1
  53.0 0.9 copy-start.3
  55.8 11.5 %collective-permute-start.10 = (bf16[64,512]{1,0:T(8,128)(2,1)S(1)}, bf16[64,512]{1,0:T(8,128)(2,1)S(1)}, u32[]{:S(2)}, u32[]{:S(2)}) collective-permute-start(bf16[64,512]{1,0:T(8,128)(2,1)S(1)} %add_convert_fusion.2), channel_id=1, source_target_pairs={{0,384},{64,448},{128,256},{192,320},{256,128},{320,192},{384,0},{... | collective-permute-start | bytes 196616 | tf_op jit(solution)/shard_map/ppermute | solution.py:25
  60.8 12.9 %collective-permute-start.9 = (bf16[64,512]{1,0:T(8,128)(2,1)S(1)}, bf16[64,512]{1,0:T(8,128)(2,1)S(1)}, u32[]{:S(2)}, u32[]{:S(2)}) collective-permute-start(bf16[64,512]{1,0:T(8,128)(2,1)S(1)} %add_convert_fusion.2), channel_id=1, source_target_pairs={{0,256},{64,320},{128,384},{192,448},{256,0},{320,64},{384,128},{4... | collective-permute-start | bytes 196616 | tf_op jit(solution)/shard_map/ppermute | solution.py:25
  65.4 10.9 %collective-permute-start.8 = (bf16[64,512]{1,0:T(8,128)(2,1)S(1)}, bf16[64,512]{1,0:T(8,128)(2,1)S(1)}, u32[]{:S(2)}, u32[]{:S(2)}) collective-permute-start(bf16[64,512]{1,0:T(8,128)(2,1)S(1)} %add_convert_fusion.2), channel_id=1, source_target_pairs={{0,128},{64,192},{128,0},{192,64},{256,384},{320,448},{384,256},{4... | collective-permute-start | bytes 196616 | tf_op jit(solution)/shard_map/ppermute | solution.py:25
  89.9 12.5 %collective-permute-start.12 = (bf16[512,512]{1,0:T(8,128)(2,1)S(1)}, bf16[512,512]{1,0:T(8,128)(2,1)S(1)}, u32[]{:S(2)}, u32[]{:S(2)}) collective-permute-start(bf16[512,512]{1,0:T(8,128)(2,1)S(1)} %shard_map.65.o0_ref), channel_id=1, source_target_pairs={{0,2},{2,0},{1,3},{3,1},{4,6},{6,4},{5,7},{7,5},{8,10},{10,8},{9,1... | collective-permute-start | bytes 1572872 | tf_op jit(solution)/shard_map/ppermute | solution.py:29
  92.9 15.1 %collective-permute-start.11 = (bf16[512,512]{1,0:T(8,128)(2,1)S(1)}, bf16[512,512]{1,0:T(8,128)(2,1)S(1)}, u32[]{:S(2)}, u32[]{:S(2)}) collective-permute-start(bf16[512,512]{1,0:T(8,128)(2,1)S(1)} %shard_map.65.o0_ref), channel_id=1, source_target_pairs={{0,1},{1,0},{2,3},{3,2},{4,5},{5,4},{6,7},{7,6},{8,9},{9,8},{10,11... | collective-permute-start | bytes 1572872 | tf_op jit(solution)/shard_map/ppermute | solution.py:29
  102.4 7.1 %collective-permute-start.13 = (bf16[512,512]{1,0:T(8,128)(2,1)S(1)}, bf16[512,512]{1,0:T(8,128)(2,1)S(1)}, u32[]{:S(2)}, u32[]{:S(2)}) collective-permute-start(bf16[512,512]{1,0:T(8,128)(2,1)S(1)} %collective-permute-done.12.o2_ref), channel_id=1, source_target_pairs={{0,1},{1,0},{2,3},{3,2},{4,5},{5,4},{6,7},{7,6},{8,9},{9,8},{10,11... | collective-permute-start | bytes 1572872 | tf_op jit(solution)/shard_map/ppermute | solution.py:29
Sparse Core Ops, SparseCore 0:
  36.3 66.4 all-gather.3

commit v3 on v2

--- a/solution.py
+++ b/solution.py
@@ -112,17 +112,20 @@
 
     state = lax.dot_general(keys, values, (((0,), (0,)), ((), ())), preferred_element_type=F32)
     sent = state.astype(BF16)
-    after, across, before = shifted(sent, "x", 1), shifted(sent, "x", 2), shifted(sent, "x", -1)
+    piece = key_size // nx
+    quarter = lax.dynamic_slice_in_dim(state, x * piece, piece)
+    parts = []
+    for by in range(1, nx):
+        mine = lax.dynamic_slice_in_dim(sent, (x + by) % nx * piece, piece)
+        parts.append(shifted(mine, "x", by))
 
     got = []
     for k in range(nu):
         pairs = [(i * nu + j, (j ^ k) * nu + i) for i in range(nx) for j in range(nu)]
         got.append(lax.ppermute(out_weight, ("x",) + QUAD, pairs))
-    *got, after, before = lax.optimization_barrier((*got, after, before))
-    weight = jnp.stack(got)
-
-    gathered = lax.all_gather(weight, "y", axis=0)
-
+    for part in parts:
+        quarter = quarter + part.astype(F32)
+    beside = crossed(quarter.astype(BF16), "y", 1)
     local, lam = pl.pallas_call(
         local_kernel,
         out_shape=(
@@ -134,13 +137,14 @@
         compiler_params=PARAMS,
     )(coef_table, level_index, queries, keys, values)
 
-    piece = key_size // nx
-    start = x * piece
-    quarter = lax.dynamic_slice_in_dim(state, start, piece)
-    for other in (after, across, before):
-        quarter = quarter + lax.dynamic_slice_in_dim(other, start, piece).astype(F32)
-    pair = (across.astype(F32) + jnp.where(x == 2, after, before).astype(F32)).astype(BF16)
-    beside = crossed(quarter.astype(BF16), "y", 1)
+    *got, beside, local = lax.optimization_barrier((*got, beside, local))
+    weight = jnp.stack(got)
+    gathered = lax.all_gather(weight, "y", axis=0)
+
+    late, beside = lax.optimization_barrier((sent, beside))
+    near = crossed(late, "x", 1)
+    pair = crossed((state + near.astype(F32)).astype(BF16), "x", 2)
+
     both = (quarter + beside.astype(F32)).astype(BF16)
     third, fourth, fifth = crossed(both, "y", 2), crossed(both, "y", 4), crossed(both, "y", 6)
     far = [beside, third, (fourth.astype(F32) + fifth.astype(F32)).astype(BF16)]
@@ -154,7 +158,7 @@
         in_specs=[SMEM] + [VMEM] * 6,
         out_specs=VMEM,
         compiler_params=PARAMS,
-    )(block, local, lam, queries, after, pair, far)
+    )(block, local, lam, queries, near, pair, far)
 
     o_z = flipped(o, "zl")
     o_c = flipped(o, "core")

time: 161 us -> 155 us (0.963)
  waiting for transfers between devices: 25.4 us -> 11.1 us
  starting transfers between devices: 55.9 us -> 62.8 us
    ppermute x4 -> x6, starting transfers between devices: 15 us -> 22.6 us  [crossed(): lax.ppermute(value, axis, [(i, i ^ by) for i in range(lax.axis_size(axis))])]
    ppermute x3, waiting for transfers between devices: 5.94 us -> 0.01 us  [shifted(): return lax.ppermute(value, axis, [(i, (i + by) % n) for i in range(n)])]
    ppermute x4, waiting for transfers between devices: 5.33 us -> 0.01 us  [on_device(): got.append(lax.ppermute(out_weight, ('x',) + QUAD, pairs))]
    ppermute x4 -> x6, waiting for transfers between devices: 8.89 us -> 5.42 us  [crossed(): lax.ppermute(value, axis, [(i, i ^ by) for i in range(lax.axis_size(axis))])]
    all_to_all x1, blocking collectives: 38.8 us -> 36.4 us  [on_device(): back = lax.all_to_all(part, TP, 0, 0, tiled=True)]
    all_gather x1, blocking collectives: 12.6 us -> 14.8 us  [on_device(): far = lax.all_gather(jnp.stack(far), 'x', axis=0)]
    ppermute x3, starting transfers between devices: 12.1 us -> 10.2 us  [shifted(): return lax.ppermute(value, axis, [(i, (i + by) % n) for i in range(n)])]
  transfers between devices with their start and end apart: 15 -> 17, of which waited for: 7 -> 5; matrix products, arithmetic and copies ran while one was open for 2% -> 1% of each run, Pallas kernels for 2% -> 2%
where the time goes in v3:
time: 155 us; the launch traced here: 154 us
  starting transfers between devices  62.8 us (41%)
  blocking collectives  51.2 us (33%)
  between operations  13.7 us (9%)
  waiting for transfers between devices  11.1 us (7%)
  Pallas kernels  8.28 us (5%)
  local copies, waits for them, and re-layouts  4.59 us (3%)
    all_to_all x1, blocking collectives, on_device(): back = lax.all_to_all(part, TP, 0, 0, tiled=True)  36.4 us
    ppermute x6, starting transfers between devices, crossed(): lax.ppermute(value, axis, [(i, i ^ by) for i in range(lax.axis_size(axis))])  22.6 us
    ppermute x4, starting transfers between devices, on_device(): got.append(lax.ppermute(out_weight, ('x',) + QUAD, pairs))  15.9 us
    all_gather x1, blocking collectives, on_device(): far = lax.all_gather(jnp.stack(far), 'x', axis=0)  14.8 us
    ppermute x3, starting transfers between devices, flipped(): return lax.ppermute(value, axis, [(0, 1), (1, 0)])  14.1 us
    ppermute x3, starting transfers between devices, shifted(): return lax.ppermute(value, axis, [(i, (i + by) % n) for i in range(n)])  10.2 us
    ppermute x3, waiting for transfers between devices, flipped(): return lax.ppermute(value, axis, [(0, 1), (1, 0)])  5.51 us
    ppermute x6, waiting for transfers between devices, crossed(): lax.ppermute(value, axis, [(i, i ^ by) for i in range(lax.axis_size(axis))])  5.42 us
  transfers between devices with their start and end apart: 17, of which 5 were waited for; matrix products, arithmetic and copies ran while one was open for 1% of the time, Pallas kernels for 2%

profile of v3, /device:TPU:1, one launch (start us, length us, event | category | flops | bytes accessed | tf_op | source)
XLA Modules:
  0.0 154.3 jit_solution(13966120406698608306)
XLA Ops:
  6.5 1.5 fusion.2
  8.1 5.2 %collective-permute-start.6 = (bf16[64,512]{1,0:T(8,128)(2,1)S(1)}, bf16[64,512]{1,0:T(8,128)(2,1)S(1)}, u32[]{:S(2)}, u32[]{:S(2)}) collective-permute-start(bf16[64,512]{1,0:T(8,128)(2,1)S(1)} %get-tuple-element.26), channel_id=1, source_target_pairs={{0,48},{16,0},{32,16},{48,32},{1,49},{17,1},{33,17},{49,33},{2,50}... | collective-permute-start | bytes 196616 | tf_op jit(solution)/shard_map/ppermute | solution.py:21
  13.3 2.4 %collective-permute-start.5 = (bf16[64,512]{1,0:T(8,128)(2,1)S(1)}, bf16[64,512]{1,0:T(8,128)(2,1)S(1)}, u32[]{:S(2)}, u32[]{:S(2)}) collective-permute-start(bf16[64,512]{1,0:T(8,128)(2,1)S(1)} %get-tuple-element.27), channel_id=1, source_target_pairs={{0,32},{16,48},{32,0},{48,16},{1,33},{17,49},{33,1},{49,17},{2,34}... | collective-permute-start | bytes 196616 | tf_op jit(solution)/shard_map/ppermute | solution.py:21
  15.7 2.5 %collective-permute-start.4 = (bf16[64,512]{1,0:T(8,128)(2,1)S(1)}, bf16[64,512]{1,0:T(8,128)(2,1)S(1)}, u32[]{:S(2)}, u32[]{:S(2)}) collective-permute-start(bf16[64,512]{1,0:T(8,128)(2,1)S(1)} %get-tuple-element.25), channel_id=1, source_target_pairs={{0,16},{16,32},{32,48},{48,0},{1,17},{17,33},{33,49},{49,1},{2,18}... | collective-permute-start | bytes 196616 | tf_op jit(solution)/shard_map/ppermute | solution.py:21
  18.3 7.5 %collective-permute-start = (bf16[512,128]{1,0:T(8,128)(2,1)}, bf16[512,128]{1,0:T(8,128)(2,1)S(1)}, u32[]{:S(2)}, u32[]{:S(2)}) collective-permute-start(bf16[512,128]{1,0:T(8,128)(2,1)} %param.11), channel_id=1, source_target_pairs={{0,0},{1,16},{2,32},{3,48},{16,1},{17,17},{18,33},{19,49},{32,2},{... | collective-permute-start | bytes 393224 | tf_op jit(solution)/shard_map/ppermute | solution.py:125
  25.7 1.9 %collective-permute-start.1 = (bf16[512,128]{1,0:T(8,128)(2,1)}, bf16[512,128]{1,0:T(8,128)(2,1)S(1)}, u32[]{:S(2)}, u32[]{:S(2)}) collective-permute-start(bf16[512,128]{1,0:T(8,128)(2,1)} %param.11), channel_id=1, source_target_pairs={{0,16},{1,0},{2,48},{3,32},{16,17},{17,1},{18,49},{19,33},{32,18},... | collective-permute-start | bytes 393224 | tf_op jit(solution)/shard_map/ppermute | solution.py:125
  27.7 3.1 %collective-permute-start.2 = (bf16[512,128]{1,0:T(8,128)(2,1)}, bf16[512,128]{1,0:T(8,128)(2,1)S(1)}, u32[]{:S(2)}, u32[]{:S(2)}) collective-permute-start(bf16[512,128]{1,0:T(8,128)(2,1)} %param.11), channel_id=1, source_target_pairs={{0,32},{1,48},{2,0},{3,16},{16,33},{17,49},{18,1},{19,17},{32,34},... | collective-permute-start | bytes 393224 | tf_op jit(solution)/shard_map/ppermute | solution.py:125
  30.8 3.4 %collective-permute-start.3 = (bf16[512,128]{1,0:T(8,128)(2,1)}, bf16[512,128]{1,0:T(8,128)(2,1)S(1)}, u32[]{:S(2)}, u32[]{:S(2)}) collective-permute-start(bf16[512,128]{1,0:T(8,128)(2,1)} %param.11), channel_id=1, source_target_pairs={{0,48},{1,32},{2,16},{3,0},{16,49},{17,33},{18,17},{19,1},{32,50},... | collective-permute-start | bytes 393224 | tf_op jit(solution)/shard_map/ppermute | solution.py:125
  34.3 2.3 %collective-permute-start.7 = (bf16[64,512]{1,0:T(8,128)(2,1)S(1)}, bf16[64,512]{1,0:T(8,128)(2,1)S(1)}, u32[]{:S(2)}, u32[]{:S(2)}) collective-permute-start(bf16[64,512]{1,0:T(8,128)(2,1)S(1)} %fusion.1), channel_id=1, source_target_pairs={{0,64},{64,0},{128,192},{192,128},{256,320},{320,256},{384,448},{4... | collective-permute-start | bytes 196616 | tf_op jit(solution)/shard_map/ppermute | solution.py:25
  37.3 0.9 copy.10.index_ref
  38.2 1.0 copy-done
  39.3 0.9 copy-done.1
  40.2 0.9 copy-done.3
  41.1 1.8 %shard_map.64 = (f32[512,512]{1,0:T(8,128)S(1)}, f32[512,15]{1,0:T(8,128)S(1)}) custom-call(f32[16,1]{1,0:T(8,128)S(1)} %copy.9.coef_ref, s32[512,15]{1,0:T(8,128)S(1)} %copy.10.index_ref, bf16[512,256]{1,0:T(8,128)(2,1)S(1)} %copy-done.1, bf16[512,256]{1,0:T(8,128)(2,1)S(1)} %copy-done.3, bf16[512,512]{1,0:T(8,128)(2,1)S(1)} %copy-done), custom_call_target="tpu_custom_call" | custom-call | tf_op jit(solution)/shard_map/pallas_call | solution.py:129
  43.0 0.9 pad_maximum_fusion
  43.9 5.0 %collective-permute-start.12 = (bf16[64,512]{1,0:T(8,128)(2,1)S(1)}, bf16[64,512]{1,0:T(8,128)(2,1)S(1)}, u32[]{:S(2)}, u32[]{:S(2)}) collective-permute-start(bf16[64,512]{1,0:T(8,128)(2,1)S(1)} %add_convert_fusion.2), channel_id=1, source_target_pairs={{0,384},{64,448},{128,256},{192,320},{256,128},{320,192},{384,0},{... | collective-permute-start | bytes 196616 | tf_op jit(solution)/shard_map/ppermute | solution.py:25
  48.9 4.4 %collective-permute-start.11 = (bf16[64,512]{1,0:T(8,128)(2,1)S(1)}, bf16[64,512]{1,0:T(8,128)(2,1)S(1)}, u32[]{:S(2)}, u32[]{:S(2)}) collective-permute-start(bf16[64,512]{1,0:T(8,128)(2,1)S(1)} %add_convert_fusion.2), channel_id=1, source_target_pairs={{0,256},{64,320},{128,384},{192,448},{256,0},{320,64},{384,128},{4... | collective-permute-start | bytes 196616 | tf_op jit(solution)/shard_map/ppermute | solution.py:25
  53.4 2.0 %collective-permute-start.10 = (bf16[64,512]{1,0:T(8,128)(2,1)S(1)}, bf16[64,512]{1,0:T(8,128)(2,1)S(1)}, u32[]{:S(2)}, u32[]{:S(2)}) collective-permute-start(bf16[64,512]{1,0:T(8,128)(2,1)S(1)} %add_convert_fusion.2), channel_id=1, source_target_pairs={{0,128},{64,192},{128,0},{192,64},{256,384},{320,448},{384,256},{4... | collective-permute-start | bytes 196616 | tf_op jit(solution)/shard_map/ppermute | solution.py:25
  55.3 5.3 %collective-permute-start.8 = (bf16[256,512]{1,0:T(8,128)(2,1)S(1)}, bf16[256,512]{1,0:T(8,128)(2,1)S(1)}, u32[]{:S(2)}, u32[]{:S(2)}) collective-permute-start(bf16[256,512]{1,0:T(8,128)(2,1)S(1)} %get-tuple-element.19), channel_id=1, source_target_pairs={{0,16},{16,0},{32,48},{48,32},{1,17},{17,1},{33,49},{49,33},{2,18}... | collective-permute-start | bytes 786440 | tf_op jit(solution)/shard_map/ppermute | solution.py:25
  60.7 1.6 %collective-permute-done.10 = bf16[64,512]{1,0:T(8,128)(2,1)S(1)} collective-permute-done((bf16[64,512]{1,0:T(8,128)(2,1)S(1)}, bf16[64,512]{1,0:T(8,128)(2,1)S(1)}, u32[]{:S(2)}, u32[]{:S(2)}) %collective-permute-start.10) | collective-permute-done | bytes 65568 | tf_op jit(solution)/shard_map/ppermute | solution.py:25
  62.4 3.8 %collective-permute-done.8.near_ref = bf16[256,512]{1,0:T(8,128)(2,1)S(1)} collective-permute-done((bf16[256,512]{1,0:T(8,128)(2,1)S(1)}, bf16[256,512]{1,0:T(8,128)(2,1)S(1)}, u32[]{:S(2)}, u32[]{:S(2)}) %collective-permute-start.8) | collective-permute-done | bytes 262176 | tf_op jit(solution)/shard_map/ppermute | solution.py:25
  66.2 3.6 %collective-permute-start.9 = (bf16[256,512]{1,0:T(8,128)(2,1)S(1)}, bf16[256,512]{1,0:T(8,128)(2,1)S(1)}, u32[]{:S(2)}, u32[]{:S(2)}) collective-permute-start(bf16[256,512]{1,0:T(8,128)(2,1)S(1)} %add_convert_fusion), channel_id=1, source_target_pairs={{0,32},{16,48},{32,0},{48,16},{1,33},{17,49},{33,1},{49,17},{2,34}... | collective-permute-start | bytes 786440 | tf_op jit(solution)/shard_map/ppermute | solution.py:25
  69.9 14.8 %all-gather = bf16[12,64,512]{2,1,0:T(8,128)(2,1)S(1)} all-gather(bf16[3,64,512]{2,1,0:T(8,128)(2,1)S(1)} %pad_maximum_fusion.1), channel_id=2, replica_groups=mesh['y'=8,'x'=4,'zh'=4,'zl'=2,'core'=2] {'x'}, dimensions={0}, use_global_device_ids=true | all-gather | bytes 983040 | tf_op jit(solution)/shard_map/all_gather | solution.py:151
  84.7 0.9 shard_map.65.o0_ref
  85.6 1.9 %collective-permute-start.14 = (bf16[512,512]{1,0:T(8,128)(2,1)S(1)}, bf16[512,512]{1,0:T(8,128)(2,1)S(1)}, u32[]{:S(2)}, u32[]{:S(2)}) collective-permute-start(bf16[512,512]{1,0:T(8,128)(2,1)S(1)} %shard_map.65.o0_ref), channel_id=1, source_target_pairs={{0,2},{2,0},{1,3},{3,1},{4,6},{6,4},{5,7},{7,5},{8,10},{10,8},{9,1... | collective-permute-start | bytes 1572872 | tf_op jit(solution)/shard_map/ppermute | solution.py:29
  87.5 6.0 %collective-permute-start.13 = (bf16[512,512]{1,0:T(8,128)(2,1)S(1)}, bf16[512,512]{1,0:T(8,128)(2,1)S(1)}, u32[]{:S(2)}, u32[]{:S(2)}) collective-permute-start(bf16[512,512]{1,0:T(8,128)(2,1)S(1)} %shard_map.65.o0_ref), channel_id=1, source_target_pairs={{0,1},{1,0},{2,3},{3,2},{4,5},{5,4},{6,7},{7,6},{8,9},{9,8},{10,11... | collective-permute-start | bytes 1572872 | tf_op jit(solution)/shard_map/ppermute | solution.py:29
  93.5 4.0 %collective-permute-done.14.o2_ref = bf16[512,512]{1,0:T(8,128)(2,1)S(1)} collective-permute-done((bf16[512,512]{1,0:T(8,128)(2,1)S(1)}, bf16[512,512]{1,0:T(8,128)(2,1)S(1)}, u32[]{:S(2)}, u32[]{:S(2)}) %collective-permute-start.14) | collective-permute-done | bytes 524320 | tf_op jit(solution)/shard_map/ppermute | solution.py:29
  97.5 6.2 %collective-permute-start.15 = (bf16[512,512]{1,0:T(8,128)(2,1)S(1)}, bf16[512,512]{1,0:T(8,128)(2,1)S(1)}, u32[]{:S(2)}, u32[]{:S(2)}) collective-permute-start(bf16[512,512]{1,0:T(8,128)(2,1)S(1)} %collective-permute-done.14.o2_ref), channel_id=1, source_target_pairs={{0,1},{1,0},{2,3},{3,2},{4,5},{5,4},{6,7},{7,6},{8,9},{9,8},{10,11... | collective-permute-start | bytes 1572872 | tf_op jit(solution)/shard_map/ppermute | solution.py:29
  103.8 1.5 collective-permute-done.15.o3_ref
  105.4 4.7 %shard_map.66 = bf16[512,1024]{1,0:T(8,128)(2,1)S(1)} custom-call(s32[1]{0:T(128)} %bitcast.flip_ref, bf16[512,512]{1,0:T(8,128)(2,1)S(1)} %shard_map.65.o0_ref, bf16[512,512]{1,0:T(8,128)(2,1)S(1)} %collective-permute-done.13.o1_ref, bf16[512,512]{1,0:T(8,128)(2,1)S(1)} %collective-permute-done.14.o2_ref, ...), custom_call_target="tpu_custom_call" | custom-call | tf_op jit(solution)/shard_map/pallas_call | solution.py:169
  110.2 36.4 %all_to_all.9 = bf16[16,32,1024]{2,1,0:T(8,128)(2,1)S(1)} all-to-all(bf16[16,32,1024]{2,1,0:T(8,128)(2,1)S(1)} %bitcast.17), channel_id=1, replica_groups=mesh['y'=8,'x'=4,'zh'=4,'zl'=2,'core'=2] {'zh','zl','core'}, dimensions={0} | all-to-all | bytes 2097152 | tf_op jit(solution)/shard_map/all_to_all | solution.py:181
  146.6 0.8 shard_map.67
  (27 shorter events, 1.2 us)
Async XLA Ops:
  6.5 98.9 %all-gather.4.cloned.1.call-start = ((), (), s32[]{:S(2)}) async-start(), calls=%async_computation.1 | async-start | bytes 4718592 | tf_op jit(solution)/shard_map/all_gather | solution.py:142
  6.5 78.1 %copy-start.2 = (bf16[512,256]{1,0:T(8,128)(2,1)S(1)}, bf16[512,256]{1,0:T(8,128)(2,1)}, u32[]{:S(2)}) copy-start(bf16[512,256]{1,0:T(8,128)(2,1)} %q_ref.3) | copy-start | bytes 786436
  8.1 19.6 %collective-permute-start.6 = (bf16[64,512]{1,0:T(8,128)(2,1)S(1)}, bf16[64,512]{1,0:T(8,128)(2,1)S(1)}, u32[]{:S(2)}, u32[]{:S(2)}) collective-permute-start(bf16[64,512]{1,0:T(8,128)(2,1)S(1)} %get-tuple-element.26), channel_id=1, source_target_pairs={{0,48},{16,0},{32,16},{48,32},{1,49},{17,1},{33,17},{49,33},{2,50}... | collective-permute-start | bytes 196616 | tf_op jit(solution)/shard_map/ppermute | solution.py:21
  13.3 17.5 %collective-permute-start.5 = (bf16[64,512]{1,0:T(8,128)(2,1)S(1)}, bf16[64,512]{1,0:T(8,128)(2,1)S(1)}, u32[]{:S(2)}, u32[]{:S(2)}) collective-permute-start(bf16[64,512]{1,0:T(8,128)(2,1)S(1)} %get-tuple-element.27), channel_id=1, source_target_pairs={{0,32},{16,48},{32,0},{48,16},{1,33},{17,49},{33,1},{49,17},{2,34}... | collective-permute-start | bytes 196616 | tf_op jit(solution)/shard_map/ppermute | solution.py:21
  15.7 18.5 %collective-permute-start.4 = (bf16[64,512]{1,0:T(8,128)(2,1)S(1)}, bf16[64,512]{1,0:T(8,128)(2,1)S(1)}, u32[]{:S(2)}, u32[]{:S(2)}) collective-permute-start(bf16[64,512]{1,0:T(8,128)(2,1)S(1)} %get-tuple-element.25), channel_id=1, source_target_pairs={{0,16},{16,32},{32,48},{48,0},{1,17},{17,33},{33,49},{49,1},{2,18}... | collective-permute-start | bytes 196616 | tf_op jit(solution)/shard_map/ppermute | solution.py:21
  18.3 24.7 %collective-permute-start = (bf16[512,128]{1,0:T(8,128)(2,1)}, bf16[512,128]{1,0:T(8,128)(2,1)S(1)}, u32[]{:S(2)}, u32[]{:S(2)}) collective-permute-start(bf16[512,128]{1,0:T(8,128)(2,1)} %param.11), channel_id=1, source_target_pairs={{0,0},{1,16},{2,32},{3,48},{16,1},{17,17},{18,33},{19,49},{32,2},{... | collective-permute-start | bytes 393224 | tf_op jit(solution)/shard_map/ppermute | solution.py:125
  25.7 17.2 %collective-permute-start.1 = (bf16[512,128]{1,0:T(8,128)(2,1)}, bf16[512,128]{1,0:T(8,128)(2,1)S(1)}, u32[]{:S(2)}, u32[]{:S(2)}) collective-permute-start(bf16[512,128]{1,0:T(8,128)(2,1)} %param.11), channel_id=1, source_target_pairs={{0,16},{1,0},{2,48},{3,32},{16,17},{17,1},{18,49},{19,33},{32,18},... | collective-permute-start | bytes 393224 | tf_op jit(solution)/shard_map/ppermute | solution.py:125
  27.7 15.3 %collective-permute-start.2 = (bf16[512,128]{1,0:T(8,128)(2,1)}, bf16[512,128]{1,0:T(8,128)(2,1)S(1)}, u32[]{:S(2)}, u32[]{:S(2)}) collective-permute-start(bf16[512,128]{1,0:T(8,128)(2,1)} %param.11), channel_id=1, source_target_pairs={{0,32},{1,48},{2,0},{3,16},{16,33},{17,49},{18,1},{19,17},{32,34},... | collective-permute-start | bytes 393224 | tf_op jit(solution)/shard_map/ppermute | solution.py:125
  30.8 12.1 %collective-permute-start.3 = (bf16[512,128]{1,0:T(8,128)(2,1)}, bf16[512,128]{1,0:T(8,128)(2,1)S(1)}, u32[]{:S(2)}, u32[]{:S(2)}) collective-permute-start(bf16[512,128]{1,0:T(8,128)(2,1)} %param.11), channel_id=1, source_target_pairs={{0,48},{1,32},{2,16},{3,0},{16,49},{17,33},{18,17},{19,1},{32,50},... | collective-permute-start | bytes 393224 | tf_op jit(solution)/shard_map/ppermute | solution.py:125
  34.3 8.7 %collective-permute-start.7 = (bf16[64,512]{1,0:T(8,128)(2,1)S(1)}, bf16[64,512]{1,0:T(8,128)(2,1)S(1)}, u32[]{:S(2)}, u32[]{:S(2)}) collective-permute-start(bf16[64,512]{1,0:T(8,128)(2,1)S(1)} %fusion.1), channel_id=1, source_target_pairs={{0,64},{64,0},{128,192},{192,128},{256,320},{320,256},{384,448},{4... | collective-permute-start | bytes 196616 | tf_op jit(solution)/shard_map/ppermute | solution.py:25
  38.2 1.0 copy-start
  39.2 0.9 copy-start.1
  40.2 0.9 copy-start.3
  43.9 16.7 %collective-permute-start.12 = (bf16[64,512]{1,0:T(8,128)(2,1)S(1)}, bf16[64,512]{1,0:T(8,128)(2,1)S(1)}, u32[]{:S(2)}, u32[]{:S(2)}) collective-permute-start(bf16[64,512]{1,0:T(8,128)(2,1)S(1)} %add_convert_fusion.2), channel_id=1, source_target_pairs={{0,384},{64,448},{128,256},{192,320},{256,128},{320,192},{384,0},{... | collective-permute-start | bytes 196616 | tf_op jit(solution)/shard_map/ppermute | solution.py:25
  48.9 11.8 %collective-permute-start.11 = (bf16[64,512]{1,0:T(8,128)(2,1)S(1)}, bf16[64,512]{1,0:T(8,128)(2,1)S(1)}, u32[]{:S(2)}, u32[]{:S(2)}) collective-permute-start(bf16[64,512]{1,0:T(8,128)(2,1)S(1)} %add_convert_fusion.2), channel_id=1, source_target_pairs={{0,256},{64,320},{128,384},{192,448},{256,0},{320,64},{384,128},{4... | collective-permute-start | bytes 196616 | tf_op jit(solution)/shard_map/ppermute | solution.py:25
  53.4 9.0 %collective-permute-start.10 = (bf16[64,512]{1,0:T(8,128)(2,1)S(1)}, bf16[64,512]{1,0:T(8,128)(2,1)S(1)}, u32[]{:S(2)}, u32[]{:S(2)}) collective-permute-start(bf16[64,512]{1,0:T(8,128)(2,1)S(1)} %add_convert_fusion.2), channel_id=1, source_target_pairs={{0,128},{64,192},{128,0},{192,64},{256,384},{320,448},{384,256},{4... | collective-permute-start | bytes 196616 | tf_op jit(solution)/shard_map/ppermute | solution.py:25
  55.3 10.8 %collective-permute-start.8 = (bf16[256,512]{1,0:T(8,128)(2,1)S(1)}, bf16[256,512]{1,0:T(8,128)(2,1)S(1)}, u32[]{:S(2)}, u32[]{:S(2)}) collective-permute-start(bf16[256,512]{1,0:T(8,128)(2,1)S(1)} %get-tuple-element.19), channel_id=1, source_target_pairs={{0,16},{16,0},{32,48},{48,32},{1,17},{17,1},{33,49},{49,33},{2,18}... | collective-permute-start | bytes 786440 | tf_op jit(solution)/shard_map/ppermute | solution.py:25
  66.2 18.4 %collective-permute-start.9 = (bf16[256,512]{1,0:T(8,128)(2,1)S(1)}, bf16[256,512]{1,0:T(8,128)(2,1)S(1)}, u32[]{:S(2)}, u32[]{:S(2)}) collective-permute-start(bf16[256,512]{1,0:T(8,128)(2,1)S(1)} %add_convert_fusion), channel_id=1, source_target_pairs={{0,32},{16,48},{32,0},{48,16},{1,33},{17,49},{33,1},{49,17},{2,34}... | collective-permute-start | bytes 786440 | tf_op jit(solution)/shard_map/ppermute | solution.py:25
  85.6 11.9 %collective-permute-start.14 = (bf16[512,512]{1,0:T(8,128)(2,1)S(1)}, bf16[512,512]{1,0:T(8,128)(2,1)S(1)}, u32[]{:S(2)}, u32[]{:S(2)}) collective-permute-start(bf16[512,512]{1,0:T(8,128)(2,1)S(1)} %shard_map.65.o0_ref), channel_id=1, source_target_pairs={{0,2},{2,0},{1,3},{3,1},{4,6},{6,4},{5,7},{7,5},{8,10},{10,8},{9,1... | collective-permute-start | bytes 1572872 | tf_op jit(solution)/shard_map/ppermute | solution.py:29
  87.5 16.2 %collective-permute-start.13 = (bf16[512,512]{1,0:T(8,128)(2,1)S(1)}, bf16[512,512]{1,0:T(8,128)(2,1)S(1)}, u32[]{:S(2)}, u32[]{:S(2)}) collective-permute-start(bf16[512,512]{1,0:T(8,128)(2,1)S(1)} %shard_map.65.o0_ref), channel_id=1, source_target_pairs={{0,1},{1,0},{2,3},{3,2},{4,5},{5,4},{6,7},{7,6},{8,9},{9,8},{10,11... | collective-permute-start | bytes 1572872 | tf_op jit(solution)/shard_map/ppermute | solution.py:29
  97.5 7.7 %collective-permute-start.15 = (bf16[512,512]{1,0:T(8,128)(2,1)S(1)}, bf16[512,512]{1,0:T(8,128)(2,1)S(1)}, u32[]{:S(2)}, u32[]{:S(2)}) collective-permute-start(bf16[512,512]{1,0:T(8,128)(2,1)S(1)} %collective-permute-done.14.o2_ref), channel_id=1, source_target_pairs={{0,1},{1,0},{2,3},{3,2},{4,5},{5,4},{6,7},{7,6},{8,9},{9,8},{10,11... | collective-permute-start | bytes 1572872 | tf_op jit(solution)/shard_map/ppermute | solution.py:29
Sparse Core Ops, SparseCore 0:
  44.0 61.3 all-gather.3

commit v4 on v2

--- a/solution.py
+++ b/solution.py
@@ -111,16 +111,17 @@
     nx, ny, nu = lax.axis_size("x"), lax.axis_size("y"), 4
 
     state = lax.dot_general(keys, values, (((0,), (0,)), ((), ())), preferred_element_type=F32)
-    sent = state.astype(BF16)
-    after, across, before = shifted(sent, "x", 1), shifted(sent, "x", 2), shifted(sent, "x", -1)
+    near = crossed(state.astype(BF16), "x", 1)
 
     got = []
     for k in range(nu):
         pairs = [(i * nu + j, (j ^ k) * nu + i) for i in range(nx) for j in range(nu)]
         got.append(lax.ppermute(out_weight, ("x",) + QUAD, pairs))
-    *got, after, before = lax.optimization_barrier((*got, after, before))
+    two = state + near.astype(F32)
+    pair = crossed(two.astype(BF16), "x", 2)
+
+    *got, near = lax.optimization_barrier((*got, near))
     weight = jnp.stack(got)
-
     gathered = lax.all_gather(weight, "y", axis=0)
 
     local, lam = pl.pallas_call(
@@ -134,12 +135,10 @@
         compiler_params=PARAMS,
     )(coef_table, level_index, queries, keys, values)
 
+    pair, local = lax.optimization_barrier((pair, local))
     piece = key_size // nx
-    start = x * piece
-    quarter = lax.dynamic_slice_in_dim(state, start, piece)
-    for other in (after, across, before):
-        quarter = quarter + lax.dynamic_slice_in_dim(other, start, piece).astype(F32)
-    pair = (across.astype(F32) + jnp.where(x == 2, after, before).astype(F32)).astype(BF16)
+    four = two + pair.astype(F32)
+    quarter = lax.dynamic_slice_in_dim(four, x * piece, piece)
     beside = crossed(quarter.astype(BF16), "y", 1)
     both = (quarter + beside.astype(F32)).astype(BF16)
     third, fourth, fifth = crossed(both, "y", 2), crossed(both, "y", 4), crossed(both, "y", 6)
@@ -154,7 +153,7 @@
         in_specs=[SMEM] + [VMEM] * 6,
         out_specs=VMEM,
         compiler_params=PARAMS,
-    )(block, local, lam, queries, after, pair, far)
+    )(block, local, lam, queries, near, pair, far)
 
     o_z = flipped(o, "zl")
     o_c = flipped(o, "core")

time: 161 us -> 157 us (0.975)
  local copies, waits for them, and re-layouts: 3.53 us -> 0.24 us
  starting transfers between devices: 55.9 us -> 53.3 us
  other arithmetic: 1.11 us -> 3.64 us
    ppermute x3 -> x0, starting transfers between devices: 12.1 us -> none  [shifted(): return lax.ppermute(value, axis, [(i, (i + by) % n) for i in range(n)])]
    ppermute x3 -> x0, waiting for transfers between devices: 5.94 us -> none  [shifted(): return lax.ppermute(value, axis, [(i, (i + by) % n) for i in range(n)])]
    ppermute x4 -> x6, waiting for transfers between devices: 8.89 us -> 14.8 us  [crossed(): lax.ppermute(value, axis, [(i, i ^ by) for i in range(lax.axis_size(axis))])]
    ppermute x4 -> x6, starting transfers between devices: 15 us -> 20.5 us  [crossed(): lax.ppermute(value, axis, [(i, i ^ by) for i in range(lax.axis_size(axis))])]
    ppermute x3, starting transfers between devices: 14.3 us -> 18.3 us  [flipped(): return lax.ppermute(value, axis, [(0, 1), (1, 0)])]
    unnamed x10 -> x12, local copies, waits for them, and re-layouts: 3.53 us -> 0.24 us
  transfers between devices with their start and end apart: 15 -> 14, of which waited for: 7 -> 10; matrix products, arithmetic and copies ran while one was open for 2% -> 2% of each run, Pallas kernels for 2% -> 2%
where the time goes in v4:
time: 157 us; the launch traced here: 156 us
  starting transfers between devices  53.3 us (34%)
  blocking collectives  50.1 us (32%)
  waiting for transfers between devices  25.4 us (16%)
  between operations  13.6 us (9%)
  Pallas kernels  8.24 us (5%)
  other arithmetic  3.64 us (2%)
    all_to_all x1, blocking collectives, on_device(): back = lax.all_to_all(part, TP, 0, 0, tiled=True)  38.5 us
    ppermute x6, starting transfers between devices, crossed(): lax.ppermute(value, axis, [(i, i ^ by) for i in range(lax.axis_size(axis))])  20.5 us
    ppermute x3, starting transfers between devices, flipped(): return lax.ppermute(value, axis, [(0, 1), (1, 0)])  18.3 us
    ppermute x6, waiting for transfers between devices, crossed(): lax.ppermute(value, axis, [(i, i ^ by) for i in range(lax.axis_size(axis))])  14.8 us
    ppermute x4, starting transfers between devices, on_device(): got.append(lax.ppermute(out_weight, ('x',) + QUAD, pairs))  14.5 us
    all_gather x1, blocking collectives, on_device(): far = lax.all_gather(jnp.stack(far), 'x', axis=0)  11.6 us
    ppermute x4, waiting for transfers between devices, on_device(): got.append(lax.ppermute(out_weight, ('x',) + QUAD, pairs))  6.79 us
    pallas_call x1, Pallas kernels, on_device(): pl.pallas_call(project_kernel, grid=(ny // 2,), out_shape=jax.ShapeDtypeS...  4.74 us
  transfers between devices with their start and end apart: 14, of which 10 were waited for; matrix products, arithmetic and copies ran while one was open for 2% of the time, Pallas kernels for 2%

profile of v4, /device:TPU:1, one launch (start us, length us, event | category | flops | bytes accessed | tf_op | source)
XLA Modules:
  0.0 156.1 jit_solution(16321911624225912894)
XLA Ops:
  6.6 1.5 fusion.3
  8.1 3.9 %collective-permute-start = (bf16[256,512]{1,0:T(8,128)(2,1)S(1)}, bf16[256,512]{1,0:T(8,128)(2,1)S(1)}, u32[]{:S(2)}, u32[]{:S(2)}) collective-permute-start(bf16[256,512]{1,0:T(8,128)(2,1)S(1)} %get-tuple-element.25), channel_id=1, source_target_pairs={{0,16},{16,0},{32,48},{48,32},{1,17},{17,1},{33,49},{49,33},{2,18}... | collective-permute-start | bytes 786440 | tf_op jit(solution)/shard_map/ppermute | solution.py:25
  12.1 8.4 %collective-permute-start.2 = (bf16[512,128]{1,0:T(8,128)(2,1)}, bf16[512,128]{1,0:T(8,128)(2,1)S(1)}, u32[]{:S(2)}, u32[]{:S(2)}) collective-permute-start(bf16[512,128]{1,0:T(8,128)(2,1)} %param.11), channel_id=1, source_target_pairs={{0,0},{1,16},{2,32},{3,48},{16,1},{17,17},{18,33},{19,49},{32,2},{... | collective-permute-start | bytes 393224 | tf_op jit(solution)/shard_map/ppermute | solution.py:119
  20.5 1.9 %collective-permute-start.3 = (bf16[512,128]{1,0:T(8,128)(2,1)}, bf16[512,128]{1,0:T(8,128)(2,1)S(1)}, u32[]{:S(2)}, u32[]{:S(2)}) collective-permute-start(bf16[512,128]{1,0:T(8,128)(2,1)} %param.11), channel_id=1, source_target_pairs={{0,16},{1,0},{2,48},{3,32},{16,17},{17,1},{18,49},{19,33},{32,18},... | collective-permute-start | bytes 393224 | tf_op jit(solution)/shard_map/ppermute | solution.py:119
  22.4 1.9 %collective-permute-start.4 = (bf16[512,128]{1,0:T(8,128)(2,1)}, bf16[512,128]{1,0:T(8,128)(2,1)S(1)}, u32[]{:S(2)}, u32[]{:S(2)}) collective-permute-start(bf16[512,128]{1,0:T(8,128)(2,1)} %param.11), channel_id=1, source_target_pairs={{0,32},{1,48},{2,0},{3,16},{16,33},{17,49},{18,1},{19,17},{32,34},... | collective-permute-start | bytes 393224 | tf_op jit(solution)/shard_map/ppermute | solution.py:119
  24.3 2.3 %collective-permute-start.5 = (bf16[512,128]{1,0:T(8,128)(2,1)}, bf16[512,128]{1,0:T(8,128)(2,1)S(1)}, u32[]{:S(2)}, u32[]{:S(2)}) collective-permute-start(bf16[512,128]{1,0:T(8,128)(2,1)} %param.11), channel_id=1, source_target_pairs={{0,48},{1,32},{2,16},{3,0},{16,49},{17,33},{18,17},{19,1},{32,50},... | collective-permute-start | bytes 393224 | tf_op jit(solution)/shard_map/ppermute | solution.py:119
  27.4 3.9 %collective-permute-done.4 = bf16[512,128]{1,0:T(8,128)(2,1)S(1)} collective-permute-done((bf16[512,128]{1,0:T(8,128)(2,1)}, bf16[512,128]{1,0:T(8,128)(2,1)S(1)}, u32[]{:S(2)}, u32[]{:S(2)}) %collective-permute-start.4) | collective-permute-done | bytes 131104 | tf_op jit(solution)/shard_map/ppermute | solution.py:119
  31.3 2.1 %collective-permute-done.5 = bf16[512,128]{1,0:T(8,128)(2,1)S(1)} collective-permute-done((bf16[512,128]{1,0:T(8,128)(2,1)}, bf16[512,128]{1,0:T(8,128)(2,1)S(1)}, u32[]{:S(2)}, u32[]{:S(2)}) %collective-permute-start.5) | collective-permute-done | bytes 131104 | tf_op jit(solution)/shard_map/ppermute | solution.py:119
  33.4 0.9 pad_maximum_fusion
  34.3 0.9 fusion.2
  35.2 3.2 %collective-permute-start.1 = (bf16[256,512]{1,0:T(8,128)(2,1)S(1)}, bf16[256,512]{1,0:T(8,128)(2,1)S(1)}, u32[]{:S(2)}, u32[]{:S(2)}) collective-permute-start(bf16[256,512]{1,0:T(8,128)(2,1)S(1)} %get-tuple-element.23), channel_id=1, source_target_pairs={{0,32},{16,48},{32,0},{48,16},{1,33},{17,49},{33,1},{49,17},{2,34}... | collective-permute-start | bytes 786440 | tf_op jit(solution)/shard_map/ppermute | solution.py:25
  38.7 1.8 %shard_map.64 = (f32[512,512]{1,0:T(8,128)S(1)}, f32[512,15]{1,0:T(8,128)S(1)}) custom-call(f32[16,1]{1,0:T(8,128)S(1)} %copy.9.coef_ref, s32[512,15]{1,0:T(8,128)S(1)} %copy.10.index_ref, bf16[512,256]{1,0:T(8,128)(2,1)S(1)} %copy-done.1, bf16[512,256]{1,0:T(8,128)(2,1)S(1)} %copy-done.2, bf16[512,512]{1,0:T(8,128)(2,1)S(1)} %copy-done), custom_call_target="tpu_custom_call" | custom-call | tf_op jit(solution)/shard_map/pallas_call | solution.py:127
  40.4 6.3 %collective-permute-done.1.pair_ref = bf16[256,512]{1,0:T(8,128)(2,1)S(1)} collective-permute-done((bf16[256,512]{1,0:T(8,128)(2,1)S(1)}, bf16[256,512]{1,0:T(8,128)(2,1)S(1)}, u32[]{:S(2)}, u32[]{:S(2)}) %collective-permute-start.1) | collective-permute-done | bytes 262176 | tf_op jit(solution)/shard_map/ppermute | solution.py:25
  46.7 0.9 fusion
  47.6 1.9 %collective-permute-start.6 = (bf16[64,512]{1,0:T(8,128)(2,1)S(1)}, bf16[64,512]{1,0:T(8,128)(2,1)S(1)}, u32[]{:S(2)}, u32[]{:S(2)}) collective-permute-start(bf16[64,512]{1,0:T(8,128)(2,1)S(1)} %fusion), channel_id=1, source_target_pairs={{0,64},{64,0},{128,192},{192,128},{256,320},{320,256},{384,448},{4... | collective-permute-start | bytes 196616 | tf_op jit(solution)/shard_map/ppermute | solution.py:25
  49.5 4.4 %collective-permute-done.6 = bf16[64,512]{1,0:T(8,128)(2,1)S(1)} collective-permute-done((bf16[64,512]{1,0:T(8,128)(2,1)S(1)}, bf16[64,512]{1,0:T(8,128)(2,1)S(1)}, u32[]{:S(2)}, u32[]{:S(2)}) %collective-permute-start.6) | collective-permute-done | bytes 65568 | tf_op jit(solution)/shard_map/ppermute | solution.py:25
  54.0 0.9 add_convert_fusion.1
  54.9 4.3 %collective-permute-start.8 = (bf16[64,512]{1,0:T(8,128)(2,1)S(1)}, bf16[64,512]{1,0:T(8,128)(2,1)S(1)}, u32[]{:S(2)}, u32[]{:S(2)}) collective-permute-start(bf16[64,512]{1,0:T(8,128)(2,1)S(1)} %add_convert_fusion.1), channel_id=1, source_target_pairs={{0,256},{64,320},{128,384},{192,448},{256,0},{320,64},{384,128},{4... | collective-permute-start | bytes 196616 | tf_op jit(solution)/shard_map/ppermute | solution.py:25
  59.2 2.0 %collective-permute-start.9 = (bf16[64,512]{1,0:T(8,128)(2,1)S(1)}, bf16[64,512]{1,0:T(8,128)(2,1)S(1)}, u32[]{:S(2)}, u32[]{:S(2)}) collective-permute-start(bf16[64,512]{1,0:T(8,128)(2,1)S(1)} %add_convert_fusion.1), channel_id=1, source_target_pairs={{0,384},{64,448},{128,256},{192,320},{256,128},{320,192},{384,0},{... | collective-permute-start | bytes 196616 | tf_op jit(solution)/shard_map/ppermute | solution.py:25
  61.2 5.1 %collective-permute-start.7 = (bf16[64,512]{1,0:T(8,128)(2,1)S(1)}, bf16[64,512]{1,0:T(8,128)(2,1)S(1)}, u32[]{:S(2)}, u32[]{:S(2)}) collective-permute-start(bf16[64,512]{1,0:T(8,128)(2,1)S(1)} %add_convert_fusion.1), channel_id=1, source_target_pairs={{0,128},{64,192},{128,0},{192,64},{256,384},{320,448},{384,256},{4... | collective-permute-start | bytes 196616 | tf_op jit(solution)/shard_map/ppermute | solution.py:25
  66.4 2.1 %collective-permute-done.9 = bf16[64,512]{1,0:T(8,128)(2,1)S(1)} collective-permute-done((bf16[64,512]{1,0:T(8,128)(2,1)S(1)}, bf16[64,512]{1,0:T(8,128)(2,1)S(1)}, u32[]{:S(2)}, u32[]{:S(2)}) %collective-permute-start.9) | collective-permute-done | bytes 65568 | tf_op jit(solution)/shard_map/ppermute | solution.py:25
  68.5 2.0 %collective-permute-done.7 = bf16[64,512]{1,0:T(8,128)(2,1)S(1)} collective-permute-done((bf16[64,512]{1,0:T(8,128)(2,1)S(1)}, bf16[64,512]{1,0:T(8,128)(2,1)S(1)}, u32[]{:S(2)}, u32[]{:S(2)}) %collective-permute-start.7) | collective-permute-done | bytes 65568 | tf_op jit(solution)/shard_map/ppermute | solution.py:25
  70.5 11.6 %all-gather = bf16[12,64,512]{2,1,0:T(8,128)(2,1)S(1)} all-gather(bf16[3,64,512]{2,1,0:T(8,128)(2,1)S(1)} %pad_maximum_fusion.1), channel_id=2, replica_groups=mesh['y'=8,'x'=4,'zh'=4,'zl'=2,'core'=2] {'x'}, dimensions={0}, use_global_device_ids=true | all-gather | bytes 983040 | tf_op jit(solution)/shard_map/all_gather | solution.py:146
  82.1 0.9 shard_map.65.o0_ref
  83.0 5.8 %collective-permute-start.11 = (bf16[512,512]{1,0:T(8,128)(2,1)S(1)}, bf16[512,512]{1,0:T(8,128)(2,1)S(1)}, u32[]{:S(2)}, u32[]{:S(2)}) collective-permute-start(bf16[512,512]{1,0:T(8,128)(2,1)S(1)} %shard_map.65.o0_ref), channel_id=1, source_target_pairs={{0,2},{2,0},{1,3},{3,1},{4,6},{6,4},{5,7},{7,5},{8,10},{10,8},{9,1... | collective-permute-start | bytes 1572872 | tf_op jit(solution)/shard_map/ppermute | solution.py:29
  88.8 6.1 %collective-permute-start.10 = (bf16[512,512]{1,0:T(8,128)(2,1)S(1)}, bf16[512,512]{1,0:T(8,128)(2,1)S(1)}, u32[]{:S(2)}, u32[]{:S(2)}) collective-permute-start(bf16[512,512]{1,0:T(8,128)(2,1)S(1)} %shard_map.65.o0_ref), channel_id=1, source_target_pairs={{0,1},{1,0},{2,3},{3,2},{4,5},{5,4},{6,7},{7,6},{8,9},{9,8},{10,11... | collective-permute-start | bytes 1572872 | tf_op jit(solution)/shard_map/ppermute | solution.py:29
  94.9 2.3 %collective-permute-done.11.o2_ref = bf16[512,512]{1,0:T(8,128)(2,1)S(1)} collective-permute-done((bf16[512,512]{1,0:T(8,128)(2,1)S(1)}, bf16[512,512]{1,0:T(8,128)(2,1)S(1)}, u32[]{:S(2)}, u32[]{:S(2)}) %collective-permute-start.11) | collective-permute-done | bytes 524320 | tf_op jit(solution)/shard_map/ppermute | solution.py:29
  97.2 6.4 %collective-permute-start.12 = (bf16[512,512]{1,0:T(8,128)(2,1)S(1)}, bf16[512,512]{1,0:T(8,128)(2,1)S(1)}, u32[]{:S(2)}, u32[]{:S(2)}) collective-permute-start(bf16[512,512]{1,0:T(8,128)(2,1)S(1)} %collective-permute-done.11.o2_ref), channel_id=1, source_target_pairs={{0,1},{1,0},{2,3},{3,2},{4,5},{5,4},{6,7},{7,6},{8,9},{9,8},{10,11... | collective-permute-start | bytes 1572872 | tf_op jit(solution)/shard_map/ppermute | solution.py:29
  103.6 1.5 collective-permute-done.12.o3_ref
  105.1 4.7 %shard_map.66 = bf16[512,1024]{1,0:T(8,128)(2,1)S(1)} custom-call(s32[1]{0:T(128)} %bitcast.flip_ref, bf16[512,512]{1,0:T(8,128)(2,1)S(1)} %shard_map.65.o0_ref, bf16[512,512]{1,0:T(8,128)(2,1)S(1)} %collective-permute-done.10.o1_ref, bf16[512,512]{1,0:T(8,128)(2,1)S(1)} %collective-permute-done.11.o2_ref, ...), custom_call_target="tpu_custom_call" | custom-call | tf_op jit(solution)/shard_map/pallas_call | solution.py:164
  109.9 38.5 %all_to_all.9 = bf16[16,32,1024]{2,1,0:T(8,128)(2,1)S(1)} all-to-all(bf16[16,32,1024]{2,1,0:T(8,128)(2,1)S(1)} %bitcast.17), channel_id=1, replica_groups=mesh['y'=8,'x'=4,'zh'=4,'zl'=2,'core'=2] {'zh','zl','core'}, dimensions={0} | all-to-all | bytes 2097152 | tf_op jit(solution)/shard_map/all_to_all | solution.py:176
  148.4 0.8 shard_map.67
  (22 shorter events, 1.2 us)
Async XLA Ops:
  6.5 32.1 %copy-start.2 = (bf16[512,256]{1,0:T(8,128)(2,1)S(1)}, bf16[512,256]{1,0:T(8,128)(2,1)}, u32[]{:S(2)}) copy-start(bf16[512,256]{1,0:T(8,128)(2,1)} %k_ref.1) | copy-start | bytes 786436
  6.5 32.1 %copy-start = (bf16[512,512]{1,0:T(8,128)(2,1)S(1)}, bf16[512,512]{1,0:T(8,128)(2,1)}, u32[]{:S(2)}) copy-start(bf16[512,512]{1,0:T(8,128)(2,1)} %v_ref.1) | copy-start | bytes 1572868
  6.5 31.9 %copy-start.3 = (s32[512,15]{0,1:T(8,128)S(1)}, s32[512,15]{0,1:T(8,128)}, u32[]{:S(2)}) copy-start(s32[512,15]{0,1:T(8,128)} %param.10) | copy-start | bytes 92164
  6.5 32.0 %copy-start.4 = (f32[16,1]{0,1:T(1,128)S(1)}, f32[16,1]{0,1:T(1,128)}, u32[]{:S(2)}) copy-start(f32[16,1]{0,1:T(1,128)} %param.9) | copy-start | bytes 196
  6.5 32.1 %copy-start.1 = (bf16[512,256]{1,0:T(8,128)(2,1)S(1)}, bf16[512,256]{1,0:T(8,128)(2,1)}, u32[]{:S(2)}) copy-start(bf16[512,256]{1,0:T(8,128)(2,1)} %q_ref.3) | copy-start | bytes 786436
  6.5 98.6 %all-gather.4.cloned.1.call-start = ((), (), s32[]{:S(2)}) async-start(), calls=%async_computation.1 | async-start | bytes 4718592 | tf_op jit(solution)/shard_map/all_gather | solution.py:125
  8.1 25.3 %collective-permute-start = (bf16[256,512]{1,0:T(8,128)(2,1)S(1)}, bf16[256,512]{1,0:T(8,128)(2,1)S(1)}, u32[]{:S(2)}, u32[]{:S(2)}) collective-permute-start(bf16[256,512]{1,0:T(8,128)(2,1)S(1)} %get-tuple-element.25), channel_id=1, source_target_pairs={{0,16},{16,0},{32,48},{48,32},{1,17},{17,1},{33,49},{49,33},{2,18}... | collective-permute-start | bytes 786440 | tf_op jit(solution)/shard_map/ppermute | solution.py:25
  12.1 14.5 %collective-permute-start.2 = (bf16[512,128]{1,0:T(8,128)(2,1)}, bf16[512,128]{1,0:T(8,128)(2,1)S(1)}, u32[]{:S(2)}, u32[]{:S(2)}) collective-permute-start(bf16[512,128]{1,0:T(8,128)(2,1)} %param.11), channel_id=1, source_target_pairs={{0,0},{1,16},{2,32},{3,48},{16,1},{17,17},{18,33},{19,49},{32,2},{... | collective-permute-start | bytes 393224 | tf_op jit(solution)/shard_map/ppermute | solution.py:119
  20.5 6.9 %collective-permute-start.3 = (bf16[512,128]{1,0:T(8,128)(2,1)}, bf16[512,128]{1,0:T(8,128)(2,1)S(1)}, u32[]{:S(2)}, u32[]{:S(2)}) collective-permute-start(bf16[512,128]{1,0:T(8,128)(2,1)} %param.11), channel_id=1, source_target_pairs={{0,16},{1,0},{2,48},{3,32},{16,17},{17,1},{18,49},{19,33},{32,18},... | collective-permute-start | bytes 393224 | tf_op jit(solution)/shard_map/ppermute | solution.py:119
  22.4 8.9 %collective-permute-start.4 = (bf16[512,128]{1,0:T(8,128)(2,1)}, bf16[512,128]{1,0:T(8,128)(2,1)S(1)}, u32[]{:S(2)}, u32[]{:S(2)}) collective-permute-start(bf16[512,128]{1,0:T(8,128)(2,1)} %param.11), channel_id=1, source_target_pairs={{0,32},{1,48},{2,0},{3,16},{16,33},{17,49},{18,1},{19,17},{32,34},... | collective-permute-start | bytes 393224 | tf_op jit(solution)/shard_map/ppermute | solution.py:119
  24.3 9.1 %collective-permute-start.5 = (bf16[512,128]{1,0:T(8,128)(2,1)}, bf16[512,128]{1,0:T(8,128)(2,1)S(1)}, u32[]{:S(2)}, u32[]{:S(2)}) collective-permute-start(bf16[512,128]{1,0:T(8,128)(2,1)} %param.11), channel_id=1, source_target_pairs={{0,48},{1,32},{2,16},{3,0},{16,49},{17,33},{18,17},{19,1},{32,50},... | collective-permute-start | bytes 393224 | tf_op jit(solution)/shard_map/ppermute | solution.py:119
  35.2 11.5 %collective-permute-start.1 = (bf16[256,512]{1,0:T(8,128)(2,1)S(1)}, bf16[256,512]{1,0:T(8,128)(2,1)S(1)}, u32[]{:S(2)}, u32[]{:S(2)}) collective-permute-start(bf16[256,512]{1,0:T(8,128)(2,1)S(1)} %get-tuple-element.23), channel_id=1, source_target_pairs={{0,32},{16,48},{32,0},{48,16},{1,33},{17,49},{33,1},{49,17},{2,34}... | collective-permute-start | bytes 786440 | tf_op jit(solution)/shard_map/ppermute | solution.py:25
  47.6 6.3 %collective-permute-start.6 = (bf16[64,512]{1,0:T(8,128)(2,1)S(1)}, bf16[64,512]{1,0:T(8,128)(2,1)S(1)}, u32[]{:S(2)}, u32[]{:S(2)}) collective-permute-start(bf16[64,512]{1,0:T(8,128)(2,1)S(1)} %fusion), channel_id=1, source_target_pairs={{0,64},{64,0},{128,192},{192,128},{256,320},{320,256},{384,448},{4... | collective-permute-start | bytes 196616 | tf_op jit(solution)/shard_map/ppermute | solution.py:25
  54.9 11.5 %collective-permute-start.8 = (bf16[64,512]{1,0:T(8,128)(2,1)S(1)}, bf16[64,512]{1,0:T(8,128)(2,1)S(1)}, u32[]{:S(2)}, u32[]{:S(2)}) collective-permute-start(bf16[64,512]{1,0:T(8,128)(2,1)S(1)} %add_convert_fusion.1), channel_id=1, source_target_pairs={{0,256},{64,320},{128,384},{192,448},{256,0},{320,64},{384,128},{4... | collective-permute-start | bytes 196616 | tf_op jit(solution)/shard_map/ppermute | solution.py:25
  59.2 9.2 %collective-permute-start.9 = (bf16[64,512]{1,0:T(8,128)(2,1)S(1)}, bf16[64,512]{1,0:T(8,128)(2,1)S(1)}, u32[]{:S(2)}, u32[]{:S(2)}) collective-permute-start(bf16[64,512]{1,0:T(8,128)(2,1)S(1)} %add_convert_fusion.1), channel_id=1, source_target_pairs={{0,384},{64,448},{128,256},{192,320},{256,128},{320,192},{384,0},{... | collective-permute-start | bytes 196616 | tf_op jit(solution)/shard_map/ppermute | solution.py:25
  61.2 9.2 %collective-permute-start.7 = (bf16[64,512]{1,0:T(8,128)(2,1)S(1)}, bf16[64,512]{1,0:T(8,128)(2,1)S(1)}, u32[]{:S(2)}, u32[]{:S(2)}) collective-permute-start(bf16[64,512]{1,0:T(8,128)(2,1)S(1)} %add_convert_fusion.1), channel_id=1, source_target_pairs={{0,128},{64,192},{128,0},{192,64},{256,384},{320,448},{384,256},{4... | collective-permute-start | bytes 196616 | tf_op jit(solution)/shard_map/ppermute | solution.py:25
  83.0 14.2 %collective-permute-start.11 = (bf16[512,512]{1,0:T(8,128)(2,1)S(1)}, bf16[512,512]{1,0:T(8,128)(2,1)S(1)}, u32[]{:S(2)}, u32[]{:S(2)}) collective-permute-start(bf16[512,512]{1,0:T(8,128)(2,1)S(1)} %shard_map.65.o0_ref), channel_id=1, source_target_pairs={{0,2},{2,0},{1,3},{3,1},{4,6},{6,4},{5,7},{7,5},{8,10},{10,8},{9,1... | collective-permute-start | bytes 1572872 | tf_op jit(solution)/shard_map/ppermute | solution.py:29
  88.8 14.8 %collective-permute-start.10 = (bf16[512,512]{1,0:T(8,128)(2,1)S(1)}, bf16[512,512]{1,0:T(8,128)(2,1)S(1)}, u32[]{:S(2)}, u32[]{:S(2)}) collective-permute-start(bf16[512,512]{1,0:T(8,128)(2,1)S(1)} %shard_map.65.o0_ref), channel_id=1, source_target_pairs={{0,1},{1,0},{2,3},{3,2},{4,5},{5,4},{6,7},{7,6},{8,9},{9,8},{10,11... | collective-permute-start | bytes 1572872 | tf_op jit(solution)/shard_map/ppermute | solution.py:29
  97.2 7.9 %collective-permute-start.12 = (bf16[512,512]{1,0:T(8,128)(2,1)S(1)}, bf16[512,512]{1,0:T(8,128)(2,1)S(1)}, u32[]{:S(2)}, u32[]{:S(2)}) collective-permute-start(bf16[512,512]{1,0:T(8,128)(2,1)S(1)} %collective-permute-done.11.o2_ref), channel_id=1, source_target_pairs={{0,1},{1,0},{2,3},{3,2},{4,5},{5,4},{6,7},{7,6},{8,9},{9,8},{10,11... | collective-permute-start | bytes 1572872 | tf_op jit(solution)/shard_map/ppermute | solution.py:29
Sparse Core Ops, SparseCore 0:
  34.4 64.8 all-gather.3

commit v5 on v4

--- a/solution.py
+++ b/solution.py
@@ -117,10 +117,11 @@
     for k in range(nu):
         pairs = [(i * nu + j, (j ^ k) * nu + i) for i in range(nx) for j in range(nu)]
         got.append(lax.ppermute(out_weight, ("x",) + QUAD, pairs))
+    near, got[0], got[1] = lax.optimization_barrier((near, got[0], got[1]))
     two = state + near.astype(F32)
     pair = crossed(two.astype(BF16), "x", 2)
 
-    *got, near = lax.optimization_barrier((*got, near))
+    *got, pair = lax.optimization_barrier((*got, pair))
     weight = jnp.stack(got)
     gathered = lax.all_gather(weight, "y", axis=0)
 
@@ -135,11 +136,11 @@
         compiler_params=PARAMS,
     )(coef_table, level_index, queries, keys, values)
 
-    pair, local = lax.optimization_barrier((pair, local))
     piece = key_size // nx
     four = two + pair.astype(F32)
     quarter = lax.dynamic_slice_in_dim(four, x * piece, piece)
     beside = crossed(quarter.astype(BF16), "y", 1)
+    beside, local = lax.optimization_barrier((beside, local))
     both = (quarter + beside.astype(F32)).astype(BF16)
     third, fourth, fifth = crossed(both, "y", 2), crossed(both, "y", 4), crossed(both, "y", 6)
     far = [beside, third, (fourth.astype(F32) + fifth.astype(F32)).astype(BF16)]

time: 157 us -> 158 us (level)
  blocking collectives: 50.1 us -> 55.2 us
  waiting for transfers between devices: 25.4 us -> 20.7 us
  starting transfers between devices: 53.3 us -> 56.3 us
  other arithmetic: 3.64 us -> 1.96 us
    ppermute x6, waiting for transfers between devices: 14.8 us -> 4.03 us  [crossed(): lax.ppermute(value, axis, [(i, i ^ by) for i in range(lax.axis_size(axis))])]
    ppermute x4, starting transfers between devices: 14.5 us -> 18.8 us  [on_device(): got.append(lax.ppermute(out_weight, ('x',) + QUAD, pairs))]
    all_gather x1, waiting for transfers between devices: 0.01 us -> 4.08 us  [on_device(): gathered = lax.all_gather(weight, 'y', axis=0)]
    all_gather x1, blocking collectives: 11.6 us -> 15.7 us  [on_device(): far = lax.all_gather(jnp.stack(far), 'x', axis=0)]
    ppermute x4, waiting for transfers between devices: 6.79 us -> 9.41 us  [on_device(): got.append(lax.ppermute(out_weight, ('x',) + QUAD, pairs))]
  transfers between devices with their start and end apart: 14 -> 14, of which waited for: 10 -> 10; matrix products, arithmetic and copies ran while one was open for 2% -> 1% of each run, Pallas kernels for 2% -> 2%
where the time goes in v5:
time: 158 us
  starting transfers between devices  56.3 us (36%)
  blocking collectives  55.2 us (35%)
  waiting for transfers between devices  20.7 us (13%)
  between operations  13.7 us (9%)
  Pallas kernels  8.25 us (5%)
  other arithmetic  1.96 us (1%)
    all_to_all x1, blocking collectives, on_device(): back = lax.all_to_all(part, TP, 0, 0, tiled=True)  39.5 us
    ppermute x6, starting transfers between devices, crossed(): lax.ppermute(value, axis, [(i, i ^ by) for i in range(lax.axis_size(axis))])  19.2 us
    ppermute x4, starting transfers between devices, on_device(): got.append(lax.ppermute(out_weight, ('x',) + QUAD, pairs))  18.8 us
    ppermute x3, starting transfers between devices, flipped(): return lax.ppermute(value, axis, [(0, 1), (1, 0)])  18.3 us
    all_gather x1, blocking collectives, on_device(): far = lax.all_gather(jnp.stack(far), 'x', axis=0)  15.7 us
    ppermute x4, waiting for transfers between devices, on_device(): got.append(lax.ppermute(out_weight, ('x',) + QUAD, pairs))  9.41 us
    pallas_call x1, Pallas kernels, on_device(): pl.pallas_call(project_kernel, grid=(ny // 2,), out_shape=jax.ShapeDtypeS...  4.74 us
    all_gather x1, waiting for transfers between devices, on_device(): gathered = lax.all_gather(weight, 'y', axis=0)  4.08 us
  transfers between devices with their start and end apart: 14, of which 10 were waited for; matrix products, arithmetic and copies ran while one was open for 1% of the time, Pallas kernels for 2%

profile of v5, /device:TPU:1, one launch (start us, length us, event | category | flops | bytes accessed | tf_op | source)
XLA Modules:
  0.0 157.8 jit_solution(8975426040684243979)
XLA Ops:
  6.6 1.5 fusion.3
  8.1 3.9 %collective-permute-start = (bf16[256,512]{1,0:T(8,128)(2,1)S(1)}, bf16[256,512]{1,0:T(8,128)(2,1)S(1)}, u32[]{:S(2)}, u32[]{:S(2)}) collective-permute-start(bf16[256,512]{1,0:T(8,128)(2,1)S(1)} %get-tuple-element.31), channel_id=1, source_target_pairs={{0,16},{16,0},{32,48},{48,32},{1,17},{17,1},{33,49},{49,33},{2,18}... | collective-permute-start | bytes 786440 | tf_op jit(solution)/shard_map/ppermute | solution.py:25
  12.1 8.4 %collective-permute-start.1 = (bf16[512,128]{1,0:T(8,128)(2,1)}, bf16[512,128]{1,0:T(8,128)(2,1)S(1)}, u32[]{:S(2)}, u32[]{:S(2)}) collective-permute-start(bf16[512,128]{1,0:T(8,128)(2,1)} %param.11), channel_id=1, source_target_pairs={{0,0},{1,16},{2,32},{3,48},{16,1},{17,17},{18,33},{19,49},{32,2},{... | collective-permute-start | bytes 393224 | tf_op jit(solution)/shard_map/ppermute | solution.py:119
  20.5 1.9 %collective-permute-start.2 = (bf16[512,128]{1,0:T(8,128)(2,1)}, bf16[512,128]{1,0:T(8,128)(2,1)S(1)}, u32[]{:S(2)}, u32[]{:S(2)}) collective-permute-start(bf16[512,128]{1,0:T(8,128)(2,1)} %param.11), channel_id=1, source_target_pairs={{0,16},{1,0},{2,48},{3,32},{16,17},{17,1},{18,49},{19,33},{32,18},... | collective-permute-start | bytes 393224 | tf_op jit(solution)/shard_map/ppermute | solution.py:119
  22.4 4.1 %collective-permute-done.1 = bf16[512,128]{1,0:T(8,128)(2,1)S(1)} collective-permute-done((bf16[512,128]{1,0:T(8,128)(2,1)}, bf16[512,128]{1,0:T(8,128)(2,1)S(1)}, u32[]{:S(2)}, u32[]{:S(2)}) %collective-permute-start.1) | collective-permute-done | bytes 131104 | tf_op jit(solution)/shard_map/ppermute | solution.py:119
  26.5 0.9 collective-permute-done.2
  27.5 1.9 %collective-permute-start.5 = (bf16[256,512]{1,0:T(8,128)(2,1)S(1)}, bf16[256,512]{1,0:T(8,128)(2,1)S(1)}, u32[]{:S(2)}, u32[]{:S(2)}) collective-permute-start(bf16[256,512]{1,0:T(8,128)(2,1)S(1)} %get-tuple-element.29), channel_id=1, source_target_pairs={{0,32},{16,48},{32,0},{48,16},{1,33},{17,49},{33,1},{49,17},{2,34}... | collective-permute-start | bytes 786440 | tf_op jit(solution)/shard_map/ppermute | solution.py:25
  29.4 6.0 %collective-permute-start.3 = (bf16[512,128]{1,0:T(8,128)(2,1)}, bf16[512,128]{1,0:T(8,128)(2,1)S(1)}, u32[]{:S(2)}, u32[]{:S(2)}) collective-permute-start(bf16[512,128]{1,0:T(8,128)(2,1)} %param.11), channel_id=1, source_target_pairs={{0,32},{1,48},{2,0},{3,16},{16,33},{17,49},{18,1},{19,17},{32,34},... | collective-permute-start | bytes 393224 | tf_op jit(solution)/shard_map/ppermute | solution.py:119
  35.4 2.5 %collective-permute-start.4 = (bf16[512,128]{1,0:T(8,128)(2,1)}, bf16[512,128]{1,0:T(8,128)(2,1)S(1)}, u32[]{:S(2)}, u32[]{:S(2)}) collective-permute-start(bf16[512,128]{1,0:T(8,128)(2,1)} %param.11), channel_id=1, source_target_pairs={{0,48},{1,32},{2,16},{3,0},{16,49},{17,33},{18,17},{19,1},{32,50},... | collective-permute-start | bytes 393224 | tf_op jit(solution)/shard_map/ppermute | solution.py:119
  37.9 3.4 %collective-permute-done.3 = bf16[512,128]{1,0:T(8,128)(2,1)S(1)} collective-permute-done((bf16[512,128]{1,0:T(8,128)(2,1)}, bf16[512,128]{1,0:T(8,128)(2,1)S(1)}, u32[]{:S(2)}, u32[]{:S(2)}) %collective-permute-start.3) | collective-permute-done | bytes 131104 | tf_op jit(solution)/shard_map/ppermute | solution.py:119
  41.3 1.1 collective-permute-done.4
  42.3 0.9 pad_maximum_fusion
  43.3 2.0 %collective-permute-start.6 = (bf16[64,512]{1,0:T(8,128)(2,1)S(1)}, bf16[64,512]{1,0:T(8,128)(2,1)S(1)}, u32[]{:S(2)}, u32[]{:S(2)}) collective-permute-start(bf16[64,512]{1,0:T(8,128)(2,1)S(1)} %fusion), channel_id=1, source_target_pairs={{0,64},{64,0},{128,192},{192,128},{256,320},{320,256},{384,448},{4... | collective-permute-start | bytes 196616 | tf_op jit(solution)/shard_map/ppermute | solution.py:25
  45.5 1.8 %shard_map.64 = (f32[512,512]{1,0:T(8,128)S(1)}, f32[512,15]{1,0:T(8,128)S(1)}) custom-call(f32[16,1]{1,0:T(8,128)S(1)} %copy.9.coef_ref, s32[512,15]{1,0:T(8,128)S(1)} %copy.10.index_ref, bf16[512,256]{1,0:T(8,128)(2,1)S(1)} %copy-done.1, bf16[512,256]{1,0:T(8,128)(2,1)S(1)} %copy-done.2, bf16[512,512]{1,0:T(8,128)(2,1)S(1)} %copy-done), custom_call_target="tpu_custom_call" | custom-call | tf_op jit(solution)/shard_map/pallas_call | solution.py:128
  47.3 1.0 collective-permute-done.6
  48.3 0.9 add_convert_fusion.1
  49.2 6.2 %collective-permute-start.8 = (bf16[64,512]{1,0:T(8,128)(2,1)S(1)}, bf16[64,512]{1,0:T(8,128)(2,1)S(1)}, u32[]{:S(2)}, u32[]{:S(2)}) collective-permute-start(bf16[64,512]{1,0:T(8,128)(2,1)S(1)} %add_convert_fusion.1), channel_id=1, source_target_pairs={{0,256},{64,320},{128,384},{192,448},{256,0},{320,64},{384,128},{4... | collective-permute-start | bytes 196616 | tf_op jit(solution)/shard_map/ppermute | solution.py:25
  55.5 2.2 %collective-permute-start.9 = (bf16[64,512]{1,0:T(8,128)(2,1)S(1)}, bf16[64,512]{1,0:T(8,128)(2,1)S(1)}, u32[]{:S(2)}, u32[]{:S(2)}) collective-permute-start(bf16[64,512]{1,0:T(8,128)(2,1)S(1)} %add_convert_fusion.1), channel_id=1, source_target_pairs={{0,384},{64,448},{128,256},{192,320},{256,128},{320,192},{384,0},{... | collective-permute-start | bytes 196616 | tf_op jit(solution)/shard_map/ppermute | solution.py:25
  57.7 2.9 %collective-permute-start.7 = (bf16[64,512]{1,0:T(8,128)(2,1)S(1)}, bf16[64,512]{1,0:T(8,128)(2,1)S(1)}, u32[]{:S(2)}, u32[]{:S(2)}) collective-permute-start(bf16[64,512]{1,0:T(8,128)(2,1)S(1)} %add_convert_fusion.1), channel_id=1, source_target_pairs={{0,128},{64,192},{128,0},{192,64},{256,384},{320,448},{384,256},{4... | collective-permute-start | bytes 196616 | tf_op jit(solution)/shard_map/ppermute | solution.py:25
  60.6 1.9 %collective-permute-done.9 = bf16[64,512]{1,0:T(8,128)(2,1)S(1)} collective-permute-done((bf16[64,512]{1,0:T(8,128)(2,1)S(1)}, bf16[64,512]{1,0:T(8,128)(2,1)S(1)}, u32[]{:S(2)}, u32[]{:S(2)}) %collective-permute-start.9) | collective-permute-done | bytes 65568 | tf_op jit(solution)/shard_map/ppermute | solution.py:25
  62.6 1.1 collective-permute-done.7
  63.7 15.7 %all-gather = bf16[12,64,512]{2,1,0:T(8,128)(2,1)S(1)} all-gather(bf16[3,64,512]{2,1,0:T(8,128)(2,1)S(1)} %pad_maximum_fusion.1), channel_id=2, replica_groups=mesh['y'=8,'x'=4,'zh'=4,'zl'=2,'core'=2] {'x'}, dimensions={0}, use_global_device_ids=true | all-gather | bytes 983040 | tf_op jit(solution)/shard_map/all_gather | solution.py:147
  79.4 0.9 shard_map.65.o0_ref
  80.3 5.2 %collective-permute-start.11 = (bf16[512,512]{1,0:T(8,128)(2,1)S(1)}, bf16[512,512]{1,0:T(8,128)(2,1)S(1)}, u32[]{:S(2)}, u32[]{:S(2)}) collective-permute-start(bf16[512,512]{1,0:T(8,128)(2,1)S(1)} %shard_map.65.o0_ref), channel_id=1, source_target_pairs={{0,2},{2,0},{1,3},{3,1},{4,6},{6,4},{5,7},{7,5},{8,10},{10,8},{9,1... | collective-permute-start | bytes 1572872 | tf_op jit(solution)/shard_map/ppermute | solution.py:29
  85.5 6.4 %collective-permute-start.10 = (bf16[512,512]{1,0:T(8,128)(2,1)S(1)}, bf16[512,512]{1,0:T(8,128)(2,1)S(1)}, u32[]{:S(2)}, u32[]{:S(2)}) collective-permute-start(bf16[512,512]{1,0:T(8,128)(2,1)S(1)} %shard_map.65.o0_ref), channel_id=1, source_target_pairs={{0,1},{1,0},{2,3},{3,2},{4,5},{5,4},{6,7},{7,6},{8,9},{9,8},{10,11... | collective-permute-start | bytes 1572872 | tf_op jit(solution)/shard_map/ppermute | solution.py:29
  91.9 1.6 %collective-permute-done.11.o2_ref = bf16[512,512]{1,0:T(8,128)(2,1)S(1)} collective-permute-done((bf16[512,512]{1,0:T(8,128)(2,1)S(1)}, bf16[512,512]{1,0:T(8,128)(2,1)S(1)}, u32[]{:S(2)}, u32[]{:S(2)}) %collective-permute-start.11) | collective-permute-done | bytes 524320 | tf_op jit(solution)/shard_map/ppermute | solution.py:29
  93.6 6.7 %collective-permute-start.12 = (bf16[512,512]{1,0:T(8,128)(2,1)S(1)}, bf16[512,512]{1,0:T(8,128)(2,1)S(1)}, u32[]{:S(2)}, u32[]{:S(2)}) collective-permute-start(bf16[512,512]{1,0:T(8,128)(2,1)S(1)} %collective-permute-done.11.o2_ref), channel_id=1, source_target_pairs={{0,1},{1,0},{2,3},{3,2},{4,5},{5,4},{6,7},{7,6},{8,9},{9,8},{10,11... | collective-permute-start | bytes 1572872 | tf_op jit(solution)/shard_map/ppermute | solution.py:29
  100.3 1.5 collective-permute-done.12.o3_ref
  101.8 4.1 %all-gather.4.cloned.1.call-done = bf16[32,512,128]{2,1,0:T(8,128)(2,1)} async-done(((bf16[4,512,128]{2,1,0:T(8,128)(2,1)}), bf16[32,512,128]{2,1,0:T(8,128)(2,1)}) %all-gather.4.cloned.1.call-update) | async-done | bytes 4194320 | tf_op jit(solution)/shard_map/all_gather | solution.py:126
  105.9 4.7 %shard_map.66 = bf16[512,1024]{1,0:T(8,128)(2,1)S(1)} custom-call(s32[1]{0:T(128)} %bitcast.flip_ref, bf16[512,512]{1,0:T(8,128)(2,1)S(1)} %shard_map.65.o0_ref, bf16[512,512]{1,0:T(8,128)(2,1)S(1)} %collective-permute-done.10.o1_ref, bf16[512,512]{1,0:T(8,128)(2,1)S(1)} %collective-permute-done.11.o2_ref, ...), custom_call_target="tpu_custom_call" | custom-call | tf_op jit(solution)/shard_map/pallas_call | solution.py:165
  110.6 39.5 %all_to_all.9 = bf16[16,32,1024]{2,1,0:T(8,128)(2,1)S(1)} all-to-all(bf16[16,32,1024]{2,1,0:T(8,128)(2,1)S(1)} %bitcast.17), channel_id=1, replica_groups=mesh['y'=8,'x'=4,'zh'=4,'zl'=2,'core'=2] {'zh','zl','core'}, dimensions={0} | all-to-all | bytes 2097152 | tf_op jit(solution)/shard_map/all_to_all | solution.py:177
  150.1 0.8 shard_map.67
  (24 shorter events, 0.5 us)
Async XLA Ops:
  6.5 39.0 %copy-start.2 = (bf16[512,256]{1,0:T(8,128)(2,1)S(1)}, bf16[512,256]{1,0:T(8,128)(2,1)}, u32[]{:S(2)}) copy-start(bf16[512,256]{1,0:T(8,128)(2,1)} %k_ref.1) | copy-start | bytes 786436
  6.5 39.0 %copy-start = (bf16[512,512]{1,0:T(8,128)(2,1)S(1)}, bf16[512,512]{1,0:T(8,128)(2,1)}, u32[]{:S(2)}) copy-start(bf16[512,512]{1,0:T(8,128)(2,1)} %v_ref.1) | copy-start | bytes 1572868
  6.5 38.7 %copy-start.4 = (s32[512,15]{0,1:T(8,128)S(1)}, s32[512,15]{0,1:T(8,128)}, u32[]{:S(2)}) copy-start(s32[512,15]{0,1:T(8,128)} %param.10) | copy-start | bytes 92164
  6.5 38.9 %copy-start.5 = (f32[16,1]{0,1:T(1,128)S(1)}, f32[16,1]{0,1:T(1,128)}, u32[]{:S(2)}) copy-start(f32[16,1]{0,1:T(1,128)} %param.9) | copy-start | bytes 196
  6.5 39.0 %copy-start.1 = (bf16[512,256]{1,0:T(8,128)(2,1)S(1)}, bf16[512,256]{1,0:T(8,128)(2,1)}, u32[]{:S(2)}) copy-start(bf16[512,256]{1,0:T(8,128)(2,1)} %q_ref.3) | copy-start | bytes 786436
  6.5 99.3 %all-gather.4.cloned.1.call-start = ((), (), s32[]{:S(2)}) async-start(), calls=%async_computation.1 | async-start | bytes 4718592 | tf_op jit(solution)/shard_map/all_gather | solution.py:126
  8.1 19.2 %collective-permute-start = (bf16[256,512]{1,0:T(8,128)(2,1)S(1)}, bf16[256,512]{1,0:T(8,128)(2,1)S(1)}, u32[]{:S(2)}, u32[]{:S(2)}) collective-permute-start(bf16[256,512]{1,0:T(8,128)(2,1)S(1)} %get-tuple-element.31), channel_id=1, source_target_pairs={{0,16},{16,0},{32,48},{48,32},{1,17},{17,1},{33,49},{49,33},{2,18}... | collective-permute-start | bytes 786440 | tf_op jit(solution)/shard_map/ppermute | solution.py:25
  12.1 14.4 %collective-permute-start.1 = (bf16[512,128]{1,0:T(8,128)(2,1)}, bf16[512,128]{1,0:T(8,128)(2,1)S(1)}, u32[]{:S(2)}, u32[]{:S(2)}) collective-permute-start(bf16[512,128]{1,0:T(8,128)(2,1)} %param.11), channel_id=1, source_target_pairs={{0,0},{1,16},{2,32},{3,48},{16,1},{17,17},{18,33},{19,49},{32,2},{... | collective-permute-start | bytes 393224 | tf_op jit(solution)/shard_map/ppermute | solution.py:119
  20.5 6.9 %collective-permute-start.2 = (bf16[512,128]{1,0:T(8,128)(2,1)}, bf16[512,128]{1,0:T(8,128)(2,1)S(1)}, u32[]{:S(2)}, u32[]{:S(2)}) collective-permute-start(bf16[512,128]{1,0:T(8,128)(2,1)} %param.11), channel_id=1, source_target_pairs={{0,16},{1,0},{2,48},{3,32},{16,17},{17,1},{18,49},{19,33},{32,18},... | collective-permute-start | bytes 393224 | tf_op jit(solution)/shard_map/ppermute | solution.py:119
  27.5 17.9 %copy-start.3 = (f32[256,512]{1,0:T(8,128)}, f32[256,512]{1,0:T(8,128)S(1)}, u32[]{:S(2)}) copy-start(f32[256,512]{1,0:T(8,128)S(1)} %get-tuple-element.30) | copy-start | bytes 1572868
  27.5 14.9 %collective-permute-start.5 = (bf16[256,512]{1,0:T(8,128)(2,1)S(1)}, bf16[256,512]{1,0:T(8,128)(2,1)S(1)}, u32[]{:S(2)}, u32[]{:S(2)}) collective-permute-start(bf16[256,512]{1,0:T(8,128)(2,1)S(1)} %get-tuple-element.29), channel_id=1, source_target_pairs={{0,32},{16,48},{32,0},{48,16},{1,33},{17,49},{33,1},{49,17},{2,34}... | collective-permute-start | bytes 786440 | tf_op jit(solution)/shard_map/ppermute | solution.py:25
  29.4 11.9 %collective-permute-start.3 = (bf16[512,128]{1,0:T(8,128)(2,1)}, bf16[512,128]{1,0:T(8,128)(2,1)S(1)}, u32[]{:S(2)}, u32[]{:S(2)}) collective-permute-start(bf16[512,128]{1,0:T(8,128)(2,1)} %param.11), channel_id=1, source_target_pairs={{0,32},{1,48},{2,0},{3,16},{16,33},{17,49},{18,1},{19,17},{32,34},... | collective-permute-start | bytes 393224 | tf_op jit(solution)/shard_map/ppermute | solution.py:119
  35.4 6.9 %collective-permute-start.4 = (bf16[512,128]{1,0:T(8,128)(2,1)}, bf16[512,128]{1,0:T(8,128)(2,1)S(1)}, u32[]{:S(2)}, u32[]{:S(2)}) collective-permute-start(bf16[512,128]{1,0:T(8,128)(2,1)} %param.11), channel_id=1, source_target_pairs={{0,48},{1,32},{2,16},{3,0},{16,49},{17,33},{18,17},{19,1},{32,50},... | collective-permute-start | bytes 393224 | tf_op jit(solution)/shard_map/ppermute | solution.py:119
  43.3 5.0 %collective-permute-start.6 = (bf16[64,512]{1,0:T(8,128)(2,1)S(1)}, bf16[64,512]{1,0:T(8,128)(2,1)S(1)}, u32[]{:S(2)}, u32[]{:S(2)}) collective-permute-start(bf16[64,512]{1,0:T(8,128)(2,1)S(1)} %fusion), channel_id=1, source_target_pairs={{0,64},{64,0},{128,192},{192,128},{256,320},{320,256},{384,448},{4... | collective-permute-start | bytes 196616 | tf_op jit(solution)/shard_map/ppermute | solution.py:25
  49.2 11.4 %collective-permute-start.8 = (bf16[64,512]{1,0:T(8,128)(2,1)S(1)}, bf16[64,512]{1,0:T(8,128)(2,1)S(1)}, u32[]{:S(2)}, u32[]{:S(2)}) collective-permute-start(bf16[64,512]{1,0:T(8,128)(2,1)S(1)} %add_convert_fusion.1), channel_id=1, source_target_pairs={{0,256},{64,320},{128,384},{192,448},{256,0},{320,64},{384,128},{4... | collective-permute-start | bytes 196616 | tf_op jit(solution)/shard_map/ppermute | solution.py:25
  55.5 7.1 %collective-permute-start.9 = (bf16[64,512]{1,0:T(8,128)(2,1)S(1)}, bf16[64,512]{1,0:T(8,128)(2,1)S(1)}, u32[]{:S(2)}, u32[]{:S(2)}) collective-permute-start(bf16[64,512]{1,0:T(8,128)(2,1)S(1)} %add_convert_fusion.1), channel_id=1, source_target_pairs={{0,384},{64,448},{128,256},{192,320},{256,128},{320,192},{384,0},{... | collective-permute-start | bytes 196616 | tf_op jit(solution)/shard_map/ppermute | solution.py:25
  57.7 6.0 %collective-permute-start.7 = (bf16[64,512]{1,0:T(8,128)(2,1)S(1)}, bf16[64,512]{1,0:T(8,128)(2,1)S(1)}, u32[]{:S(2)}, u32[]{:S(2)}) collective-permute-start(bf16[64,512]{1,0:T(8,128)(2,1)S(1)} %add_convert_fusion.1), channel_id=1, source_target_pairs={{0,128},{64,192},{128,0},{192,64},{256,384},{320,448},{384,256},{4... | collective-permute-start | bytes 196616 | tf_op jit(solution)/shard_map/ppermute | solution.py:25
  80.3 13.3 %collective-permute-start.11 = (bf16[512,512]{1,0:T(8,128)(2,1)S(1)}, bf16[512,512]{1,0:T(8,128)(2,1)S(1)}, u32[]{:S(2)}, u32[]{:S(2)}) collective-permute-start(bf16[512,512]{1,0:T(8,128)(2,1)S(1)} %shard_map.65.o0_ref), channel_id=1, source_target_pairs={{0,2},{2,0},{1,3},{3,1},{4,6},{6,4},{5,7},{7,5},{8,10},{10,8},{9,1... | collective-permute-start | bytes 1572872 | tf_op jit(solution)/shard_map/ppermute | solution.py:29
  85.5 14.8 %collective-permute-start.10 = (bf16[512,512]{1,0:T(8,128)(2,1)S(1)}, bf16[512,512]{1,0:T(8,128)(2,1)S(1)}, u32[]{:S(2)}, u32[]{:S(2)}) collective-permute-start(bf16[512,512]{1,0:T(8,128)(2,1)S(1)} %shard_map.65.o0_ref), channel_id=1, source_target_pairs={{0,1},{1,0},{2,3},{3,2},{4,5},{5,4},{6,7},{7,6},{8,9},{9,8},{10,11... | collective-permute-start | bytes 1572872 | tf_op jit(solution)/shard_map/ppermute | solution.py:29
  93.6 8.2 %collective-permute-start.12 = (bf16[512,512]{1,0:T(8,128)(2,1)S(1)}, bf16[512,512]{1,0:T(8,128)(2,1)S(1)}, u32[]{:S(2)}, u32[]{:S(2)}) collective-permute-start(bf16[512,512]{1,0:T(8,128)(2,1)S(1)} %collective-permute-done.11.o2_ref), channel_id=1, source_target_pairs={{0,1},{1,0},{2,3},{3,2},{4,5},{5,4},{6,7},{7,6},{8,9},{9,8},{10,11... | collective-permute-start | bytes 1572872 | tf_op jit(solution)/shard_map/ppermute | solution.py:29
Sparse Core Ops, SparseCore 0:
  43.4 62.4 all-gather.3

commit v6 on v5

--- a/solution.py
+++ b/solution.py
@@ -74,7 +74,7 @@
         elif bit == 1:
             node = pair_ref[...]
         else:
-            node = jnp.concatenate([far_ref[i, bit - 2] for i in range(far_ref.shape[0])], axis=0)
+            node = jnp.concatenate([far_ref[i, bit - 2] for i in (0, 2, 1, 3)], axis=0)
         setbit = (bits_ref[0] >> bit & 1).astype(F32)
         factor = lam_ref[:, base + bit : base + bit + 1] * inverse_scale * setbit
         total = total + jnp.dot(q, node, preferred_element_type=F32) * factor
@@ -111,19 +111,32 @@
     nx, ny, nu = lax.axis_size("x"), lax.axis_size("y"), 4
 
     state = lax.dot_general(keys, values, (((0,), (0,)), ((), ())), preferred_element_type=F32)
-    near = crossed(state.astype(BF16), "x", 1)
+    half, piece = key_size // 2, key_size // nx
+    odd, high = x % 2, x // 2
+    given = lax.dynamic_slice_in_dim(state, (1 - odd) * half, half).astype(BF16)
+    kept = lax.dynamic_slice_in_dim(state, odd * half, half)
+    one = crossed(given, "x", 1)
 
     got = []
     for k in range(nu):
         pairs = [(i * nu + j, (j ^ k) * nu + i) for i in range(nx) for j in range(nu)]
         got.append(lax.ppermute(out_weight, ("x",) + QUAD, pairs))
-    near, got[0], got[1] = lax.optimization_barrier((near, got[0], got[1]))
-    two = state + near.astype(F32)
-    pair = crossed(two.astype(BF16), "x", 2)
-
-    *got, pair = lax.optimization_barrier((*got, pair))
+
+    *got, one = lax.optimization_barrier((*got, one))
     weight = jnp.stack(got)
     gathered = lax.all_gather(weight, "y", axis=0)
+
+    halves = kept + one.astype(F32)
+    given = lax.dynamic_slice_in_dim(halves, (1 - high) * piece, piece).astype(BF16)
+    quarter = lax.dynamic_slice_in_dim(halves, high * piece, piece)
+    part = crossed(given, "x", 2)
+    quarter = quarter + part.astype(F32)
+    beside = crossed(quarter.astype(BF16), "y", 1)
+
+    late, part = lax.optimization_barrier((kept.astype(BF16), part))
+    rest = crossed(late, "x", 1)
+    near = jnp.where(odd == 1, jnp.concatenate([rest, one]), jnp.concatenate([one, rest]))
+    pair = crossed((state + near.astype(F32)).astype(BF16), "x", 2)
 
     local, lam = pl.pallas_call(
         local_kernel,
@@ -136,10 +149,6 @@
         compiler_params=PARAMS,
     )(coef_table, level_index, queries, keys, values)
 
-    piece = key_size // nx
-    four = two + pair.astype(F32)
-    quarter = lax.dynamic_slice_in_dim(four, x * piece, piece)
-    beside = crossed(quarter.astype(BF16), "y", 1)
     beside, local = lax.optimization_barrier((beside, local))
     both = (quarter + beside.astype(F32)).astype(BF16)
     third, fourth, fifth = crossed(both, "y", 2), crossed(both, "y", 4), crossed(both, "y", 6)

time: 158 us -> 152 us (0.962)
  waiting for transfers between devices: 20.7 us -> 18 us
  blocking collectives: 55.2 us -> 53.1 us
    ppermute x6 -> x8, starting transfers between devices: 19.2 us -> 26.8 us  [crossed(): lax.ppermute(value, axis, [(i, i ^ by) for i in range(lax.axis_size(axis))])]
    ppermute x4, starting transfers between devices: 18.8 us -> 14.5 us  [on_device(): got.append(lax.ppermute(out_weight, ('x',) + QUAD, pairs))]
    ppermute x3, starting transfers between devices: 18.3 us -> 14.1 us  [flipped(): return lax.ppermute(value, axis, [(0, 1), (1, 0)])]
    all_gather x1, waiting for transfers between devices: 4.08 us -> 0.01 us  [on_device(): gathered = lax.all_gather(weight, 'y', axis=0)]
    ppermute x4, waiting for transfers between devices: 9.41 us -> 6.78 us  [on_device(): got.append(lax.ppermute(out_weight, ('x',) + QUAD, pairs))]
    ppermute x3, waiting for transfers between devices: 3.12 us -> 5.49 us  [flipped(): return lax.ppermute(value, axis, [(0, 1), (1, 0)])]
    ppermute x6 -> x8, waiting for transfers between devices: 4.03 us -> 5.69 us  [crossed(): lax.ppermute(value, axis, [(i, i ^ by) for i in range(lax.axis_size(axis))])]
  transfers between devices with their start and end apart: 14 -> 16, of which waited for: 10 -> 7; matrix products, arithmetic and copies ran while one was open for 1% -> 0% of each run, Pallas kernels for 2% -> 2%
where the time goes in v6:
time: 152 us
  starting transfers between devices  55.5 us (37%)
  blocking collectives  53.1 us (35%)
  waiting for transfers between devices  18 us (12%)
  between operations  13.8 us (9%)
  Pallas kernels  8.27 us (5%)
    all_to_all x1, blocking collectives, on_device(): back = lax.all_to_all(part, TP, 0, 0, tiled=True)  38.1 us
    ppermute x8, starting transfers between devices, crossed(): lax.ppermute(value, axis, [(i, i ^ by) for i in range(lax.axis_size(axis))])  26.8 us
    all_gather x1, blocking collectives, on_device(): far = lax.all_gather(jnp.stack(far), 'x', axis=0)  15 us
    ppermute x4, starting transfers between devices, on_device(): got.append(lax.ppermute(out_weight, ('x',) + QUAD, pairs))  14.5 us
    ppermute x3, starting transfers between devices, flipped(): return lax.ppermute(value, axis, [(0, 1), (1, 0)])  14.1 us
    ppermute x4, waiting for transfers between devices, on_device(): got.append(lax.ppermute(out_weight, ('x',) + QUAD, pairs))  6.78 us
    ppermute x8, waiting for transfers between devices, crossed(): lax.ppermute(value, axis, [(i, i ^ by) for i in range(lax.axis_size(axis))])  5.69 us
    ppermute x3, waiting for transfers between devices, flipped(): return lax.ppermute(value, axis, [(0, 1), (1, 0)])  5.49 us
  transfers between devices with their start and end apart: 16, of which 7 were waited for; matrix products, arithmetic and copies ran while one was open for 0% of the time, Pallas kernels for 2%

profile of v6, /device:TPU:1, one launch (start us, length us, event | category | flops | bytes accessed | tf_op | source)
XLA Modules:
  0.0 151.6 jit_solution(10215548104862680018)
XLA Ops:
  6.6 1.5 fusion.2
  8.2 3.9 %collective-permute-start.4 = (bf16[128,512]{1,0:T(8,128)(2,1)S(1)}, bf16[128,512]{1,0:T(8,128)(2,1)S(1)}, u32[]{:S(2)}, u32[]{:S(2)}) collective-permute-start(bf16[128,512]{1,0:T(8,128)(2,1)S(1)} %get-tuple-element.28), channel_id=1, source_target_pairs={{0,16},{16,0},{32,48},{48,32},{1,17},{17,1},{33,49},{49,33},{2,18}... | collective-permute-start | bytes 393224 | tf_op jit(solution)/shard_map/ppermute | solution.py:25
  12.1 8.4 %collective-permute-start = (bf16[512,128]{1,0:T(8,128)(2,1)}, bf16[512,128]{1,0:T(8,128)(2,1)S(1)}, u32[]{:S(2)}, u32[]{:S(2)}) collective-permute-start(bf16[512,128]{1,0:T(8,128)(2,1)} %param.11), channel_id=1, source_target_pairs={{0,0},{1,16},{2,32},{3,48},{16,1},{17,17},{18,33},{19,49},{32,2},{... | collective-permute-start | bytes 393224 | tf_op jit(solution)/shard_map/ppermute | solution.py:123
  20.5 1.9 %collective-permute-start.1 = (bf16[512,128]{1,0:T(8,128)(2,1)}, bf16[512,128]{1,0:T(8,128)(2,1)S(1)}, u32[]{:S(2)}, u32[]{:S(2)}) collective-permute-start(bf16[512,128]{1,0:T(8,128)(2,1)} %param.11), channel_id=1, source_target_pairs={{0,16},{1,0},{2,48},{3,32},{16,17},{17,1},{18,49},{19,33},{32,18},... | collective-permute-start | bytes 393224 | tf_op jit(solution)/shard_map/ppermute | solution.py:123
  22.5 1.9 %collective-permute-start.2 = (bf16[512,128]{1,0:T(8,128)(2,1)}, bf16[512,128]{1,0:T(8,128)(2,1)S(1)}, u32[]{:S(2)}, u32[]{:S(2)}) collective-permute-start(bf16[512,128]{1,0:T(8,128)(2,1)} %param.11), channel_id=1, source_target_pairs={{0,32},{1,48},{2,0},{3,16},{16,33},{17,49},{18,1},{19,17},{32,34},... | collective-permute-start | bytes 393224 | tf_op jit(solution)/shard_map/ppermute | solution.py:123
  24.4 2.3 %collective-permute-start.3 = (bf16[512,128]{1,0:T(8,128)(2,1)}, bf16[512,128]{1,0:T(8,128)(2,1)S(1)}, u32[]{:S(2)}, u32[]{:S(2)}) collective-permute-start(bf16[512,128]{1,0:T(8,128)(2,1)} %param.11), channel_id=1, source_target_pairs={{0,48},{1,32},{2,16},{3,0},{16,49},{17,33},{18,17},{19,1},{32,50},... | collective-permute-start | bytes 393224 | tf_op jit(solution)/shard_map/ppermute | solution.py:123
  26.7 4.6 %collective-permute-done.2 = bf16[512,128]{1,0:T(8,128)(2,1)S(1)} collective-permute-done((bf16[512,128]{1,0:T(8,128)(2,1)}, bf16[512,128]{1,0:T(8,128)(2,1)S(1)}, u32[]{:S(2)}, u32[]{:S(2)}) %collective-permute-start.2) | collective-permute-done | bytes 131104 | tf_op jit(solution)/shard_map/ppermute | solution.py:123
  31.4 2.1 %collective-permute-done.3 = bf16[512,128]{1,0:T(8,128)(2,1)S(1)} collective-permute-done((bf16[512,128]{1,0:T(8,128)(2,1)}, bf16[512,128]{1,0:T(8,128)(2,1)S(1)}, u32[]{:S(2)}, u32[]{:S(2)}) %collective-permute-start.3) | collective-permute-done | bytes 131104 | tf_op jit(solution)/shard_map/ppermute | solution.py:123
  33.5 0.9 pad_maximum_fusion
  34.4 3.2 %collective-permute-start.5 = (bf16[64,512]{1,0:T(8,128)(2,1)S(1)}, bf16[64,512]{1,0:T(8,128)(2,1)S(1)}, u32[]{:S(2)}, u32[]{:S(2)}) collective-permute-start(bf16[64,512]{1,0:T(8,128)(2,1)S(1)} %dynamic-slice_convert_fusion.2), channel_id=1, source_target_pairs={{0,32},{16,48},{32,0},{48,16},{1,33},{17,49},{33,1},{49,17},{2,34}... | collective-permute-start | bytes 196616 | tf_op jit(solution)/shard_map/ppermute | solution.py:25
  37.7 4.1 %collective-permute-done.5 = bf16[64,512]{1,0:T(8,128)(2,1)S(1)} collective-permute-done((bf16[64,512]{1,0:T(8,128)(2,1)S(1)}, bf16[64,512]{1,0:T(8,128)(2,1)S(1)}, u32[]{:S(2)}, u32[]{:S(2)}) %collective-permute-start.5) | collective-permute-done | bytes 65568 | tf_op jit(solution)/shard_map/ppermute | solution.py:25
  41.8 1.9 %collective-permute-start.6 = (bf16[64,512]{1,0:T(8,128)(2,1)S(1)}, bf16[64,512]{1,0:T(8,128)(2,1)S(1)}, u32[]{:S(2)}, u32[]{:S(2)}) collective-permute-start(bf16[64,512]{1,0:T(8,128)(2,1)S(1)} %fusion), channel_id=1, source_target_pairs={{0,64},{64,0},{128,192},{192,128},{256,320},{320,256},{384,448},{4... | collective-permute-start | bytes 196616 | tf_op jit(solution)/shard_map/ppermute | solution.py:25
  43.7 0.1 copy.10.index_ref
  43.9 0.1 copy.9.coef_ref
  44.0 1.8 %shard_map.64 = (f32[512,512]{1,0:T(8,128)S(1)}, f32[512,15]{1,0:T(8,128)S(1)}) custom-call(f32[16,1]{1,0:T(8,128)S(1)} %copy.9.coef_ref, s32[512,15]{1,0:T(8,128)S(1)} %copy.10.index_ref, bf16[512,256]{1,0:T(8,128)(2,1)S(1)} %copy-done.2, bf16[512,256]{1,0:T(8,128)(2,1)S(1)} %copy-done.1, bf16[512,512]{1,0:T(8,128)(2,1)S(1)} %copy-done), custom_call_target="tpu_custom_call" | custom-call | tf_op jit(solution)/shard_map/pallas_call | solution.py:141
  45.7 2.1 %collective-permute-start.7 = (bf16[128,512]{1,0:T(8,128)(2,1)S(1)}, bf16[128,512]{1,0:T(8,128)(2,1)S(1)}, u32[]{:S(2)}, u32[]{:S(2)}) collective-permute-start(bf16[128,512]{1,0:T(8,128)(2,1)S(1)} %get-tuple-element.19), channel_id=1, source_target_pairs={{0,16},{16,0},{32,48},{48,32},{1,17},{17,1},{33,49},{49,33},{2,18}... | collective-permute-start | bytes 393224 | tf_op jit(solution)/shard_map/ppermute | solution.py:25
  47.9 6.0 %collective-permute-start.10 = (bf16[64,512]{1,0:T(8,128)(2,1)S(1)}, bf16[64,512]{1,0:T(8,128)(2,1)S(1)}, u32[]{:S(2)}, u32[]{:S(2)}) collective-permute-start(bf16[64,512]{1,0:T(8,128)(2,1)S(1)} %add_convert_fusion.2), channel_id=1, source_target_pairs={{0,256},{64,320},{128,384},{192,448},{256,0},{320,64},{384,128},{4... | collective-permute-start | bytes 196616 | tf_op jit(solution)/shard_map/ppermute | solution.py:25
  54.0 2.9 %collective-permute-start.11 = (bf16[64,512]{1,0:T(8,128)(2,1)S(1)}, bf16[64,512]{1,0:T(8,128)(2,1)S(1)}, u32[]{:S(2)}, u32[]{:S(2)}) collective-permute-start(bf16[64,512]{1,0:T(8,128)(2,1)S(1)} %add_convert_fusion.2), channel_id=1, source_target_pairs={{0,384},{64,448},{128,256},{192,320},{256,128},{320,192},{384,0},{... | collective-permute-start | bytes 196616 | tf_op jit(solution)/shard_map/ppermute | solution.py:25
  56.8 2.5 %collective-permute-start.9 = (bf16[64,512]{1,0:T(8,128)(2,1)S(1)}, bf16[64,512]{1,0:T(8,128)(2,1)S(1)}, u32[]{:S(2)}, u32[]{:S(2)}) collective-permute-start(bf16[64,512]{1,0:T(8,128)(2,1)S(1)} %add_convert_fusion.2), channel_id=1, source_target_pairs={{0,128},{64,192},{128,0},{192,64},{256,384},{320,448},{384,256},{4... | collective-permute-start | bytes 196616 | tf_op jit(solution)/shard_map/ppermute | solution.py:25
  59.3 0.2 add_convert_fusion
  59.5 4.2 %collective-permute-start.8 = (bf16[256,512]{1,0:T(8,128)(2,1)S(1)}, bf16[256,512]{1,0:T(8,128)(2,1)S(1)}, u32[]{:S(2)}, u32[]{:S(2)}) collective-permute-start(bf16[256,512]{1,0:T(8,128)(2,1)S(1)} %get-tuple-element.25), channel_id=1, source_target_pairs={{0,32},{16,48},{32,0},{48,16},{1,33},{17,49},{33,1},{49,17},{2,34}... | collective-permute-start | bytes 786440 | tf_op jit(solution)/shard_map/ppermute | solution.py:25
  63.8 1.6 %collective-permute-done.9 = bf16[64,512]{1,0:T(8,128)(2,1)S(1)} collective-permute-done((bf16[64,512]{1,0:T(8,128)(2,1)S(1)}, bf16[64,512]{1,0:T(8,128)(2,1)S(1)}, u32[]{:S(2)}, u32[]{:S(2)}) %collective-permute-start.9) | collective-permute-done | bytes 65568 | tf_op jit(solution)/shard_map/ppermute | solution.py:25
  65.4 15.0 %all-gather = bf16[12,64,512]{2,1,0:T(8,128)(2,1)S(1)} all-gather(bf16[3,64,512]{2,1,0:T(8,128)(2,1)S(1)} %pad_maximum_fusion.1), channel_id=2, replica_groups=mesh['y'=8,'x'=4,'zh'=4,'zl'=2,'core'=2] {'x'}, dimensions={0}, use_global_device_ids=true | all-gather | bytes 983040 | tf_op jit(solution)/shard_map/all_gather | solution.py:156
  80.4 0.9 shard_map.65.o0_ref
  81.4 2.1 %collective-permute-start.13 = (bf16[512,512]{1,0:T(8,128)(2,1)S(1)}, bf16[512,512]{1,0:T(8,128)(2,1)S(1)}, u32[]{:S(2)}, u32[]{:S(2)}) collective-permute-start(bf16[512,512]{1,0:T(8,128)(2,1)S(1)} %shard_map.65.o0_ref), channel_id=1, source_target_pairs={{0,2},{2,0},{1,3},{3,1},{4,6},{6,4},{5,7},{7,5},{8,10},{10,8},{9,1... | collective-permute-start | bytes 1572872 | tf_op jit(solution)/shard_map/ppermute | solution.py:29
  83.5 6.3 %collective-permute-start.12 = (bf16[512,512]{1,0:T(8,128)(2,1)S(1)}, bf16[512,512]{1,0:T(8,128)(2,1)S(1)}, u32[]{:S(2)}, u32[]{:S(2)}) collective-permute-start(bf16[512,512]{1,0:T(8,128)(2,1)S(1)} %shard_map.65.o0_ref), channel_id=1, source_target_pairs={{0,1},{1,0},{2,3},{3,2},{4,5},{5,4},{6,7},{7,6},{8,9},{9,8},{10,11... | collective-permute-start | bytes 1572872 | tf_op jit(solution)/shard_map/ppermute | solution.py:29
  89.8 4.0 %collective-permute-done.13.o2_ref = bf16[512,512]{1,0:T(8,128)(2,1)S(1)} collective-permute-done((bf16[512,512]{1,0:T(8,128)(2,1)S(1)}, bf16[512,512]{1,0:T(8,128)(2,1)S(1)}, u32[]{:S(2)}, u32[]{:S(2)}) %collective-permute-start.13) | collective-permute-done | bytes 524320 | tf_op jit(solution)/shard_map/ppermute | solution.py:29
  93.8 5.7 %collective-permute-start.14 = (bf16[512,512]{1,0:T(8,128)(2,1)S(1)}, bf16[512,512]{1,0:T(8,128)(2,1)S(1)}, u32[]{:S(2)}, u32[]{:S(2)}) collective-permute-start(bf16[512,512]{1,0:T(8,128)(2,1)S(1)} %collective-permute-done.13.o2_ref), channel_id=1, source_target_pairs={{0,1},{1,0},{2,3},{3,2},{4,5},{5,4},{6,7},{7,6},{8,9},{9,8},{10,11... | collective-permute-start | bytes 1572872 | tf_op jit(solution)/shard_map/ppermute | solution.py:29
  99.5 1.5 collective-permute-done.14.o3_ref
  101.0 4.7 %shard_map.66 = bf16[512,1024]{1,0:T(8,128)(2,1)S(1)} custom-call(s32[1]{0:T(128)} %bitcast.flip_ref, bf16[512,512]{1,0:T(8,128)(2,1)S(1)} %shard_map.65.o0_ref, bf16[512,512]{1,0:T(8,128)(2,1)S(1)} %collective-permute-done.12.o1_ref, bf16[512,512]{1,0:T(8,128)(2,1)S(1)} %collective-permute-done.13.o2_ref, ...), custom_call_target="tpu_custom_call" | custom-call | tf_op jit(solution)/shard_map/pallas_call | solution.py:174
  105.8 38.1 %all_to_all.9 = bf16[16,32,1024]{2,1,0:T(8,128)(2,1)S(1)} all-to-all(bf16[16,32,1024]{2,1,0:T(8,128)(2,1)S(1)} %bitcast.17), channel_id=1, replica_groups=mesh['y'=8,'x'=4,'zh'=4,'zl'=2,'core'=2] {'zh','zl','core'}, dimensions={0} | all-to-all | bytes 2097152 | tf_op jit(solution)/shard_map/all_to_all | solution.py:186
  143.9 0.8 shard_map.67
  (29 shorter events, 0.3 us)
Async XLA Ops:
  6.5 37.4 %copy-start.1 = (bf16[512,256]{1,0:T(8,128)(2,1)S(1)}, bf16[512,256]{1,0:T(8,128)(2,1)}, u32[]{:S(2)}) copy-start(bf16[512,256]{1,0:T(8,128)(2,1)} %k_ref.1) | copy-start | bytes 786436
  6.5 37.4 %copy-start = (bf16[512,512]{1,0:T(8,128)(2,1)S(1)}, bf16[512,512]{1,0:T(8,128)(2,1)}, u32[]{:S(2)}) copy-start(bf16[512,512]{1,0:T(8,128)(2,1)} %v_ref.1) | copy-start | bytes 1572868
  6.5 37.2 %copy-start.3 = (s32[512,15]{0,1:T(8,128)S(1)}, s32[512,15]{0,1:T(8,128)}, u32[]{:S(2)}) copy-start(s32[512,15]{0,1:T(8,128)} %param.10) | copy-start | bytes 92164
  6.5 37.3 %copy-start.4 = (f32[16,1]{0,1:T(1,128)S(1)}, f32[16,1]{0,1:T(1,128)}, u32[]{:S(2)}) copy-start(f32[16,1]{0,1:T(1,128)} %param.9) | copy-start | bytes 196
  6.5 37.4 %copy-start.2 = (bf16[512,256]{1,0:T(8,128)(2,1)S(1)}, bf16[512,256]{1,0:T(8,128)(2,1)}, u32[]{:S(2)}) copy-start(bf16[512,256]{1,0:T(8,128)(2,1)} %q_ref.3) | copy-start | bytes 786436
  6.5 94.5 %all-gather.4.cloned.1.call-start = ((), (), s32[]{:S(2)}) async-start(), calls=%async_computation.1 | async-start | bytes 4718592 | tf_op jit(solution)/shard_map/all_gather | solution.py:127
  8.2 18.5 %collective-permute-start.4 = (bf16[128,512]{1,0:T(8,128)(2,1)S(1)}, bf16[128,512]{1,0:T(8,128)(2,1)S(1)}, u32[]{:S(2)}, u32[]{:S(2)}) collective-permute-start(bf16[128,512]{1,0:T(8,128)(2,1)S(1)} %get-tuple-element.28), channel_id=1, source_target_pairs={{0,16},{16,0},{32,48},{48,32},{1,17},{17,1},{33,49},{49,33},{2,18}... | collective-permute-start | bytes 393224 | tf_op jit(solution)/shard_map/ppermute | solution.py:25
  12.1 14.5 %collective-permute-start = (bf16[512,128]{1,0:T(8,128)(2,1)}, bf16[512,128]{1,0:T(8,128)(2,1)S(1)}, u32[]{:S(2)}, u32[]{:S(2)}) collective-permute-start(bf16[512,128]{1,0:T(8,128)(2,1)} %param.11), channel_id=1, source_target_pairs={{0,0},{1,16},{2,32},{3,48},{16,1},{17,17},{18,33},{19,49},{32,2},{... | collective-permute-start | bytes 393224 | tf_op jit(solution)/shard_map/ppermute | solution.py:123
  20.5 6.2 %collective-permute-start.1 = (bf16[512,128]{1,0:T(8,128)(2,1)}, bf16[512,128]{1,0:T(8,128)(2,1)S(1)}, u32[]{:S(2)}, u32[]{:S(2)}) collective-permute-start(bf16[512,128]{1,0:T(8,128)(2,1)} %param.11), channel_id=1, source_target_pairs={{0,16},{1,0},{2,48},{3,32},{16,17},{17,1},{18,49},{19,33},{32,18},... | collective-permute-start | bytes 393224 | tf_op jit(solution)/shard_map/ppermute | solution.py:123
  22.5 8.9 %collective-permute-start.2 = (bf16[512,128]{1,0:T(8,128)(2,1)}, bf16[512,128]{1,0:T(8,128)(2,1)S(1)}, u32[]{:S(2)}, u32[]{:S(2)}) collective-permute-start(bf16[512,128]{1,0:T(8,128)(2,1)} %param.11), channel_id=1, source_target_pairs={{0,32},{1,48},{2,0},{3,16},{16,33},{17,49},{18,1},{19,17},{32,34},... | collective-permute-start | bytes 393224 | tf_op jit(solution)/shard_map/ppermute | solution.py:123
  24.4 9.1 %collective-permute-start.3 = (bf16[512,128]{1,0:T(8,128)(2,1)}, bf16[512,128]{1,0:T(8,128)(2,1)S(1)}, u32[]{:S(2)}, u32[]{:S(2)}) collective-permute-start(bf16[512,128]{1,0:T(8,128)(2,1)} %param.11), channel_id=1, source_target_pairs={{0,48},{1,32},{2,16},{3,0},{16,49},{17,33},{18,17},{19,1},{32,50},... | collective-permute-start | bytes 393224 | tf_op jit(solution)/shard_map/ppermute | solution.py:123
  34.4 7.3 %collective-permute-start.5 = (bf16[64,512]{1,0:T(8,128)(2,1)S(1)}, bf16[64,512]{1,0:T(8,128)(2,1)S(1)}, u32[]{:S(2)}, u32[]{:S(2)}) collective-permute-start(bf16[64,512]{1,0:T(8,128)(2,1)S(1)} %dynamic-slice_convert_fusion.2), channel_id=1, source_target_pairs={{0,32},{16,48},{32,0},{48,16},{1,33},{17,49},{33,1},{49,17},{2,34}... | collective-permute-start | bytes 196616 | tf_op jit(solution)/shard_map/ppermute | solution.py:25
  41.8 6.1 %collective-permute-start.6 = (bf16[64,512]{1,0:T(8,128)(2,1)S(1)}, bf16[64,512]{1,0:T(8,128)(2,1)S(1)}, u32[]{:S(2)}, u32[]{:S(2)}) collective-permute-start(bf16[64,512]{1,0:T(8,128)(2,1)S(1)} %fusion), channel_id=1, source_target_pairs={{0,64},{64,0},{128,192},{192,128},{256,320},{320,256},{384,448},{4... | collective-permute-start | bytes 196616 | tf_op jit(solution)/shard_map/ppermute | solution.py:25
  45.7 13.6 %collective-permute-start.7 = (bf16[128,512]{1,0:T(8,128)(2,1)S(1)}, bf16[128,512]{1,0:T(8,128)(2,1)S(1)}, u32[]{:S(2)}, u32[]{:S(2)}) collective-permute-start(bf16[128,512]{1,0:T(8,128)(2,1)S(1)} %get-tuple-element.19), channel_id=1, source_target_pairs={{0,16},{16,0},{32,48},{48,32},{1,17},{17,1},{33,49},{49,33},{2,18}... | collective-permute-start | bytes 393224 | tf_op jit(solution)/shard_map/ppermute | solution.py:25
  47.9 15.8 %collective-permute-start.10 = (bf16[64,512]{1,0:T(8,128)(2,1)S(1)}, bf16[64,512]{1,0:T(8,128)(2,1)S(1)}, u32[]{:S(2)}, u32[]{:S(2)}) collective-permute-start(bf16[64,512]{1,0:T(8,128)(2,1)S(1)} %add_convert_fusion.2), channel_id=1, source_target_pairs={{0,256},{64,320},{128,384},{192,448},{256,0},{320,64},{384,128},{4... | collective-permute-start | bytes 196616 | tf_op jit(solution)/shard_map/ppermute | solution.py:25
  54.0 9.8 %collective-permute-start.11 = (bf16[64,512]{1,0:T(8,128)(2,1)S(1)}, bf16[64,512]{1,0:T(8,128)(2,1)S(1)}, u32[]{:S(2)}, u32[]{:S(2)}) collective-permute-start(bf16[64,512]{1,0:T(8,128)(2,1)S(1)} %add_convert_fusion.2), channel_id=1, source_target_pairs={{0,384},{64,448},{128,256},{192,320},{256,128},{320,192},{384,0},{... | collective-permute-start | bytes 196616 | tf_op jit(solution)/shard_map/ppermute | solution.py:25
  56.8 8.6 %collective-permute-start.9 = (bf16[64,512]{1,0:T(8,128)(2,1)S(1)}, bf16[64,512]{1,0:T(8,128)(2,1)S(1)}, u32[]{:S(2)}, u32[]{:S(2)}) collective-permute-start(bf16[64,512]{1,0:T(8,128)(2,1)S(1)} %add_convert_fusion.2), channel_id=1, source_target_pairs={{0,128},{64,192},{128,0},{192,64},{256,384},{320,448},{384,256},{4... | collective-permute-start | bytes 196616 | tf_op jit(solution)/shard_map/ppermute | solution.py:25
  59.5 20.9 %collective-permute-start.8 = (bf16[256,512]{1,0:T(8,128)(2,1)S(1)}, bf16[256,512]{1,0:T(8,128)(2,1)S(1)}, u32[]{:S(2)}, u32[]{:S(2)}) collective-permute-start(bf16[256,512]{1,0:T(8,128)(2,1)S(1)} %get-tuple-element.25), channel_id=1, source_target_pairs={{0,32},{16,48},{32,0},{48,16},{1,33},{17,49},{33,1},{49,17},{2,34}... | collective-permute-start | bytes 786440 | tf_op jit(solution)/shard_map/ppermute | solution.py:25
  81.4 12.4 %collective-permute-start.13 = (bf16[512,512]{1,0:T(8,128)(2,1)S(1)}, bf16[512,512]{1,0:T(8,128)(2,1)S(1)}, u32[]{:S(2)}, u32[]{:S(2)}) collective-permute-start(bf16[512,512]{1,0:T(8,128)(2,1)S(1)} %shard_map.65.o0_ref), channel_id=1, source_target_pairs={{0,2},{2,0},{1,3},{3,1},{4,6},{6,4},{5,7},{7,5},{8,10},{10,8},{9,1... | collective-permute-start | bytes 1572872 | tf_op jit(solution)/shard_map/ppermute | solution.py:29
  83.5 16.0 %collective-permute-start.12 = (bf16[512,512]{1,0:T(8,128)(2,1)S(1)}, bf16[512,512]{1,0:T(8,128)(2,1)S(1)}, u32[]{:S(2)}, u32[]{:S(2)}) collective-permute-start(bf16[512,512]{1,0:T(8,128)(2,1)S(1)} %shard_map.65.o0_ref), channel_id=1, source_target_pairs={{0,1},{1,0},{2,3},{3,2},{4,5},{5,4},{6,7},{7,6},{8,9},{9,8},{10,11... | collective-permute-start | bytes 1572872 | tf_op jit(solution)/shard_map/ppermute | solution.py:29
  93.8 7.2 %collective-permute-start.14 = (bf16[512,512]{1,0:T(8,128)(2,1)S(1)}, bf16[512,512]{1,0:T(8,128)(2,1)S(1)}, u32[]{:S(2)}, u32[]{:S(2)}) collective-permute-start(bf16[512,512]{1,0:T(8,128)(2,1)S(1)} %collective-permute-done.13.o2_ref), channel_id=1, source_target_pairs={{0,1},{1,0},{2,3},{3,2},{4,5},{5,4},{6,7},{7,6},{8,9},{9,8},{10,11... | collective-permute-start | bytes 1572872 | tf_op jit(solution)/shard_map/ppermute | solution.py:29
Sparse Core Ops, SparseCore 0:
  34.5 64.8 all-gather.3

commit v7 on v6

--- a/solution.py
+++ b/solution.py
@@ -81,14 +81,22 @@
     o_ref[...] = total.astype(BF16)
 
 
-def project_kernel(flip_ref, o0_ref, o1_ref, o2_ref, o3_ref, w_ref, part_ref):
-    total = None
-    for j, o_ref in enumerate((o0_ref, o1_ref, o2_ref, o3_ref)):
-        k = jnp.bitwise_xor(flip_ref[0], j)
-        w = jnp.concatenate([w_ref[0, k], w_ref[1, k]], axis=1)
-        term = jnp.dot(o_ref[...], w, preferred_element_type=F32)
-        total = term if total is None else total + term
-    part_ref[...] = total.astype(BF16)
+def project_kernel(flip_ref, o0_ref, o1_ref, o2_ref, o3_ref, w_ref, part_ref, held_ref, sems):
+    copies = []
+    for i in range(w_ref.shape[0] // 2):
+        blocks = pl.ds(2 * i, 2)
+        copies.append(pltpu.make_async_copy(w_ref.at[blocks], held_ref.at[blocks], sems.at[i]))
+        copies[-1].start()
+    width = 2 * w_ref.shape[3]
+    for i, copy in enumerate(copies):
+        copy.wait()
+        total = None
+        for j, o_ref in enumerate((o0_ref, o1_ref, o2_ref, o3_ref)):
+            k = jnp.bitwise_xor(flip_ref[0], j)
+            w = jnp.concatenate([held_ref[2 * i, k], held_ref[2 * i + 1, k]], axis=1)
+            term = jnp.dot(o_ref[...], w, preferred_element_type=F32)
+            total = term if total is None else total + term
+        part_ref[:, i * width : (i + 1) * width] = total.astype(BF16)
 
 
 def sum_kernel(got_ref, out_ref):
@@ -170,15 +178,15 @@
     o_zc = flipped(o_z, "core")
     flip = jnp.bitwise_xor(x, u).astype(jnp.int32).reshape(1)
     width = out_weight.shape[1]
-    whole = pl.BlockSpec((rows, value_size), lambda i: (0, 0))
     part = pl.pallas_call(
         project_kernel,
-        grid=(ny // 2,),
         out_shape=jax.ShapeDtypeStruct((rows, ny * width), BF16),
-        in_specs=[SMEM]
-        + [whole] * 4
-        + [pl.BlockSpec((2, nu, value_size, width), lambda i: (i, 0, 0, 0))],
-        out_specs=pl.BlockSpec((rows, 2 * width), lambda i: (0, i)),
+        in_specs=[SMEM] + [VMEM] * 4 + [pl.BlockSpec(memory_space=pl.ANY)],
+        out_specs=VMEM,
+        scratch_shapes=[
+            pltpu.VMEM((ny, nu, value_size, width), BF16),
+            pltpu.SemaphoreType.DMA((ny // 2,)),
+        ],
         compiler_params=PARAMS,
     )(flip, o, o_c, o_z, o_zc, gathered)
 

time: 152 us -> 154 us (1.013)
  no operation moved by 1% of the time
where the time goes in v7:
time: 154 us; the launch traced here: 153 us
  starting transfers between devices  55.5 us (36%)
  blocking collectives  53.1 us (34%)
  waiting for transfers between devices  18 us (12%)
  between operations  13.8 us (9%)
  Pallas kernels  9.71 us (6%)
    all_to_all x1, blocking collectives, on_device(): back = lax.all_to_all(part, TP, 0, 0, tiled=True)  38.1 us
    ppermute x8, starting transfers between devices, crossed(): lax.ppermute(value, axis, [(i, i ^ by) for i in range(lax.axis_size(axis))])  26.8 us
    all_gather x1, blocking collectives, on_device(): far = lax.all_gather(jnp.stack(far), 'x', axis=0)  15 us
    ppermute x4, starting transfers between devices, on_device(): got.append(lax.ppermute(out_weight, ('x',) + QUAD, pairs))  14.5 us
    ppermute x3, starting transfers between devices, flipped(): return lax.ppermute(value, axis, [(0, 1), (1, 0)])  14.1 us
    ppermute x4, waiting for transfers between devices, on_device(): got.append(lax.ppermute(out_weight, ('x',) + QUAD, pairs))  6.78 us
    pallas_call x1, Pallas kernels, on_device(): pl.pallas_call(project_kernel, out_shape=jax.ShapeDtypeStruct((rows, ny *...  6.18 us
    ppermute x8, waiting for transfers between devices, crossed(): lax.ppermute(value, axis, [(i, i ^ by) for i in range(lax.axis_size(axis))])  5.69 us
  transfers between devices with their start and end apart: 16, of which 7 were waited for; matrix products, arithmetic and copies ran while one was open for 0% of the time, Pallas kernels for 2%

profile of v7, /device:TPU:1, one launch (start us, length us, event | category | flops | bytes accessed | tf_op | source)
XLA Modules:
  0.0 153.0 jit_solution(9906315426453653925)
XLA Ops:
  6.6 1.5 fusion.2
  8.2 3.9 %collective-permute-start.4 = (bf16[128,512]{1,0:T(8,128)(2,1)S(1)}, bf16[128,512]{1,0:T(8,128)(2,1)S(1)}, u32[]{:S(2)}, u32[]{:S(2)}) collective-permute-start(bf16[128,512]{1,0:T(8,128)(2,1)S(1)} %get-tuple-element.28), channel_id=1, source_target_pairs={{0,16},{16,0},{32,48},{48,32},{1,17},{17,1},{33,49},{49,33},{2,18}... | collective-permute-start | bytes 393224 | tf_op jit(solution)/shard_map/ppermute | solution.py:25
  12.1 8.4 %collective-permute-start = (bf16[512,128]{1,0:T(8,128)(2,1)}, bf16[512,128]{1,0:T(8,128)(2,1)S(1)}, u32[]{:S(2)}, u32[]{:S(2)}) collective-permute-start(bf16[512,128]{1,0:T(8,128)(2,1)} %param.11), channel_id=1, source_target_pairs={{0,0},{1,16},{2,32},{3,48},{16,1},{17,17},{18,33},{19,49},{32,2},{... | collective-permute-start | bytes 393224 | tf_op jit(solution)/shard_map/ppermute | solution.py:131
  20.5 1.9 %collective-permute-start.1 = (bf16[512,128]{1,0:T(8,128)(2,1)}, bf16[512,128]{1,0:T(8,128)(2,1)S(1)}, u32[]{:S(2)}, u32[]{:S(2)}) collective-permute-start(bf16[512,128]{1,0:T(8,128)(2,1)} %param.11), channel_id=1, source_target_pairs={{0,16},{1,0},{2,48},{3,32},{16,17},{17,1},{18,49},{19,33},{32,18},... | collective-permute-start | bytes 393224 | tf_op jit(solution)/shard_map/ppermute | solution.py:131
  22.5 1.9 %collective-permute-start.2 = (bf16[512,128]{1,0:T(8,128)(2,1)}, bf16[512,128]{1,0:T(8,128)(2,1)S(1)}, u32[]{:S(2)}, u32[]{:S(2)}) collective-permute-start(bf16[512,128]{1,0:T(8,128)(2,1)} %param.11), channel_id=1, source_target_pairs={{0,32},{1,48},{2,0},{3,16},{16,33},{17,49},{18,1},{19,17},{32,34},... | collective-permute-start | bytes 393224 | tf_op jit(solution)/shard_map/ppermute | solution.py:131
  24.4 2.3 %collective-permute-start.3 = (bf16[512,128]{1,0:T(8,128)(2,1)}, bf16[512,128]{1,0:T(8,128)(2,1)S(1)}, u32[]{:S(2)}, u32[]{:S(2)}) collective-permute-start(bf16[512,128]{1,0:T(8,128)(2,1)} %param.11), channel_id=1, source_target_pairs={{0,48},{1,32},{2,16},{3,0},{16,49},{17,33},{18,17},{19,1},{32,50},... | collective-permute-start | bytes 393224 | tf_op jit(solution)/shard_map/ppermute | solution.py:131
  26.7 4.6 %collective-permute-done.2 = bf16[512,128]{1,0:T(8,128)(2,1)S(1)} collective-permute-done((bf16[512,128]{1,0:T(8,128)(2,1)}, bf16[512,128]{1,0:T(8,128)(2,1)S(1)}, u32[]{:S(2)}, u32[]{:S(2)}) %collective-permute-start.2) | collective-permute-done | bytes 131104 | tf_op jit(solution)/shard_map/ppermute | solution.py:131
  31.4 2.1 %collective-permute-done.3 = bf16[512,128]{1,0:T(8,128)(2,1)S(1)} collective-permute-done((bf16[512,128]{1,0:T(8,128)(2,1)}, bf16[512,128]{1,0:T(8,128)(2,1)S(1)}, u32[]{:S(2)}, u32[]{:S(2)}) %collective-permute-start.3) | collective-permute-done | bytes 131104 | tf_op jit(solution)/shard_map/ppermute | solution.py:131
  33.5 0.9 pad_maximum_fusion
  34.4 3.2 %collective-permute-start.5 = (bf16[64,512]{1,0:T(8,128)(2,1)S(1)}, bf16[64,512]{1,0:T(8,128)(2,1)S(1)}, u32[]{:S(2)}, u32[]{:S(2)}) collective-permute-start(bf16[64,512]{1,0:T(8,128)(2,1)S(1)} %dynamic-slice_convert_fusion.2), channel_id=1, source_target_pairs={{0,32},{16,48},{32,0},{48,16},{1,33},{17,49},{33,1},{49,17},{2,34}... | collective-permute-start | bytes 196616 | tf_op jit(solution)/shard_map/ppermute | solution.py:25
  37.7 4.1 %collective-permute-done.5 = bf16[64,512]{1,0:T(8,128)(2,1)S(1)} collective-permute-done((bf16[64,512]{1,0:T(8,128)(2,1)S(1)}, bf16[64,512]{1,0:T(8,128)(2,1)S(1)}, u32[]{:S(2)}, u32[]{:S(2)}) %collective-permute-start.5) | collective-permute-done | bytes 65568 | tf_op jit(solution)/shard_map/ppermute | solution.py:25
  41.8 1.9 %collective-permute-start.6 = (bf16[64,512]{1,0:T(8,128)(2,1)S(1)}, bf16[64,512]{1,0:T(8,128)(2,1)S(1)}, u32[]{:S(2)}, u32[]{:S(2)}) collective-permute-start(bf16[64,512]{1,0:T(8,128)(2,1)S(1)} %fusion), channel_id=1, source_target_pairs={{0,64},{64,0},{128,192},{192,128},{256,320},{320,256},{384,448},{4... | collective-permute-start | bytes 196616 | tf_op jit(solution)/shard_map/ppermute | solution.py:25
  43.7 0.1 copy.10.index_ref
  43.9 0.1 copy.9.coef_ref
  44.0 1.8 %shard_map.64 = (f32[512,512]{1,0:T(8,128)S(1)}, f32[512,15]{1,0:T(8,128)S(1)}) custom-call(f32[16,1]{1,0:T(8,128)S(1)} %copy.9.coef_ref, s32[512,15]{1,0:T(8,128)S(1)} %copy.10.index_ref, bf16[512,256]{1,0:T(8,128)(2,1)S(1)} %copy-done.2, bf16[512,256]{1,0:T(8,128)(2,1)S(1)} %copy-done.1, bf16[512,512]{1,0:T(8,128)(2,1)S(1)} %copy-done), custom_call_target="tpu_custom_call" | custom-call | tf_op jit(solution)/shard_map/pallas_call | solution.py:149
  45.7 2.1 %collective-permute-start.7 = (bf16[128,512]{1,0:T(8,128)(2,1)S(1)}, bf16[128,512]{1,0:T(8,128)(2,1)S(1)}, u32[]{:S(2)}, u32[]{:S(2)}) collective-permute-start(bf16[128,512]{1,0:T(8,128)(2,1)S(1)} %get-tuple-element.19), channel_id=1, source_target_pairs={{0,16},{16,0},{32,48},{48,32},{1,17},{17,1},{33,49},{49,33},{2,18}... | collective-permute-start | bytes 393224 | tf_op jit(solution)/shard_map/ppermute | solution.py:25
  47.9 6.0 %collective-permute-start.10 = (bf16[64,512]{1,0:T(8,128)(2,1)S(1)}, bf16[64,512]{1,0:T(8,128)(2,1)S(1)}, u32[]{:S(2)}, u32[]{:S(2)}) collective-permute-start(bf16[64,512]{1,0:T(8,128)(2,1)S(1)} %add_convert_fusion.2), channel_id=1, source_target_pairs={{0,256},{64,320},{128,384},{192,448},{256,0},{320,64},{384,128},{4... | collective-permute-start | bytes 196616 | tf_op jit(solution)/shard_map/ppermute | solution.py:25
  54.0 2.9 %collective-permute-start.11 = (bf16[64,512]{1,0:T(8,128)(2,1)S(1)}, bf16[64,512]{1,0:T(8,128)(2,1)S(1)}, u32[]{:S(2)}, u32[]{:S(2)}) collective-permute-start(bf16[64,512]{1,0:T(8,128)(2,1)S(1)} %add_convert_fusion.2), channel_id=1, source_target_pairs={{0,384},{64,448},{128,256},{192,320},{256,128},{320,192},{384,0},{... | collective-permute-start | bytes 196616 | tf_op jit(solution)/shard_map/ppermute | solution.py:25
  56.8 2.5 %collective-permute-start.9 = (bf16[64,512]{1,0:T(8,128)(2,1)S(1)}, bf16[64,512]{1,0:T(8,128)(2,1)S(1)}, u32[]{:S(2)}, u32[]{:S(2)}) collective-permute-start(bf16[64,512]{1,0:T(8,128)(2,1)S(1)} %add_convert_fusion.2), channel_id=1, source_target_pairs={{0,128},{64,192},{128,0},{192,64},{256,384},{320,448},{384,256},{4... | collective-permute-start | bytes 196616 | tf_op jit(solution)/shard_map/ppermute | solution.py:25
  59.3 0.2 add_convert_fusion
  59.5 4.2 %collective-permute-start.8 = (bf16[256,512]{1,0:T(8,128)(2,1)S(1)}, bf16[256,512]{1,0:T(8,128)(2,1)S(1)}, u32[]{:S(2)}, u32[]{:S(2)}) collective-permute-start(bf16[256,512]{1,0:T(8,128)(2,1)S(1)} %get-tuple-element.25), channel_id=1, source_target_pairs={{0,32},{16,48},{32,0},{48,16},{1,33},{17,49},{33,1},{49,17},{2,34}... | collective-permute-start | bytes 786440 | tf_op jit(solution)/shard_map/ppermute | solution.py:25
  63.8 1.6 %collective-permute-done.9 = bf16[64,512]{1,0:T(8,128)(2,1)S(1)} collective-permute-done((bf16[64,512]{1,0:T(8,128)(2,1)S(1)}, bf16[64,512]{1,0:T(8,128)(2,1)S(1)}, u32[]{:S(2)}, u32[]{:S(2)}) %collective-permute-start.9) | collective-permute-done | bytes 65568 | tf_op jit(solution)/shard_map/ppermute | solution.py:25
  65.4 15.0 %all-gather = bf16[12,64,512]{2,1,0:T(8,128)(2,1)S(1)} all-gather(bf16[3,64,512]{2,1,0:T(8,128)(2,1)S(1)} %pad_maximum_fusion.1), channel_id=2, replica_groups=mesh['y'=8,'x'=4,'zh'=4,'zl'=2,'core'=2] {'x'}, dimensions={0}, use_global_device_ids=true | all-gather | bytes 983040 | tf_op jit(solution)/shard_map/all_gather | solution.py:164
  80.4 0.9 shard_map.65.o0_ref
  81.4 2.1 %collective-permute-start.13 = (bf16[512,512]{1,0:T(8,128)(2,1)S(1)}, bf16[512,512]{1,0:T(8,128)(2,1)S(1)}, u32[]{:S(2)}, u32[]{:S(2)}) collective-permute-start(bf16[512,512]{1,0:T(8,128)(2,1)S(1)} %shard_map.65.o0_ref), channel_id=1, source_target_pairs={{0,2},{2,0},{1,3},{3,1},{4,6},{6,4},{5,7},{7,5},{8,10},{10,8},{9,1... | collective-permute-start | bytes 1572872 | tf_op jit(solution)/shard_map/ppermute | solution.py:29
  83.5 6.3 %collective-permute-start.12 = (bf16[512,512]{1,0:T(8,128)(2,1)S(1)}, bf16[512,512]{1,0:T(8,128)(2,1)S(1)}, u32[]{:S(2)}, u32[]{:S(2)}) collective-permute-start(bf16[512,512]{1,0:T(8,128)(2,1)S(1)} %shard_map.65.o0_ref), channel_id=1, source_target_pairs={{0,1},{1,0},{2,3},{3,2},{4,5},{5,4},{6,7},{7,6},{8,9},{9,8},{10,11... | collective-permute-start | bytes 1572872 | tf_op jit(solution)/shard_map/ppermute | solution.py:29
  89.8 4.0 %collective-permute-done.13.o2_ref = bf16[512,512]{1,0:T(8,128)(2,1)S(1)} collective-permute-done((bf16[512,512]{1,0:T(8,128)(2,1)S(1)}, bf16[512,512]{1,0:T(8,128)(2,1)S(1)}, u32[]{:S(2)}, u32[]{:S(2)}) %collective-permute-start.13) | collective-permute-done | bytes 524320 | tf_op jit(solution)/shard_map/ppermute | solution.py:29
  93.8 5.7 %collective-permute-start.14 = (bf16[512,512]{1,0:T(8,128)(2,1)S(1)}, bf16[512,512]{1,0:T(8,128)(2,1)S(1)}, u32[]{:S(2)}, u32[]{:S(2)}) collective-permute-start(bf16[512,512]{1,0:T(8,128)(2,1)S(1)} %collective-permute-done.13.o2_ref), channel_id=1, source_target_pairs={{0,1},{1,0},{2,3},{3,2},{4,5},{5,4},{6,7},{7,6},{8,9},{9,8},{10,11... | collective-permute-start | bytes 1572872 | tf_op jit(solution)/shard_map/ppermute | solution.py:29
  99.5 1.5 collective-permute-done.14.o3_ref
  101.0 6.2 %shard_map.66 = bf16[512,1024]{1,0:T(8,128)(2,1)S(1)} custom-call(s32[1]{0:T(128)} %bitcast.flip_ref, bf16[512,512]{1,0:T(8,128)(2,1)S(1)} %shard_map.65.o0_ref, bf16[512,512]{1,0:T(8,128)(2,1)S(1)} %collective-permute-done.12.o1_ref, bf16[512,512]{1,0:T(8,128)(2,1)S(1)} %collective-permute-done.13.o2_ref, ...), custom_call_target="tpu_custom_call" | custom-call | tf_op jit(solution)/shard_map/pallas_call | solution.py:181
  107.2 38.1 %all_to_all.9 = bf16[16,32,1024]{2,1,0:T(8,128)(2,1)S(1)} all-to-all(bf16[16,32,1024]{2,1,0:T(8,128)(2,1)S(1)} %bitcast.17), channel_id=1, replica_groups=mesh['y'=8,'x'=4,'zh'=4,'zl'=2,'core'=2] {'zh','zl','core'}, dimensions={0} | all-to-all | bytes 2097152 | tf_op jit(solution)/shard_map/all_to_all | solution.py:194
  145.3 0.8 shard_map.67
  (29 shorter events, 0.3 us)
Async XLA Ops:
  6.5 37.4 %copy-start.1 = (bf16[512,256]{1,0:T(8,128)(2,1)S(1)}, bf16[512,256]{1,0:T(8,128)(2,1)}, u32[]{:S(2)}) copy-start(bf16[512,256]{1,0:T(8,128)(2,1)} %k_ref.1) | copy-start | bytes 786436
  6.5 37.4 %copy-start = (bf16[512,512]{1,0:T(8,128)(2,1)S(1)}, bf16[512,512]{1,0:T(8,128)(2,1)}, u32[]{:S(2)}) copy-start(bf16[512,512]{1,0:T(8,128)(2,1)} %v_ref.1) | copy-start | bytes 1572868
  6.5 37.2 %copy-start.3 = (s32[512,15]{0,1:T(8,128)S(1)}, s32[512,15]{0,1:T(8,128)}, u32[]{:S(2)}) copy-start(s32[512,15]{0,1:T(8,128)} %param.10) | copy-start | bytes 92164
  6.5 37.3 %copy-start.4 = (f32[16,1]{0,1:T(1,128)S(1)}, f32[16,1]{0,1:T(1,128)}, u32[]{:S(2)}) copy-start(f32[16,1]{0,1:T(1,128)} %param.9) | copy-start | bytes 196
  6.5 37.4 %copy-start.2 = (bf16[512,256]{1,0:T(8,128)(2,1)S(1)}, bf16[512,256]{1,0:T(8,128)(2,1)}, u32[]{:S(2)}) copy-start(bf16[512,256]{1,0:T(8,128)(2,1)} %q_ref.3) | copy-start | bytes 786436
  6.5 94.5 %all-gather.4.cloned.1.call-start = ((), (), s32[]{:S(2)}) async-start(), calls=%async_computation.1 | async-start | bytes 4718592 | tf_op jit(solution)/shard_map/all_gather | solution.py:135
  8.2 18.5 %collective-permute-start.4 = (bf16[128,512]{1,0:T(8,128)(2,1)S(1)}, bf16[128,512]{1,0:T(8,128)(2,1)S(1)}, u32[]{:S(2)}, u32[]{:S(2)}) collective-permute-start(bf16[128,512]{1,0:T(8,128)(2,1)S(1)} %get-tuple-element.28), channel_id=1, source_target_pairs={{0,16},{16,0},{32,48},{48,32},{1,17},{17,1},{33,49},{49,33},{2,18}... | collective-permute-start | bytes 393224 | tf_op jit(solution)/shard_map/ppermute | solution.py:25
  12.1 14.5 %collective-permute-start = (bf16[512,128]{1,0:T(8,128)(2,1)}, bf16[512,128]{1,0:T(8,128)(2,1)S(1)}, u32[]{:S(2)}, u32[]{:S(2)}) collective-permute-start(bf16[512,128]{1,0:T(8,128)(2,1)} %param.11), channel_id=1, source_target_pairs={{0,0},{1,16},{2,32},{3,48},{16,1},{17,17},{18,33},{19,49},{32,2},{... | collective-permute-start | bytes 393224 | tf_op jit(solution)/shard_map/ppermute | solution.py:131
  20.5 6.2 %collective-permute-start.1 = (bf16[512,128]{1,0:T(8,128)(2,1)}, bf16[512,128]{1,0:T(8,128)(2,1)S(1)}, u32[]{:S(2)}, u32[]{:S(2)}) collective-permute-start(bf16[512,128]{1,0:T(8,128)(2,1)} %param.11), channel_id=1, source_target_pairs={{0,16},{1,0},{2,48},{3,32},{16,17},{17,1},{18,49},{19,33},{32,18},... | collective-permute-start | bytes 393224 | tf_op jit(solution)/shard_map/ppermute | solution.py:131
  22.5 8.9 %collective-permute-start.2 = (bf16[512,128]{1,0:T(8,128)(2,1)}, bf16[512,128]{1,0:T(8,128)(2,1)S(1)}, u32[]{:S(2)}, u32[]{:S(2)}) collective-permute-start(bf16[512,128]{1,0:T(8,128)(2,1)} %param.11), channel_id=1, source_target_pairs={{0,32},{1,48},{2,0},{3,16},{16,33},{17,49},{18,1},{19,17},{32,34},... | collective-permute-start | bytes 393224 | tf_op jit(solution)/shard_map/ppermute | solution.py:131
  24.4 9.1 %collective-permute-start.3 = (bf16[512,128]{1,0:T(8,128)(2,1)}, bf16[512,128]{1,0:T(8,128)(2,1)S(1)}, u32[]{:S(2)}, u32[]{:S(2)}) collective-permute-start(bf16[512,128]{1,0:T(8,128)(2,1)} %param.11), channel_id=1, source_target_pairs={{0,48},{1,32},{2,16},{3,0},{16,49},{17,33},{18,17},{19,1},{32,50},... | collective-permute-start | bytes 393224 | tf_op jit(solution)/shard_map/ppermute | solution.py:131
  34.4 7.3 %collective-permute-start.5 = (bf16[64,512]{1,0:T(8,128)(2,1)S(1)}, bf16[64,512]{1,0:T(8,128)(2,1)S(1)}, u32[]{:S(2)}, u32[]{:S(2)}) collective-permute-start(bf16[64,512]{1,0:T(8,128)(2,1)S(1)} %dynamic-slice_convert_fusion.2), channel_id=1, source_target_pairs={{0,32},{16,48},{32,0},{48,16},{1,33},{17,49},{33,1},{49,17},{2,34}... | collective-permute-start | bytes 196616 | tf_op jit(solution)/shard_map/ppermute | solution.py:25
  41.8 6.1 %collective-permute-start.6 = (bf16[64,512]{1,0:T(8,128)(2,1)S(1)}, bf16[64,512]{1,0:T(8,128)(2,1)S(1)}, u32[]{:S(2)}, u32[]{:S(2)}) collective-permute-start(bf16[64,512]{1,0:T(8,128)(2,1)S(1)} %fusion), channel_id=1, source_target_pairs={{0,64},{64,0},{128,192},{192,128},{256,320},{320,256},{384,448},{4... | collective-permute-start | bytes 196616 | tf_op jit(solution)/shard_map/ppermute | solution.py:25
  45.7 13.6 %collective-permute-start.7 = (bf16[128,512]{1,0:T(8,128)(2,1)S(1)}, bf16[128,512]{1,0:T(8,128)(2,1)S(1)}, u32[]{:S(2)}, u32[]{:S(2)}) collective-permute-start(bf16[128,512]{1,0:T(8,128)(2,1)S(1)} %get-tuple-element.19), channel_id=1, source_target_pairs={{0,16},{16,0},{32,48},{48,32},{1,17},{17,1},{33,49},{49,33},{2,18}... | collective-permute-start | bytes 393224 | tf_op jit(solution)/shard_map/ppermute | solution.py:25
  47.9 15.8 %collective-permute-start.10 = (bf16[64,512]{1,0:T(8,128)(2,1)S(1)}, bf16[64,512]{1,0:T(8,128)(2,1)S(1)}, u32[]{:S(2)}, u32[]{:S(2)}) collective-permute-start(bf16[64,512]{1,0:T(8,128)(2,1)S(1)} %add_convert_fusion.2), channel_id=1, source_target_pairs={{0,256},{64,320},{128,384},{192,448},{256,0},{320,64},{384,128},{4... | collective-permute-start | bytes 196616 | tf_op jit(solution)/shard_map/ppermute | solution.py:25
  54.0 9.8 %collective-permute-start.11 = (bf16[64,512]{1,0:T(8,128)(2,1)S(1)}, bf16[64,512]{1,0:T(8,128)(2,1)S(1)}, u32[]{:S(2)}, u32[]{:S(2)}) collective-permute-start(bf16[64,512]{1,0:T(8,128)(2,1)S(1)} %add_convert_fusion.2), channel_id=1, source_target_pairs={{0,384},{64,448},{128,256},{192,320},{256,128},{320,192},{384,0},{... | collective-permute-start | bytes 196616 | tf_op jit(solution)/shard_map/ppermute | solution.py:25
  56.8 8.6 %collective-permute-start.9 = (bf16[64,512]{1,0:T(8,128)(2,1)S(1)}, bf16[64,512]{1,0:T(8,128)(2,1)S(1)}, u32[]{:S(2)}, u32[]{:S(2)}) collective-permute-start(bf16[64,512]{1,0:T(8,128)(2,1)S(1)} %add_convert_fusion.2), channel_id=1, source_target_pairs={{0,128},{64,192},{128,0},{192,64},{256,384},{320,448},{384,256},{4... | collective-permute-start | bytes 196616 | tf_op jit(solution)/shard_map/ppermute | solution.py:25
  59.5 20.9 %collective-permute-start.8 = (bf16[256,512]{1,0:T(8,128)(2,1)S(1)}, bf16[256,512]{1,0:T(8,128)(2,1)S(1)}, u32[]{:S(2)}, u32[]{:S(2)}) collective-permute-start(bf16[256,512]{1,0:T(8,128)(2,1)S(1)} %get-tuple-element.25), channel_id=1, source_target_pairs={{0,32},{16,48},{32,0},{48,16},{1,33},{17,49},{33,1},{49,17},{2,34}... | collective-permute-start | bytes 786440 | tf_op jit(solution)/shard_map/ppermute | solution.py:25
  81.4 12.4 %collective-permute-start.13 = (bf16[512,512]{1,0:T(8,128)(2,1)S(1)}, bf16[512,512]{1,0:T(8,128)(2,1)S(1)}, u32[]{:S(2)}, u32[]{:S(2)}) collective-permute-start(bf16[512,512]{1,0:T(8,128)(2,1)S(1)} %shard_map.65.o0_ref), channel_id=1, source_target_pairs={{0,2},{2,0},{1,3},{3,1},{4,6},{6,4},{5,7},{7,5},{8,10},{10,8},{9,1... | collective-permute-start | bytes 1572872 | tf_op jit(solution)/shard_map/ppermute | solution.py:29
  83.5 16.0 %collective-permute-start.12 = (bf16[512,512]{1,0:T(8,128)(2,1)S(1)}, bf16[512,512]{1,0:T(8,128)(2,1)S(1)}, u32[]{:S(2)}, u32[]{:S(2)}) collective-permute-start(bf16[512,512]{1,0:T(8,128)(2,1)S(1)} %shard_map.65.o0_ref), channel_id=1, source_target_pairs={{0,1},{1,0},{2,3},{3,2},{4,5},{5,4},{6,7},{7,6},{8,9},{9,8},{10,11... | collective-permute-start | bytes 1572872 | tf_op jit(solution)/shard_map/ppermute | solution.py:29
  93.8 7.2 %collective-permute-start.14 = (bf16[512,512]{1,0:T(8,128)(2,1)S(1)}, bf16[512,512]{1,0:T(8,128)(2,1)S(1)}, u32[]{:S(2)}, u32[]{:S(2)}) collective-permute-start(bf16[512,512]{1,0:T(8,128)(2,1)S(1)} %collective-permute-done.13.o2_ref), channel_id=1, source_target_pairs={{0,1},{1,0},{2,3},{3,2},{4,5},{5,4},{6,7},{7,6},{8,9},{9,8},{10,11... | collective-permute-start | bytes 1572872 | tf_op jit(solution)/shard_map/ppermute | solution.py:29
Sparse Core Ops, SparseCore 0:
  34.5 64.8 all-gather.3

commit v8 on v6

--- a/solution.py
+++ b/solution.py
@@ -23,6 +23,11 @@
 
 def crossed(value, axis, by):
     return lax.ppermute(value, axis, [(i, i ^ by) for i in range(lax.axis_size(axis))])
+
+
+def onward(value, axis, by, bit):
+    pairs = [(i, i ^ by) for i in range(lax.axis_size(axis)) if not i & bit]
+    return lax.ppermute(value, axis, pairs)
 
 
 def flipped(value, axis):
@@ -136,7 +141,7 @@
     late, part = lax.optimization_barrier((kept.astype(BF16), part))
     rest = crossed(late, "x", 1)
     near = jnp.where(odd == 1, jnp.concatenate([rest, one]), jnp.concatenate([one, rest]))
-    pair = crossed((state + near.astype(F32)).astype(BF16), "x", 2)
+    pair = onward((state + near.astype(F32)).astype(BF16), "x", 2, 2)
 
     local, lam = pl.pallas_call(
         local_kernel,
@@ -151,7 +156,7 @@
 
     beside, local = lax.optimization_barrier((beside, local))
     both = (quarter + beside.astype(F32)).astype(BF16)
-    third, fourth, fifth = crossed(both, "y", 2), crossed(both, "y", 4), crossed(both, "y", 6)
+    third, fourth, fifth = onward(both, "y", 2, 2), onward(both, "y", 4, 4), onward(both, "y", 6, 4)
     far = [beside, third, (fourth.astype(F32) + fifth.astype(F32)).astype(BF16)]
     far = lax.all_gather(jnp.stack(far), "x", axis=0)
 

time: 152 us -> 150 us (0.987)
  starting transfers between devices: 55.5 us -> 53.8 us
    ppermute x8 -> x4, starting transfers between devices: 26.8 us -> 11.2 us  [crossed(): lax.ppermute(value, axis, [(i, i ^ by) for i in range(lax.axis_size(axis))])]
    ppermute x0 -> x4, starting transfers between devices: none -> 14.5 us  [onward(): return lax.ppermute(value, axis, pairs)]
    ppermute x8 -> x4, waiting for transfers between devices: 5.69 us -> 4.09 us  [crossed(): lax.ppermute(value, axis, [(i, i ^ by) for i in range(lax.axis_size(axis))])]
  transfers between devices with their start and end apart: 16 -> 16, of which waited for: 7 -> 6; matrix products, arithmetic and copies ran while one was open for 0% -> 0% of each run, Pallas kernels for 2% -> 2%
where the time goes in v8:
time: 150 us; the launch traced here: 149 us
  starting transfers between devices  53.8 us (36%)
  blocking collectives  53.3 us (36%)
  waiting for transfers between devices  16.9 us (11%)
  between operations  13.8 us (9%)
  Pallas kernels  8.27 us (6%)
  matrix products  1.51 us (1%)
    all_to_all x1, blocking collectives, on_device(): back = lax.all_to_all(part, TP, 0, 0, tiled=True)  38.3 us
    all_gather x1, blocking collectives, on_device(): far = lax.all_gather(jnp.stack(far), 'x', axis=0)  15 us
    ppermute x4, starting transfers between devices, onward(): return lax.ppermute(value, axis, pairs)  14.5 us
    ppermute x4, starting transfers between devices, on_device(): got.append(lax.ppermute(out_weight, ('x',) + QUAD, pairs))  14.5 us
    ppermute x3, starting transfers between devices, flipped(): return lax.ppermute(value, axis, [(0, 1), (1, 0)])  13.6 us
    ppermute x4, starting transfers between devices, crossed(): lax.ppermute(value, axis, [(i, i ^ by) for i in range(lax.axis_size(axis))])  11.2 us
    ppermute x4, waiting for transfers between devices, on_device(): got.append(lax.ppermute(out_weight, ('x',) + QUAD, pairs))  6.78 us
    ppermute x3, waiting for transfers between devices, flipped(): return lax.ppermute(value, axis, [(0, 1), (1, 0)])  6.06 us
  transfers between devices with their start and end apart: 16, of which 6 were waited for; matrix products, arithmetic and copies ran while one was open for 0% of the time, Pallas kernels for 2%

profile of v8, /device:TPU:1, one launch (start us, length us, event | category | flops | bytes accessed | tf_op | source)
XLA Modules:
  0.0 149.1 jit_solution(4977690655563770737)
XLA Ops:
  6.6 1.5 %fusion.2 = f32[256,512]{1,0:T(8,128)S(1)} fusion(bf16[512,256]{1,0:T(8,128)(2,1)} %k_ref.1, bf16[512,512]{1,0:T(8,128)(2,1)} %v_ref.1), kind=kOutput, calls=%fused_computation.13 | convolution fusion | flops 134217728 | bytes 1310720 | tf_op jit(solution)/shard_map/dot_general | solution.py:118
  8.2 3.9 %collective-permute-start.4 = (bf16[128,512]{1,0:T(8,128)(2,1)S(1)}, bf16[128,512]{1,0:T(8,128)(2,1)S(1)}, u32[]{:S(2)}, u32[]{:S(2)}) collective-permute-start(bf16[128,512]{1,0:T(8,128)(2,1)S(1)} %get-tuple-element.28), channel_id=1, source_target_pairs={{0,16},{16,0},{32,48},{48,32},{1,17},{17,1},{33,49},{49,33},{2,18}... | collective-permute-start | bytes 393224 | tf_op jit(solution)/shard_map/ppermute | solution.py:25
  12.1 8.4 %collective-permute-start = (bf16[512,128]{1,0:T(8,128)(2,1)}, bf16[512,128]{1,0:T(8,128)(2,1)S(1)}, u32[]{:S(2)}, u32[]{:S(2)}) collective-permute-start(bf16[512,128]{1,0:T(8,128)(2,1)} %param.11), channel_id=1, source_target_pairs={{0,0},{1,16},{2,32},{3,48},{16,1},{17,17},{18,33},{19,49},{32,2},{... | collective-permute-start | bytes 393224 | tf_op jit(solution)/shard_map/ppermute | solution.py:128
  20.5 1.9 %collective-permute-start.1 = (bf16[512,128]{1,0:T(8,128)(2,1)}, bf16[512,128]{1,0:T(8,128)(2,1)S(1)}, u32[]{:S(2)}, u32[]{:S(2)}) collective-permute-start(bf16[512,128]{1,0:T(8,128)(2,1)} %param.11), channel_id=1, source_target_pairs={{0,16},{1,0},{2,48},{3,32},{16,17},{17,1},{18,49},{19,33},{32,18},... | collective-permute-start | bytes 393224 | tf_op jit(solution)/shard_map/ppermute | solution.py:128
  22.5 1.9 %collective-permute-start.2 = (bf16[512,128]{1,0:T(8,128)(2,1)}, bf16[512,128]{1,0:T(8,128)(2,1)S(1)}, u32[]{:S(2)}, u32[]{:S(2)}) collective-permute-start(bf16[512,128]{1,0:T(8,128)(2,1)} %param.11), channel_id=1, source_target_pairs={{0,32},{1,48},{2,0},{3,16},{16,33},{17,49},{18,1},{19,17},{32,34},... | collective-permute-start | bytes 393224 | tf_op jit(solution)/shard_map/ppermute | solution.py:128
  24.4 2.3 %collective-permute-start.3 = (bf16[512,128]{1,0:T(8,128)(2,1)}, bf16[512,128]{1,0:T(8,128)(2,1)S(1)}, u32[]{:S(2)}, u32[]{:S(2)}) collective-permute-start(bf16[512,128]{1,0:T(8,128)(2,1)} %param.11), channel_id=1, source_target_pairs={{0,48},{1,32},{2,16},{3,0},{16,49},{17,33},{18,17},{19,1},{32,50},... | collective-permute-start | bytes 393224 | tf_op jit(solution)/shard_map/ppermute | solution.py:128
  26.7 0.1 collective-permute-done.1
  26.7 4.6 %collective-permute-done.2 = bf16[512,128]{1,0:T(8,128)(2,1)S(1)} collective-permute-done((bf16[512,128]{1,0:T(8,128)(2,1)}, bf16[512,128]{1,0:T(8,128)(2,1)S(1)}, u32[]{:S(2)}, u32[]{:S(2)}) %collective-permute-start.2) | collective-permute-done | bytes 131104 | tf_op jit(solution)/shard_map/ppermute | solution.py:128
  31.4 2.1 %collective-permute-done.3 = bf16[512,128]{1,0:T(8,128)(2,1)S(1)} collective-permute-done((bf16[512,128]{1,0:T(8,128)(2,1)}, bf16[512,128]{1,0:T(8,128)(2,1)S(1)}, u32[]{:S(2)}, u32[]{:S(2)}) %collective-permute-start.3) | collective-permute-done | bytes 131104 | tf_op jit(solution)/shard_map/ppermute | solution.py:128
  33.5 0.9 pad_maximum_fusion
  34.4 3.2 %collective-permute-start.5 = (bf16[64,512]{1,0:T(8,128)(2,1)S(1)}, bf16[64,512]{1,0:T(8,128)(2,1)S(1)}, u32[]{:S(2)}, u32[]{:S(2)}) collective-permute-start(bf16[64,512]{1,0:T(8,128)(2,1)S(1)} %dynamic-slice_convert_fusion.2), channel_id=1, source_target_pairs={{0,32},{16,48},{32,0},{48,16},{1,33},{17,49},{33,1},{49,17},{2,34}... | collective-permute-start | bytes 196616 | tf_op jit(solution)/shard_map/ppermute | solution.py:25
  37.7 4.1 %collective-permute-done.5 = bf16[64,512]{1,0:T(8,128)(2,1)S(1)} collective-permute-done((bf16[64,512]{1,0:T(8,128)(2,1)S(1)}, bf16[64,512]{1,0:T(8,128)(2,1)S(1)}, u32[]{:S(2)}, u32[]{:S(2)}) %collective-permute-start.5) | collective-permute-done | bytes 65568 | tf_op jit(solution)/shard_map/ppermute | solution.py:25
  41.8 1.9 %collective-permute-start.6 = (bf16[64,512]{1,0:T(8,128)(2,1)S(1)}, bf16[64,512]{1,0:T(8,128)(2,1)S(1)}, u32[]{:S(2)}, u32[]{:S(2)}) collective-permute-start(bf16[64,512]{1,0:T(8,128)(2,1)S(1)} %fusion), channel_id=1, source_target_pairs={{0,64},{64,0},{128,192},{192,128},{256,320},{320,256},{384,448},{4... | collective-permute-start | bytes 196616 | tf_op jit(solution)/shard_map/ppermute | solution.py:25
  43.7 0.1 copy.10.index_ref
  43.9 0.1 copy.9.coef_ref
  44.0 1.8 %shard_map.64 = (f32[512,512]{1,0:T(8,128)S(1)}, f32[512,15]{1,0:T(8,128)S(1)}) custom-call(f32[16,1]{1,0:T(8,128)S(1)} %copy.9.coef_ref, s32[512,15]{1,0:T(8,128)S(1)} %copy.10.index_ref, bf16[512,256]{1,0:T(8,128)(2,1)S(1)} %copy-done.2, bf16[512,256]{1,0:T(8,128)(2,1)S(1)} %copy-done.1, bf16[512,512]{1,0:T(8,128)(2,1)S(1)} %copy-done), custom_call_target="tpu_custom_call" | custom-call | tf_op jit(solution)/shard_map/pallas_call | solution.py:146
  45.7 2.1 %collective-permute-start.7 = (bf16[128,512]{1,0:T(8,128)(2,1)S(1)}, bf16[128,512]{1,0:T(8,128)(2,1)S(1)}, u32[]{:S(2)}, u32[]{:S(2)}) collective-permute-start(bf16[128,512]{1,0:T(8,128)(2,1)S(1)} %get-tuple-element.19), channel_id=1, source_target_pairs={{0,16},{16,0},{32,48},{48,32},{1,17},{17,1},{33,49},{49,33},{2,18}... | collective-permute-start | bytes 393224 | tf_op jit(solution)/shard_map/ppermute | solution.py:25
  47.9 6.0 %collective-permute-start.10 = (bf16[64,512]{1,0:T(8,128)(2,1)S(1)}, bf16[64,512]{1,0:T(8,128)(2,1)S(1)}, u32[]{:S(2)}, u32[]{:S(2)}) collective-permute-start(bf16[64,512]{1,0:T(8,128)(2,1)S(1)} %add_convert_fusion.2), channel_id=1, source_target_pairs={{0,256},{64,320},{128,384},{192,448},{1,257},{65,321},{129,385},{1... | collective-permute-start | bytes 196616 | tf_op jit(solution)/shard_map/ppermute | solution.py:30
  54.0 1.3 collective-permute-start.11
  55.3 2.4 %collective-permute-start.9 = (bf16[64,512]{1,0:T(8,128)(2,1)S(1)}, bf16[64,512]{1,0:T(8,128)(2,1)S(1)}, u32[]{:S(2)}, u32[]{:S(2)}) collective-permute-start(bf16[64,512]{1,0:T(8,128)(2,1)S(1)} %add_convert_fusion.2), channel_id=1, source_target_pairs={{0,128},{64,192},{256,384},{320,448},{1,129},{65,193},{257,385},{3... | collective-permute-start | bytes 196616 | tf_op jit(solution)/shard_map/ppermute | solution.py:30
  57.7 0.2 add_convert_fusion
  57.8 4.8 %collective-permute-start.8 = (bf16[256,512]{1,0:T(8,128)(2,1)S(1)}, bf16[256,512]{1,0:T(8,128)(2,1)S(1)}, u32[]{:S(2)}, u32[]{:S(2)}) collective-permute-start(bf16[256,512]{1,0:T(8,128)(2,1)S(1)} %get-tuple-element.25), channel_id=1, source_target_pairs={{0,32},{16,48},{1,33},{17,49},{2,34},{18,50},{3,35},{19,51},{4,36}... | collective-permute-start | bytes 786440 | tf_op jit(solution)/shard_map/ppermute | solution.py:30
  62.7 15.0 %all-gather = bf16[12,64,512]{2,1,0:T(8,128)(2,1)S(1)} all-gather(bf16[3,64,512]{2,1,0:T(8,128)(2,1)S(1)} %pad_maximum_fusion.1), channel_id=2, replica_groups=mesh['y'=8,'x'=4,'zh'=4,'zl'=2,'core'=2] {'x'}, dimensions={0}, use_global_device_ids=true | all-gather | bytes 983040 | tf_op jit(solution)/shard_map/all_gather | solution.py:161
  77.7 0.9 shard_map.65.o0_ref
  78.6 1.9 %collective-permute-start.13 = (bf16[512,512]{1,0:T(8,128)(2,1)S(1)}, bf16[512,512]{1,0:T(8,128)(2,1)S(1)}, u32[]{:S(2)}, u32[]{:S(2)}) collective-permute-start(bf16[512,512]{1,0:T(8,128)(2,1)S(1)} %shard_map.65.o0_ref), channel_id=1, source_target_pairs={{0,2},{2,0},{1,3},{3,1},{4,6},{6,4},{5,7},{7,5},{8,10},{10,8},{9,1... | collective-permute-start | bytes 1572872 | tf_op jit(solution)/shard_map/ppermute | solution.py:34
  80.6 5.6 %collective-permute-start.12 = (bf16[512,512]{1,0:T(8,128)(2,1)S(1)}, bf16[512,512]{1,0:T(8,128)(2,1)S(1)}, u32[]{:S(2)}, u32[]{:S(2)}) collective-permute-start(bf16[512,512]{1,0:T(8,128)(2,1)S(1)} %shard_map.65.o0_ref), channel_id=1, source_target_pairs={{0,1},{1,0},{2,3},{3,2},{4,5},{5,4},{6,7},{7,6},{8,9},{9,8},{10,11... | collective-permute-start | bytes 1572872 | tf_op jit(solution)/shard_map/ppermute | solution.py:34
  86.2 4.6 %collective-permute-done.13.o2_ref = bf16[512,512]{1,0:T(8,128)(2,1)S(1)} collective-permute-done((bf16[512,512]{1,0:T(8,128)(2,1)S(1)}, bf16[512,512]{1,0:T(8,128)(2,1)S(1)}, u32[]{:S(2)}, u32[]{:S(2)}) %collective-permute-start.13) | collective-permute-done | bytes 524320 | tf_op jit(solution)/shard_map/ppermute | solution.py:34
  90.8 6.0 %collective-permute-start.14 = (bf16[512,512]{1,0:T(8,128)(2,1)S(1)}, bf16[512,512]{1,0:T(8,128)(2,1)S(1)}, u32[]{:S(2)}, u32[]{:S(2)}) collective-permute-start(bf16[512,512]{1,0:T(8,128)(2,1)S(1)} %collective-permute-done.13.o2_ref), channel_id=1, source_target_pairs={{0,1},{1,0},{2,3},{3,2},{4,5},{5,4},{6,7},{7,6},{8,9},{9,8},{10,11... | collective-permute-start | bytes 1572872 | tf_op jit(solution)/shard_map/ppermute | solution.py:34
  96.8 1.5 %collective-permute-done.14.o3_ref = bf16[512,512]{1,0:T(8,128)(2,1)S(1)} collective-permute-done((bf16[512,512]{1,0:T(8,128)(2,1)S(1)}, bf16[512,512]{1,0:T(8,128)(2,1)S(1)}, u32[]{:S(2)}, u32[]{:S(2)}) %collective-permute-start.14) | collective-permute-done | bytes 524320 | tf_op jit(solution)/shard_map/ppermute | solution.py:34
  98.3 4.7 %shard_map.66 = bf16[512,1024]{1,0:T(8,128)(2,1)S(1)} custom-call(s32[1]{0:T(128)} %bitcast.flip_ref, bf16[512,512]{1,0:T(8,128)(2,1)S(1)} %shard_map.65.o0_ref, bf16[512,512]{1,0:T(8,128)(2,1)S(1)} %collective-permute-done.12.o1_ref, bf16[512,512]{1,0:T(8,128)(2,1)S(1)} %collective-permute-done.13.o2_ref, ...), custom_call_target="tpu_custom_call" | custom-call | tf_op jit(solution)/shard_map/pallas_call | solution.py:179
  103.0 38.3 %all_to_all.9 = bf16[16,32,1024]{2,1,0:T(8,128)(2,1)S(1)} all-to-all(bf16[16,32,1024]{2,1,0:T(8,128)(2,1)S(1)} %bitcast.17), channel_id=1, replica_groups=mesh['y'=8,'x'=4,'zh'=4,'zl'=2,'core'=2] {'zh','zl','core'}, dimensions={0} | all-to-all | bytes 2097152 | tf_op jit(solution)/shard_map/all_to_all | solution.py:191
  141.4 0.8 shard_map.67
  (29 shorter events, 0.3 us)
Async XLA Ops:
  6.5 37.4 %copy-start.1 = (bf16[512,256]{1,0:T(8,128)(2,1)S(1)}, bf16[512,256]{1,0:T(8,128)(2,1)}, u32[]{:S(2)}) copy-start(bf16[512,256]{1,0:T(8,128)(2,1)} %k_ref.1) | copy-start | bytes 786436
  6.5 37.4 %copy-start = (bf16[512,512]{1,0:T(8,128)(2,1)S(1)}, bf16[512,512]{1,0:T(8,128)(2,1)}, u32[]{:S(2)}) copy-start(bf16[512,512]{1,0:T(8,128)(2,1)} %v_ref.1) | copy-start | bytes 1572868
  6.5 37.2 %copy-start.3 = (s32[512,15]{0,1:T(8,128)S(1)}, s32[512,15]{0,1:T(8,128)}, u32[]{:S(2)}) copy-start(s32[512,15]{0,1:T(8,128)} %param.10) | copy-start | bytes 92164
  6.5 37.3 %copy-start.4 = (f32[16,1]{0,1:T(1,128)S(1)}, f32[16,1]{0,1:T(1,128)}, u32[]{:S(2)}) copy-start(f32[16,1]{0,1:T(1,128)} %param.9) | copy-start | bytes 196
  6.5 37.4 %copy-start.2 = (bf16[512,256]{1,0:T(8,128)(2,1)S(1)}, bf16[512,256]{1,0:T(8,128)(2,1)}, u32[]{:S(2)}) copy-start(bf16[512,256]{1,0:T(8,128)(2,1)} %q_ref.3) | copy-start | bytes 786436
  6.5 91.7 %all-gather.4.cloned.1.call-start = ((), (), s32[]{:S(2)}) async-start(), calls=%async_computation.1 | async-start | bytes 4718592 | tf_op jit(solution)/shard_map/all_gather | solution.py:132
  8.2 18.5 %collective-permute-start.4 = (bf16[128,512]{1,0:T(8,128)(2,1)S(1)}, bf16[128,512]{1,0:T(8,128)(2,1)S(1)}, u32[]{:S(2)}, u32[]{:S(2)}) collective-permute-start(bf16[128,512]{1,0:T(8,128)(2,1)S(1)} %get-tuple-element.28), channel_id=1, source_target_pairs={{0,16},{16,0},{32,48},{48,32},{1,17},{17,1},{33,49},{49,33},{2,18}... | collective-permute-start | bytes 393224 | tf_op jit(solution)/shard_map/ppermute | solution.py:25
  12.1 14.5 %collective-permute-start = (bf16[512,128]{1,0:T(8,128)(2,1)}, bf16[512,128]{1,0:T(8,128)(2,1)S(1)}, u32[]{:S(2)}, u32[]{:S(2)}) collective-permute-start(bf16[512,128]{1,0:T(8,128)(2,1)} %param.11), channel_id=1, source_target_pairs={{0,0},{1,16},{2,32},{3,48},{16,1},{17,17},{18,33},{19,49},{32,2},{... | collective-permute-start | bytes 393224 | tf_op jit(solution)/shard_map/ppermute | solution.py:128
  20.5 6.2 %collective-permute-start.1 = (bf16[512,128]{1,0:T(8,128)(2,1)}, bf16[512,128]{1,0:T(8,128)(2,1)S(1)}, u32[]{:S(2)}, u32[]{:S(2)}) collective-permute-start(bf16[512,128]{1,0:T(8,128)(2,1)} %param.11), channel_id=1, source_target_pairs={{0,16},{1,0},{2,48},{3,32},{16,17},{17,1},{18,49},{19,33},{32,18},... | collective-permute-start | bytes 393224 | tf_op jit(solution)/shard_map/ppermute | solution.py:128
  22.5 8.9 %collective-permute-start.2 = (bf16[512,128]{1,0:T(8,128)(2,1)}, bf16[512,128]{1,0:T(8,128)(2,1)S(1)}, u32[]{:S(2)}, u32[]{:S(2)}) collective-permute-start(bf16[512,128]{1,0:T(8,128)(2,1)} %param.11), channel_id=1, source_target_pairs={{0,32},{1,48},{2,0},{3,16},{16,33},{17,49},{18,1},{19,17},{32,34},... | collective-permute-start | bytes 393224 | tf_op jit(solution)/shard_map/ppermute | solution.py:128
  24.4 9.1 %collective-permute-start.3 = (bf16[512,128]{1,0:T(8,128)(2,1)}, bf16[512,128]{1,0:T(8,128)(2,1)S(1)}, u32[]{:S(2)}, u32[]{:S(2)}) collective-permute-start(bf16[512,128]{1,0:T(8,128)(2,1)} %param.11), channel_id=1, source_target_pairs={{0,48},{1,32},{2,16},{3,0},{16,49},{17,33},{18,17},{19,1},{32,50},... | collective-permute-start | bytes 393224 | tf_op jit(solution)/shard_map/ppermute | solution.py:128
  34.4 7.3 %collective-permute-start.5 = (bf16[64,512]{1,0:T(8,128)(2,1)S(1)}, bf16[64,512]{1,0:T(8,128)(2,1)S(1)}, u32[]{:S(2)}, u32[]{:S(2)}) collective-permute-start(bf16[64,512]{1,0:T(8,128)(2,1)S(1)} %dynamic-slice_convert_fusion.2), channel_id=1, source_target_pairs={{0,32},{16,48},{32,0},{48,16},{1,33},{17,49},{33,1},{49,17},{2,34}... | collective-permute-start | bytes 196616 | tf_op jit(solution)/shard_map/ppermute | solution.py:25
  41.8 6.1 %collective-permute-start.6 = (bf16[64,512]{1,0:T(8,128)(2,1)S(1)}, bf16[64,512]{1,0:T(8,128)(2,1)S(1)}, u32[]{:S(2)}, u32[]{:S(2)}) collective-permute-start(bf16[64,512]{1,0:T(8,128)(2,1)S(1)} %fusion), channel_id=1, source_target_pairs={{0,64},{64,0},{128,192},{192,128},{256,320},{320,256},{384,448},{4... | collective-permute-start | bytes 196616 | tf_op jit(solution)/shard_map/ppermute | solution.py:25
  45.7 12.0 %collective-permute-start.7 = (bf16[128,512]{1,0:T(8,128)(2,1)S(1)}, bf16[128,512]{1,0:T(8,128)(2,1)S(1)}, u32[]{:S(2)}, u32[]{:S(2)}) collective-permute-start(bf16[128,512]{1,0:T(8,128)(2,1)S(1)} %get-tuple-element.19), channel_id=1, source_target_pairs={{0,16},{16,0},{32,48},{48,32},{1,17},{17,1},{33,49},{49,33},{2,18}... | collective-permute-start | bytes 393224 | tf_op jit(solution)/shard_map/ppermute | solution.py:25
  47.9 14.7 %collective-permute-start.10 = (bf16[64,512]{1,0:T(8,128)(2,1)S(1)}, bf16[64,512]{1,0:T(8,128)(2,1)S(1)}, u32[]{:S(2)}, u32[]{:S(2)}) collective-permute-start(bf16[64,512]{1,0:T(8,128)(2,1)S(1)} %add_convert_fusion.2), channel_id=1, source_target_pairs={{0,256},{64,320},{128,384},{192,448},{1,257},{65,321},{129,385},{1... | collective-permute-start | bytes 196616 | tf_op jit(solution)/shard_map/ppermute | solution.py:30
  54.0 8.7 %collective-permute-start.11 = (bf16[64,512]{1,0:T(8,128)(2,1)S(1)}, bf16[64,512]{1,0:T(8,128)(2,1)S(1)}, u32[]{:S(2)}, u32[]{:S(2)}) collective-permute-start(bf16[64,512]{1,0:T(8,128)(2,1)S(1)} %add_convert_fusion.2), channel_id=1, source_target_pairs={{0,384},{64,448},{128,256},{192,320},{1,385},{65,449},{129,257},{1... | collective-permute-start | bytes 196616 | tf_op jit(solution)/shard_map/ppermute | solution.py:30
  55.3 7.4 %collective-permute-start.9 = (bf16[64,512]{1,0:T(8,128)(2,1)S(1)}, bf16[64,512]{1,0:T(8,128)(2,1)S(1)}, u32[]{:S(2)}, u32[]{:S(2)}) collective-permute-start(bf16[64,512]{1,0:T(8,128)(2,1)S(1)} %add_convert_fusion.2), channel_id=1, source_target_pairs={{0,128},{64,192},{256,384},{320,448},{1,129},{65,193},{257,385},{3... | collective-permute-start | bytes 196616 | tf_op jit(solution)/shard_map/ppermute | solution.py:30
  57.8 19.8 %collective-permute-start.8 = (bf16[256,512]{1,0:T(8,128)(2,1)S(1)}, bf16[256,512]{1,0:T(8,128)(2,1)S(1)}, u32[]{:S(2)}, u32[]{:S(2)}) collective-permute-start(bf16[256,512]{1,0:T(8,128)(2,1)S(1)} %get-tuple-element.25), channel_id=1, source_target_pairs={{0,32},{16,48},{1,33},{17,49},{2,34},{18,50},{3,35},{19,51},{4,36}... | collective-permute-start | bytes 786440 | tf_op jit(solution)/shard_map/ppermute | solution.py:30
  78.6 12.1 %collective-permute-start.13 = (bf16[512,512]{1,0:T(8,128)(2,1)S(1)}, bf16[512,512]{1,0:T(8,128)(2,1)S(1)}, u32[]{:S(2)}, u32[]{:S(2)}) collective-permute-start(bf16[512,512]{1,0:T(8,128)(2,1)S(1)} %shard_map.65.o0_ref), channel_id=1, source_target_pairs={{0,2},{2,0},{1,3},{3,1},{4,6},{6,4},{5,7},{7,5},{8,10},{10,8},{9,1... | collective-permute-start | bytes 1572872 | tf_op jit(solution)/shard_map/ppermute | solution.py:34
  80.6 16.2 %collective-permute-start.12 = (bf16[512,512]{1,0:T(8,128)(2,1)S(1)}, bf16[512,512]{1,0:T(8,128)(2,1)S(1)}, u32[]{:S(2)}, u32[]{:S(2)}) collective-permute-start(bf16[512,512]{1,0:T(8,128)(2,1)S(1)} %shard_map.65.o0_ref), channel_id=1, source_target_pairs={{0,1},{1,0},{2,3},{3,2},{4,5},{5,4},{6,7},{7,6},{8,9},{9,8},{10,11... | collective-permute-start | bytes 1572872 | tf_op jit(solution)/shard_map/ppermute | solution.py:34
  90.8 7.5 %collective-permute-start.14 = (bf16[512,512]{1,0:T(8,128)(2,1)S(1)}, bf16[512,512]{1,0:T(8,128)(2,1)S(1)}, u32[]{:S(2)}, u32[]{:S(2)}) collective-permute-start(bf16[512,512]{1,0:T(8,128)(2,1)S(1)} %collective-permute-done.13.o2_ref), channel_id=1, source_target_pairs={{0,1},{1,0},{2,3},{3,2},{4,5},{5,4},{6,7},{7,6},{8,9},{9,8},{10,11... | collective-permute-start | bytes 1572872 | tf_op jit(solution)/shard_map/ppermute | solution.py:34
Sparse Core Ops, SparseCore 0:
  34.5 62.0 all-gather.3

commit v9 on v8

--- a/solution.py
+++ b/solution.py
@@ -139,7 +139,7 @@
     beside = crossed(quarter.astype(BF16), "y", 1)
 
     late, part = lax.optimization_barrier((kept.astype(BF16), part))
-    rest = crossed(late, "x", 1)
+    rest = lax.ppermute(late, "x", [(0, 1), (1, 0), (2, 3)])
     near = jnp.where(odd == 1, jnp.concatenate([rest, one]), jnp.concatenate([one, rest]))
     pair = onward((state + near.astype(F32)).astype(BF16), "x", 2, 2)
 
@@ -175,13 +175,12 @@
     o_zc = flipped(o_z, "core")
     flip = jnp.bitwise_xor(x, u).astype(jnp.int32).reshape(1)
     width = out_weight.shape[1]
-    whole = pl.BlockSpec((rows, value_size), lambda i: (0, 0))
     part = pl.pallas_call(
         project_kernel,
         grid=(ny // 2,),
         out_shape=jax.ShapeDtypeStruct((rows, ny * width), BF16),
         in_specs=[SMEM]
-        + [whole] * 4
+        + [VMEM] * 4
         + [pl.BlockSpec((2, nu, value_size, width), lambda i: (i, 0, 0, 0))],
         out_specs=pl.BlockSpec((rows, 2 * width), lambda i: (0, i)),
         compiler_params=PARAMS,

time: 150 us -> 148 us (0.987)
  waiting for transfers between devices: 16.9 us -> 14.4 us
  starting transfers between devices: 53.8 us -> 56.1 us
    ppermute x3, starting transfers between devices: 13.6 us -> 16.1 us  [flipped(): return lax.ppermute(value, axis, [(0, 1), (1, 0)])]
    ppermute x3, waiting for transfers between devices: 6.06 us -> 3.48 us  [flipped(): return lax.ppermute(value, axis, [(0, 1), (1, 0)])]
    ppermute x0 -> x1, starting transfers between devices: none -> 2.12 us  [on_device(): rest = lax.ppermute(late, 'x', [(0, 1), (1, 0), (2, 3)])]
    ppermute x4 -> x3, starting transfers between devices: 11.2 us -> 9.09 us  [crossed(): lax.ppermute(value, axis, [(i, i ^ by) for i in range(lax.axis_size(axis))])]
    ppermute x4 -> x3, waiting for transfers between devices: 4.09 us -> 4.08 us  [crossed(): lax.ppermute(value, axis, [(i, i ^ by) for i in range(lax.axis_size(axis))])]
where the time goes in v9:
time: 148 us
  starting transfers between devices  56.1 us (38%)
  blocking collectives  52 us (35%)
  waiting for transfers between devices  14.4 us (10%)
  between operations  13.8 us (9%)
  Pallas kernels  8.27 us (6%)
  matrix products  1.51 us (1%)
    all_to_all x1, blocking collectives, on_device(): back = lax.all_to_all(part, TP, 0, 0, tiled=True)  38.4 us
    ppermute x3, starting transfers between devices, flipped(): return lax.ppermute(value, axis, [(0, 1), (1, 0)])  16.1 us
    ppermute x4, starting transfers between devices, on_device(): got.append(lax.ppermute(out_weight, ('x',) + QUAD, pairs))  14.5 us
    ppermute x4, starting transfers between devices, onward(): return lax.ppermute(value, axis, pairs)  14.3 us
    all_gather x1, blocking collectives, on_device(): far = lax.all_gather(jnp.stack(far), 'x', axis=0)  13.6 us
    ppermute x3, starting transfers between devices, crossed(): lax.ppermute(value, axis, [(i, i ^ by) for i in range(lax.axis_size(axis))])  9.09 us
    ppermute x4, waiting for transfers between devices, on_device(): got.append(lax.ppermute(out_weight, ('x',) + QUAD, pairs))  6.78 us
    pallas_call x1, Pallas kernels, on_device(): pl.pallas_call(project_kernel, grid=(ny // 2,), out_shape=jax.ShapeDtypeS...  4.74 us
  transfers between devices with their start and end apart: 16, of which 6 were waited for; matrix products, arithmetic and copies ran while one was open for 0% of the time, Pallas kernels for 2%

profile of v9, /device:TPU:1, one launch (start us, length us, event | category | flops | bytes accessed | tf_op | source)
XLA Modules:
  0.0 147.5 jit_solution(8937723404003328493)
XLA Ops:
  6.6 1.5 %fusion.2 = f32[256,512]{1,0:T(8,128)S(1)} fusion(bf16[512,256]{1,0:T(8,128)(2,1)} %k_ref.1, bf16[512,512]{1,0:T(8,128)(2,1)} %v_ref.1), kind=kOutput, calls=%fused_computation.13 | convolution fusion | flops 134217728 | bytes 1310720 | tf_op jit(solution)/shard_map/dot_general | solution.py:118
  8.2 3.9 %collective-permute-start.4 = (bf16[128,512]{1,0:T(8,128)(2,1)S(1)}, bf16[128,512]{1,0:T(8,128)(2,1)S(1)}, u32[]{:S(2)}, u32[]{:S(2)}) collective-permute-start(bf16[128,512]{1,0:T(8,128)(2,1)S(1)} %get-tuple-element.28), channel_id=1, source_target_pairs={{0,16},{16,0},{32,48},{48,32},{1,17},{17,1},{33,49},{49,33},{2,18}... | collective-permute-start | bytes 393224 | tf_op jit(solution)/shard_map/ppermute | solution.py:25
  12.1 8.4 %collective-permute-start = (bf16[512,128]{1,0:T(8,128)(2,1)}, bf16[512,128]{1,0:T(8,128)(2,1)S(1)}, u32[]{:S(2)}, u32[]{:S(2)}) collective-permute-start(bf16[512,128]{1,0:T(8,128)(2,1)} %param.11), channel_id=1, source_target_pairs={{0,0},{1,16},{2,32},{3,48},{16,1},{17,17},{18,33},{19,49},{32,2},{... | collective-permute-start | bytes 393224 | tf_op jit(solution)/shard_map/ppermute | solution.py:128
  20.5 1.9 %collective-permute-start.1 = (bf16[512,128]{1,0:T(8,128)(2,1)}, bf16[512,128]{1,0:T(8,128)(2,1)S(1)}, u32[]{:S(2)}, u32[]{:S(2)}) collective-permute-start(bf16[512,128]{1,0:T(8,128)(2,1)} %param.11), channel_id=1, source_target_pairs={{0,16},{1,0},{2,48},{3,32},{16,17},{17,1},{18,49},{19,33},{32,18},... | collective-permute-start | bytes 393224 | tf_op jit(solution)/shard_map/ppermute | solution.py:128
  22.5 1.9 %collective-permute-start.2 = (bf16[512,128]{1,0:T(8,128)(2,1)}, bf16[512,128]{1,0:T(8,128)(2,1)S(1)}, u32[]{:S(2)}, u32[]{:S(2)}) collective-permute-start(bf16[512,128]{1,0:T(8,128)(2,1)} %param.11), channel_id=1, source_target_pairs={{0,32},{1,48},{2,0},{3,16},{16,33},{17,49},{18,1},{19,17},{32,34},... | collective-permute-start | bytes 393224 | tf_op jit(solution)/shard_map/ppermute | solution.py:128
  24.4 2.3 %collective-permute-start.3 = (bf16[512,128]{1,0:T(8,128)(2,1)}, bf16[512,128]{1,0:T(8,128)(2,1)S(1)}, u32[]{:S(2)}, u32[]{:S(2)}) collective-permute-start(bf16[512,128]{1,0:T(8,128)(2,1)} %param.11), channel_id=1, source_target_pairs={{0,48},{1,32},{2,16},{3,0},{16,49},{17,33},{18,17},{19,1},{32,50},... | collective-permute-start | bytes 393224 | tf_op jit(solution)/shard_map/ppermute | solution.py:128
  26.7 0.1 collective-permute-done.1
  26.7 4.6 %collective-permute-done.2 = bf16[512,128]{1,0:T(8,128)(2,1)S(1)} collective-permute-done((bf16[512,128]{1,0:T(8,128)(2,1)}, bf16[512,128]{1,0:T(8,128)(2,1)S(1)}, u32[]{:S(2)}, u32[]{:S(2)}) %collective-permute-start.2) | collective-permute-done | bytes 131104 | tf_op jit(solution)/shard_map/ppermute | solution.py:128
  31.4 2.1 %collective-permute-done.3 = bf16[512,128]{1,0:T(8,128)(2,1)S(1)} collective-permute-done((bf16[512,128]{1,0:T(8,128)(2,1)}, bf16[512,128]{1,0:T(8,128)(2,1)S(1)}, u32[]{:S(2)}, u32[]{:S(2)}) %collective-permute-start.3) | collective-permute-done | bytes 131104 | tf_op jit(solution)/shard_map/ppermute | solution.py:128
  33.5 0.9 pad_maximum_fusion
  34.4 3.2 %collective-permute-start.5 = (bf16[64,512]{1,0:T(8,128)(2,1)S(1)}, bf16[64,512]{1,0:T(8,128)(2,1)S(1)}, u32[]{:S(2)}, u32[]{:S(2)}) collective-permute-start(bf16[64,512]{1,0:T(8,128)(2,1)S(1)} %dynamic-slice_convert_fusion.2), channel_id=1, source_target_pairs={{0,32},{16,48},{32,0},{48,16},{1,33},{17,49},{33,1},{49,17},{2,34}... | collective-permute-start | bytes 196616 | tf_op jit(solution)/shard_map/ppermute | solution.py:25
  37.7 4.1 %collective-permute-done.5 = bf16[64,512]{1,0:T(8,128)(2,1)S(1)} collective-permute-done((bf16[64,512]{1,0:T(8,128)(2,1)S(1)}, bf16[64,512]{1,0:T(8,128)(2,1)S(1)}, u32[]{:S(2)}, u32[]{:S(2)}) %collective-permute-start.5) | collective-permute-done | bytes 65568 | tf_op jit(solution)/shard_map/ppermute | solution.py:25
  41.8 1.9 %collective-permute-start.6 = (bf16[64,512]{1,0:T(8,128)(2,1)S(1)}, bf16[64,512]{1,0:T(8,128)(2,1)S(1)}, u32[]{:S(2)}, u32[]{:S(2)}) collective-permute-start(bf16[64,512]{1,0:T(8,128)(2,1)S(1)} %fusion), channel_id=1, source_target_pairs={{0,64},{64,0},{128,192},{192,128},{256,320},{320,256},{384,448},{4... | collective-permute-start | bytes 196616 | tf_op jit(solution)/shard_map/ppermute | solution.py:25
  43.7 0.1 copy.10.index_ref
  43.9 0.1 copy.9.coef_ref
  44.0 1.8 %shard_map.64 = (f32[512,512]{1,0:T(8,128)S(1)}, f32[512,15]{1,0:T(8,128)S(1)}) custom-call(f32[16,1]{1,0:T(8,128)S(1)} %copy.9.coef_ref, s32[512,15]{1,0:T(8,128)S(1)} %copy.10.index_ref, bf16[512,256]{1,0:T(8,128)(2,1)S(1)} %copy-done.2, bf16[512,256]{1,0:T(8,128)(2,1)S(1)} %copy-done.1, bf16[512,512]{1,0:T(8,128)(2,1)S(1)} %copy-done), custom_call_target="tpu_custom_call" | custom-call | tf_op jit(solution)/shard_map/pallas_call | solution.py:146
  45.7 2.1 %collective-permute-start.7 = (bf16[128,512]{1,0:T(8,128)(2,1)S(1)}, bf16[128,512]{1,0:T(8,128)(2,1)S(1)}, u32[]{:S(2)}, u32[]{:S(2)}) collective-permute-start(bf16[128,512]{1,0:T(8,128)(2,1)S(1)} %get-tuple-element.19), channel_id=1, source_target_pairs={{0,16},{16,0},{32,48},{1,17},{17,1},{33,49},{2,18},{18,2},{34,50},... | collective-permute-start | bytes 393224 | tf_op jit(solution)/shard_map/ppermute | solution.py:142
  47.9 6.0 %collective-permute-start.10 = (bf16[64,512]{1,0:T(8,128)(2,1)S(1)}, bf16[64,512]{1,0:T(8,128)(2,1)S(1)}, u32[]{:S(2)}, u32[]{:S(2)}) collective-permute-start(bf16[64,512]{1,0:T(8,128)(2,1)S(1)} %add_convert_fusion.2), channel_id=1, source_target_pairs={{0,256},{64,320},{128,384},{192,448},{1,257},{65,321},{129,385},{1... | collective-permute-start | bytes 196616 | tf_op jit(solution)/shard_map/ppermute | solution.py:30
  54.0 1.3 collective-permute-start.11
  55.3 2.4 %collective-permute-start.9 = (bf16[64,512]{1,0:T(8,128)(2,1)S(1)}, bf16[64,512]{1,0:T(8,128)(2,1)S(1)}, u32[]{:S(2)}, u32[]{:S(2)}) collective-permute-start(bf16[64,512]{1,0:T(8,128)(2,1)S(1)} %add_convert_fusion.2), channel_id=1, source_target_pairs={{0,128},{64,192},{256,384},{320,448},{1,129},{65,193},{257,385},{3... | collective-permute-start | bytes 196616 | tf_op jit(solution)/shard_map/ppermute | solution.py:30
  57.7 0.2 add_convert_fusion
  57.8 4.5 %collective-permute-start.8 = (bf16[256,512]{1,0:T(8,128)(2,1)S(1)}, bf16[256,512]{1,0:T(8,128)(2,1)S(1)}, u32[]{:S(2)}, u32[]{:S(2)}) collective-permute-start(bf16[256,512]{1,0:T(8,128)(2,1)S(1)} %get-tuple-element.25), channel_id=1, source_target_pairs={{0,32},{16,48},{1,33},{17,49},{2,34},{18,50},{3,35},{19,51},{4,36}... | collective-permute-start | bytes 786440 | tf_op jit(solution)/shard_map/ppermute | solution.py:30
  62.5 13.6 %all-gather = bf16[12,64,512]{2,1,0:T(8,128)(2,1)S(1)} all-gather(bf16[3,64,512]{2,1,0:T(8,128)(2,1)S(1)} %pad_maximum_fusion.1), channel_id=2, replica_groups=mesh['y'=8,'x'=4,'zh'=4,'zl'=2,'core'=2] {'x'}, dimensions={0}, use_global_device_ids=true | all-gather | bytes 983040 | tf_op jit(solution)/shard_map/all_gather | solution.py:161
  76.1 0.9 shard_map.65.o0_ref
  77.0 3.2 %collective-permute-start.13 = (bf16[512,512]{1,0:T(8,128)(2,1)S(1)}, bf16[512,512]{1,0:T(8,128)(2,1)S(1)}, u32[]{:S(2)}, u32[]{:S(2)}) collective-permute-start(bf16[512,512]{1,0:T(8,128)(2,1)S(1)} %shard_map.65.o0_ref), channel_id=1, source_target_pairs={{0,2},{2,0},{1,3},{3,1},{4,6},{6,4},{5,7},{7,5},{8,10},{10,8},{9,1... | collective-permute-start | bytes 1572872 | tf_op jit(solution)/shard_map/ppermute | solution.py:34
  80.3 5.9 %collective-permute-start.12 = (bf16[512,512]{1,0:T(8,128)(2,1)S(1)}, bf16[512,512]{1,0:T(8,128)(2,1)S(1)}, u32[]{:S(2)}, u32[]{:S(2)}) collective-permute-start(bf16[512,512]{1,0:T(8,128)(2,1)S(1)} %shard_map.65.o0_ref), channel_id=1, source_target_pairs={{0,1},{1,0},{2,3},{3,2},{4,5},{5,4},{6,7},{7,6},{8,9},{9,8},{10,11... | collective-permute-start | bytes 1572872 | tf_op jit(solution)/shard_map/ppermute | solution.py:34
  86.2 2.0 %collective-permute-done.13.o2_ref = bf16[512,512]{1,0:T(8,128)(2,1)S(1)} collective-permute-done((bf16[512,512]{1,0:T(8,128)(2,1)S(1)}, bf16[512,512]{1,0:T(8,128)(2,1)S(1)}, u32[]{:S(2)}, u32[]{:S(2)}) %collective-permute-start.13) | collective-permute-done | bytes 524320 | tf_op jit(solution)/shard_map/ppermute | solution.py:34
  88.2 7.0 %collective-permute-start.14 = (bf16[512,512]{1,0:T(8,128)(2,1)S(1)}, bf16[512,512]{1,0:T(8,128)(2,1)S(1)}, u32[]{:S(2)}, u32[]{:S(2)}) collective-permute-start(bf16[512,512]{1,0:T(8,128)(2,1)S(1)} %collective-permute-done.13.o2_ref), channel_id=1, source_target_pairs={{0,1},{1,0},{2,3},{3,2},{4,5},{5,4},{6,7},{7,6},{8,9},{9,8},{10,11... | collective-permute-start | bytes 1572872 | tf_op jit(solution)/shard_map/ppermute | solution.py:34
  95.2 1.5 %collective-permute-done.14.o3_ref = bf16[512,512]{1,0:T(8,128)(2,1)S(1)} collective-permute-done((bf16[512,512]{1,0:T(8,128)(2,1)S(1)}, bf16[512,512]{1,0:T(8,128)(2,1)S(1)}, u32[]{:S(2)}, u32[]{:S(2)}) %collective-permute-start.14) | collective-permute-done | bytes 524320 | tf_op jit(solution)/shard_map/ppermute | solution.py:34
  96.7 4.7 %shard_map.66 = bf16[512,1024]{1,0:T(8,128)(2,1)S(1)} custom-call(s32[1]{0:T(128)} %bitcast.flip_ref, bf16[512,512]{1,0:T(8,128)(2,1)S(1)} %shard_map.65.o0_ref, bf16[512,512]{1,0:T(8,128)(2,1)S(1)} %collective-permute-done.12.o1_ref, bf16[512,512]{1,0:T(8,128)(2,1)S(1)} %collective-permute-done.13.o2_ref, ...), custom_call_target="tpu_custom_call" | custom-call | tf_op jit(solution)/shard_map/pallas_call | solution.py:178
  101.4 38.4 %all_to_all.9 = bf16[16,32,1024]{2,1,0:T(8,128)(2,1)S(1)} all-to-all(bf16[16,32,1024]{2,1,0:T(8,128)(2,1)S(1)} %bitcast.17), channel_id=1, replica_groups=mesh['y'=8,'x'=4,'zh'=4,'zl'=2,'core'=2] {'zh','zl','core'}, dimensions={0} | all-to-all | bytes 2097152 | tf_op jit(solution)/shard_map/all_to_all | solution.py:190
  139.8 0.8 shard_map.67
  (29 shorter events, 0.3 us)
Async XLA Ops:
  6.5 37.4 %copy-start.1 = (bf16[512,256]{1,0:T(8,128)(2,1)S(1)}, bf16[512,256]{1,0:T(8,128)(2,1)}, u32[]{:S(2)}) copy-start(bf16[512,256]{1,0:T(8,128)(2,1)} %k_ref.1) | copy-start | bytes 786436
  6.5 37.4 %copy-start = (bf16[512,512]{1,0:T(8,128)(2,1)S(1)}, bf16[512,512]{1,0:T(8,128)(2,1)}, u32[]{:S(2)}) copy-start(bf16[512,512]{1,0:T(8,128)(2,1)} %v_ref.1) | copy-start | bytes 1572868
  6.5 37.2 %copy-start.3 = (s32[512,15]{0,1:T(8,128)S(1)}, s32[512,15]{0,1:T(8,128)}, u32[]{:S(2)}) copy-start(s32[512,15]{0,1:T(8,128)} %param.10) | copy-start | bytes 92164
  6.5 37.3 %copy-start.4 = (f32[16,1]{0,1:T(1,128)S(1)}, f32[16,1]{0,1:T(1,128)}, u32[]{:S(2)}) copy-start(f32[16,1]{0,1:T(1,128)} %param.9) | copy-start | bytes 196
  6.5 37.4 %copy-start.2 = (bf16[512,256]{1,0:T(8,128)(2,1)S(1)}, bf16[512,256]{1,0:T(8,128)(2,1)}, u32[]{:S(2)}) copy-start(bf16[512,256]{1,0:T(8,128)(2,1)} %q_ref.3) | copy-start | bytes 786436
  6.5 90.1 %all-gather.4.cloned.1.call-start = ((), (), s32[]{:S(2)}) async-start(), calls=%async_computation.1 | async-start | bytes 4718592 | tf_op jit(solution)/shard_map/all_gather | solution.py:132
  8.2 18.5 %collective-permute-start.4 = (bf16[128,512]{1,0:T(8,128)(2,1)S(1)}, bf16[128,512]{1,0:T(8,128)(2,1)S(1)}, u32[]{:S(2)}, u32[]{:S(2)}) collective-permute-start(bf16[128,512]{1,0:T(8,128)(2,1)S(1)} %get-tuple-element.28), channel_id=1, source_target_pairs={{0,16},{16,0},{32,48},{48,32},{1,17},{17,1},{33,49},{49,33},{2,18}... | collective-permute-start | bytes 393224 | tf_op jit(solution)/shard_map/ppermute | solution.py:25
  12.1 14.5 %collective-permute-start = (bf16[512,128]{1,0:T(8,128)(2,1)}, bf16[512,128]{1,0:T(8,128)(2,1)S(1)}, u32[]{:S(2)}, u32[]{:S(2)}) collective-permute-start(bf16[512,128]{1,0:T(8,128)(2,1)} %param.11), channel_id=1, source_target_pairs={{0,0},{1,16},{2,32},{3,48},{16,1},{17,17},{18,33},{19,49},{32,2},{... | collective-permute-start | bytes 393224 | tf_op jit(solution)/shard_map/ppermute | solution.py:128
  20.5 6.2 %collective-permute-start.1 = (bf16[512,128]{1,0:T(8,128)(2,1)}, bf16[512,128]{1,0:T(8,128)(2,1)S(1)}, u32[]{:S(2)}, u32[]{:S(2)}) collective-permute-start(bf16[512,128]{1,0:T(8,128)(2,1)} %param.11), channel_id=1, source_target_pairs={{0,16},{1,0},{2,48},{3,32},{16,17},{17,1},{18,49},{19,33},{32,18},... | collective-permute-start | bytes 393224 | tf_op jit(solution)/shard_map/ppermute | solution.py:128
  22.5 8.9 %collective-permute-start.2 = (bf16[512,128]{1,0:T(8,128)(2,1)}, bf16[512,128]{1,0:T(8,128)(2,1)S(1)}, u32[]{:S(2)}, u32[]{:S(2)}) collective-permute-start(bf16[512,128]{1,0:T(8,128)(2,1)} %param.11), channel_id=1, source_target_pairs={{0,32},{1,48},{2,0},{3,16},{16,33},{17,49},{18,1},{19,17},{32,34},... | collective-permute-start | bytes 393224 | tf_op jit(solution)/shard_map/ppermute | solution.py:128
  24.4 9.1 %collective-permute-start.3 = (bf16[512,128]{1,0:T(8,128)(2,1)}, bf16[512,128]{1,0:T(8,128)(2,1)S(1)}, u32[]{:S(2)}, u32[]{:S(2)}) collective-permute-start(bf16[512,128]{1,0:T(8,128)(2,1)} %param.11), channel_id=1, source_target_pairs={{0,48},{1,32},{2,16},{3,0},{16,49},{17,33},{18,17},{19,1},{32,50},... | collective-permute-start | bytes 393224 | tf_op jit(solution)/shard_map/ppermute | solution.py:128
  34.4 7.3 %collective-permute-start.5 = (bf16[64,512]{1,0:T(8,128)(2,1)S(1)}, bf16[64,512]{1,0:T(8,128)(2,1)S(1)}, u32[]{:S(2)}, u32[]{:S(2)}) collective-permute-start(bf16[64,512]{1,0:T(8,128)(2,1)S(1)} %dynamic-slice_convert_fusion.2), channel_id=1, source_target_pairs={{0,32},{16,48},{32,0},{48,16},{1,33},{17,49},{33,1},{49,17},{2,34}... | collective-permute-start | bytes 196616 | tf_op jit(solution)/shard_map/ppermute | solution.py:25
  41.8 6.1 %collective-permute-start.6 = (bf16[64,512]{1,0:T(8,128)(2,1)S(1)}, bf16[64,512]{1,0:T(8,128)(2,1)S(1)}, u32[]{:S(2)}, u32[]{:S(2)}) collective-permute-start(bf16[64,512]{1,0:T(8,128)(2,1)S(1)} %fusion), channel_id=1, source_target_pairs={{0,64},{64,0},{128,192},{192,128},{256,320},{320,256},{384,448},{4... | collective-permute-start | bytes 196616 | tf_op jit(solution)/shard_map/ppermute | solution.py:25
  45.7 12.0 %collective-permute-start.7 = (bf16[128,512]{1,0:T(8,128)(2,1)S(1)}, bf16[128,512]{1,0:T(8,128)(2,1)S(1)}, u32[]{:S(2)}, u32[]{:S(2)}) collective-permute-start(bf16[128,512]{1,0:T(8,128)(2,1)S(1)} %get-tuple-element.19), channel_id=1, source_target_pairs={{0,16},{16,0},{32,48},{1,17},{17,1},{33,49},{2,18},{18,2},{34,50},... | collective-permute-start | bytes 393224 | tf_op jit(solution)/shard_map/ppermute | solution.py:142
  47.9 14.5 %collective-permute-start.10 = (bf16[64,512]{1,0:T(8,128)(2,1)S(1)}, bf16[64,512]{1,0:T(8,128)(2,1)S(1)}, u32[]{:S(2)}, u32[]{:S(2)}) collective-permute-start(bf16[64,512]{1,0:T(8,128)(2,1)S(1)} %add_convert_fusion.2), channel_id=1, source_target_pairs={{0,256},{64,320},{128,384},{192,448},{1,257},{65,321},{129,385},{1... | collective-permute-start | bytes 196616 | tf_op jit(solution)/shard_map/ppermute | solution.py:30
  54.0 8.4 %collective-permute-start.11 = (bf16[64,512]{1,0:T(8,128)(2,1)S(1)}, bf16[64,512]{1,0:T(8,128)(2,1)S(1)}, u32[]{:S(2)}, u32[]{:S(2)}) collective-permute-start(bf16[64,512]{1,0:T(8,128)(2,1)S(1)} %add_convert_fusion.2), channel_id=1, source_target_pairs={{0,384},{64,448},{128,256},{192,320},{1,385},{65,449},{129,257},{1... | collective-permute-start | bytes 196616 | tf_op jit(solution)/shard_map/ppermute | solution.py:30
  55.3 7.2 %collective-permute-start.9 = (bf16[64,512]{1,0:T(8,128)(2,1)S(1)}, bf16[64,512]{1,0:T(8,128)(2,1)S(1)}, u32[]{:S(2)}, u32[]{:S(2)}) collective-permute-start(bf16[64,512]{1,0:T(8,128)(2,1)S(1)} %add_convert_fusion.2), channel_id=1, source_target_pairs={{0,128},{64,192},{256,384},{320,448},{1,129},{65,193},{257,385},{3... | collective-permute-start | bytes 196616 | tf_op jit(solution)/shard_map/ppermute | solution.py:30
  57.8 18.2 %collective-permute-start.8 = (bf16[256,512]{1,0:T(8,128)(2,1)S(1)}, bf16[256,512]{1,0:T(8,128)(2,1)S(1)}, u32[]{:S(2)}, u32[]{:S(2)}) collective-permute-start(bf16[256,512]{1,0:T(8,128)(2,1)S(1)} %get-tuple-element.25), channel_id=1, source_target_pairs={{0,32},{16,48},{1,33},{17,49},{2,34},{18,50},{3,35},{19,51},{4,36}... | collective-permute-start | bytes 786440 | tf_op jit(solution)/shard_map/ppermute | solution.py:30
  77.0 11.2 %collective-permute-start.13 = (bf16[512,512]{1,0:T(8,128)(2,1)S(1)}, bf16[512,512]{1,0:T(8,128)(2,1)S(1)}, u32[]{:S(2)}, u32[]{:S(2)}) collective-permute-start(bf16[512,512]{1,0:T(8,128)(2,1)S(1)} %shard_map.65.o0_ref), channel_id=1, source_target_pairs={{0,2},{2,0},{1,3},{3,1},{4,6},{6,4},{5,7},{7,5},{8,10},{10,8},{9,1... | collective-permute-start | bytes 1572872 | tf_op jit(solution)/shard_map/ppermute | solution.py:34
  80.3 14.9 %collective-permute-start.12 = (bf16[512,512]{1,0:T(8,128)(2,1)S(1)}, bf16[512,512]{1,0:T(8,128)(2,1)S(1)}, u32[]{:S(2)}, u32[]{:S(2)}) collective-permute-start(bf16[512,512]{1,0:T(8,128)(2,1)S(1)} %shard_map.65.o0_ref), channel_id=1, source_target_pairs={{0,1},{1,0},{2,3},{3,2},{4,5},{5,4},{6,7},{7,6},{8,9},{9,8},{10,11... | collective-permute-start | bytes 1572872 | tf_op jit(solution)/shard_map/ppermute | solution.py:34
  88.2 8.5 %collective-permute-start.14 = (bf16[512,512]{1,0:T(8,128)(2,1)S(1)}, bf16[512,512]{1,0:T(8,128)(2,1)S(1)}, u32[]{:S(2)}, u32[]{:S(2)}) collective-permute-start(bf16[512,512]{1,0:T(8,128)(2,1)S(1)} %collective-permute-done.13.o2_ref), channel_id=1, source_target_pairs={{0,1},{1,0},{2,3},{3,2},{4,5},{5,4},{6,7},{7,6},{8,9},{9,8},{10,11... | collective-permute-start | bytes 1572872 | tf_op jit(solution)/shard_map/ppermute | solution.py:34
Sparse Core Ops, SparseCore 0:
  34.5 62.0 all-gather.3
